TPU v7x, 32 devices: a whole 2x2x4 slice. The times are simulated.
32 devices in a mesh: grp: 2 (over x), wave: 16 (over z, y, core).
Axes of the slice: x: 2, y: 2, z: 4, core: 2. Of those that a mesh axis runs over, the one named last changes fastest.
Arguments:
- north_rows: bfloat16 [2560, 128, 274], P(('grp', 'wave')), parts along dimension 0, may hold values from -6 to 6
- south_rows: bfloat16 [2560, 128, 274], P(('grp', 'wave')), parts along dimension 0, may hold values from -6 to 6
- lon_counts: int32 [1280], replicated, may hold values from 20 to 5148, as said below
- slot_wave: int32 [128], replicated, may hold values from 0 to 2559, as said below
- legendre: bfloat16 [128, 1280, 1280], P('wave'), may hold values from -0.15625 to 0.15625
- mode_rates: float32 [137], replicated, may hold values from 0.05 to 20
- to_modes: bfloat16 [137, 137], replicated, may hold values from -0.5 to 0.5
- from_modes: bfloat16 [137, 137], replicated, may hold values from -0.5 to 0.5
Outputs:
- spec_state: bfloat16 [256, 1280, 274], P(('grp', 'wave')), parts along dimension 0
- new_rows: bfloat16 [2560, 128, 274], P(('grp', 'wave')), parts along dimension 0
There are 2 independent parts, one for each index of `grp`. A program takes and returns all parts, laid end to end along the dimension named above; an argument that names none is the same for every part. Nothing has to cross between parts.
Inputs may be any that keep to these rules, and one draw needn't show every extreme that they name: Wavenumber m is present in latitude row j only if 2 m is below lon_counts[j]. `slot_wave`: distinct zonal wavenumbers.
All inputs are finite; a program needn't handle non-finite values.
Results may differ from a plain program's by a relative error of at most 0.0065.
Values may be sent and summed in bfloat16 or wider, within the bound.
No kernel may reach another device: no remote copies, remote signals or barrier semaphores. Data moves between devices by JAX's collectives and lax.ppermute only.
A program may use at most 192 MiB of HBM per device.

v0:
```python
import jax
import jax.numpy as jnp
from jax import lax
from jax.sharding import PartitionSpec as P

NMAX = 2559


def vertical_step(direct, own_waves, mode_rates, to_modes, from_modes):
    slot_count, row_total, channels = direct.shape
    levels = to_modes.shape[0]
    modal_part = jnp.dot(direct.reshape(-1, levels), to_modes, preferred_element_type=jnp.float32)
    modal_part = modal_part.reshape(slot_count, row_total, 2, levels)
    degree = own_waves[:, None] + 2 * jnp.arange(row_total, dtype=jnp.int32)[None, :]
    degree_f = degree.astype(jnp.float32)
    scaled_degree = degree_f * (degree_f + 1.0) / float(NMAX * (NMAX + 1))
    divisor = 1.0 + mode_rates[None, None, None, :] * scaled_degree[:, :, None, None]
    scaled = (modal_part / divisor).astype(jnp.bfloat16).reshape(-1, levels)
    result = jnp.dot(scaled, from_modes, preferred_element_type=jnp.float32)
    result = result.reshape(slot_count, row_total, channels)
    return jnp.where((degree <= NMAX)[:, :, None], result, 0.0).astype(jnp.bfloat16)


def per_device(
    north_rows, south_rows, lon_counts, slot_wave, legendre, mode_rates, to_modes, from_modes
):
    lat_dev = north_rows.shape[0]
    slot_dev, row_total, lat_total = legendre.shape
    my_index = lax.axis_index("wave")
    own_waves = lax.dynamic_slice_in_dim(slot_wave, my_index * slot_dev, slot_dev)
    live_own = 2 * own_waves[None, :] < lon_counts[:, None]
    local_counts = lax.dynamic_slice_in_dim(lon_counts, my_index * lat_dev, lat_dev)
    live_here = 2 * slot_wave[None, :] < local_counts[:, None]
    summed = north_rows.astype(jnp.float32) + south_rows.astype(jnp.float32)
    sym_here = jnp.where(live_here[:, :, None], summed, 0.0).astype(jnp.bfloat16)
    columns = lax.all_to_all(sym_here, "wave", split_axis=1, concat_axis=0, tiled=True)
    direct = jnp.einsum(
        "snj,jsc->snc", legendre, columns, preferred_element_type=jnp.float32
    ).astype(jnp.bfloat16)
    spec_state = vertical_step(direct, own_waves, mode_rates, to_modes, from_modes)
    returned = jnp.einsum("snj,snc->jsc", legendre, spec_state, preferred_element_type=jnp.float32)
    returned = jnp.where(live_own[:, :, None], returned, 0.0).astype(jnp.bfloat16)
    new_rows = lax.all_to_all(returned, "wave", split_axis=0, concat_axis=1, tiled=True)
    return (spec_state, new_rows)


def solution(mesh):
    in_specs = (
        P(("grp", "wave"), None, None),
        P(("grp", "wave"), None, None),
        P(),
        P(),
        P("wave", None, None),
        P(),
        P(),
        P(),
    )
    out_specs = (P(("grp", "wave"), None, None), P(("grp", "wave"), None, None))
    return jax.shard_map(
        per_device, mesh=mesh, in_specs=in_specs, out_specs=out_specs, check_vma=False
    )
```

profile of v0, /device:TPU:13, one launch (start us, length us, event | category | flops | bytes accessed | tf_op | source)
XLA Modules:
  0.0 580.2 jit_solution(6979879642193113835)
XLA Ops:
  0.6 0.0 copy-start
  0.7 11.0 %copy.45 = bf16[80,128,274]{2,0,1:T(8,128)(2,1)} copy(bf16[80,128,274]{1,0,2:T(8,128)(2,1)} %param.9) | data formatting | bytes 11223040 | tf_op args[1]
  11.6 0.0 copy-start.5
  11.6 0.0 copy-start.3
  11.6 11.0 %copy.44 = bf16[80,128,274]{2,0,1:T(8,128)(2,1)} copy(bf16[80,128,274]{1,0,2:T(8,128)(2,1)} %param.8) | data formatting | bytes 11223040 | tf_op args[0]
  22.7 0.0 copy-done.5
  22.7 0.0 copy-done.3
  22.7 0.1 dynamic_slice.7
  22.8 0.1 broadcast_compare_fusion
  22.9 9.6 %select_convert_fusion.1 = bf16[80,128,274]{2,0,1:T(8,128)(2,1)} fusion(bf16[80,128,274]{2,0,1:T(8,128)(2,1)} %copy.45, bf16[80,128,274]{2,0,1:T(8,128)(2,1)} %copy.44, pred[80,128]{0,1:T(8,128)(4,1)S(1)} %broadcast_compare_fusion), kind=kLoop, calls=%fused_computation.1 | loop fusion | flops 14028800 | bytes 16844800 | tf_op jit(solution)/shard_map/convert_element_type | solution.py:35
  32.5 0.0 copy-start.4
  32.5 6.7 %all-to-all-start = ((bf16[80,128,274]{2,0,1:T(8,128)(2,1)}), bf16[80,128,274]{2,0,1:T(8,128)(2,1)}, u32[]{:S(2)}, u32[]{:S(2)}) async-start(bf16[80,128,274]{2,0,1:T(8,128)(2,1)} %select_convert_fusion.1), calls=%async_computation | async-start | bytes 15728640 | tf_op jit(solution)/shard_map/all_to_all | solution.py:36
  39.2 0.1 broadcast_multiply_fusion
  39.3 0.1 broadcast_compare_fusion.1
  39.3 0.1 add_compare_fusion
  39.4 0.1 fusion.3
  39.5 0.0 copy-done.4
  39.5 3.2 multiply_add_fusion
  42.7 167.6 %all-to-all-done = bf16[80,128,274]{2,0,1:T(8,128)(2,1)} async-done(((bf16[80,128,274]{2,0,1:T(8,128)(2,1)}), bf16[80,128,274]{2,0,1:T(8,128)(2,1)}, u32[]{:S(2)}, u32[]{:S(2)}) %all-to-all-start) | async-done | bytes 5611552 | tf_op jit(solution)/shard_map/all_to_all | solution.py:36
  210.3 14.5 %copy.65 = bf16[16,80,8,274]{1,0,3,2:T(8,128)(2,1)} copy(bf16[16,80,8,274]{3,1,2,0:T(8,128)(2,1)} %bitcast.2) | data formatting | bytes 11223040 | tf_op jit(solution)/shard_map/all_to_all | solution.py:36
  224.8 13.2 %reshape.146 = bf16[1280,8,274]{0,2,1:T(8,128)(2,1)} reshape(bf16[16,80,8,274]{1,0,3,2:T(8,128)(2,1)} %copy.65) | data formatting | bytes 11223040 | tf_op jit(solution)/shard_map/all_to_all | solution.py:36
  238.1 25.7 %convert_bitcast_fusion = bf16[8,1280,274]{1,2,0:T(8,128)(2,1)} fusion(bf16[1280,8,274]{0,2,1:T(8,128)(2,1)} %reshape.146, bf16[8,1280,1280]{2,1,0:T(8,128)(2,1)} %param.12), kind=kOutput, calls=%fused_computation.8 | convolution fusion | flops 7185551360 | bytes 37437440 | tf_op jit(solution)/shard_map/snj,jsc->snc/dot_general | solution.py:37
  263.7 3.7 copy.49
  267.4 0.0 copy-done
  267.4 6.4 %divide_convert_fusion = bf16[8,1280,2,137]{1,3,2,0:T(8,128)(2,1)} fusion(bf16[8,1280,2,137]{1,0,3,2:T(8,128)(2,1)S(1)} %bitcast.31, f32[8,1280,137]{1,2,0:T(8,128)} %multiply_add_fusion, bf16[137,137]{1,0:T(8,128)(2,1)S(1)} %copy-done), kind=kOutput, calls=%fused_computation.2 | convolution fusion | flops 774389760 | bytes 16872098 | tf_op jit(solution)/shard_map/dot_general | solution.py:12
  273.9 25.2 %copy.52 = bf16[8,1280,2,137]{3,2,1,0:T(2,128)(2,1)} copy(bf16[8,1280,2,137]{1,3,2,0:T(8,128)(2,1)} %divide_convert_fusion) | data formatting | bytes 11223040 | tf_op jit(solution)/shard_map/convert_element_type | solution.py:18
  299.1 0.0 copy-start.2
  299.1 18.9 %reshape.143 = bf16[20480,137]{1,0:T(8,128)(2,1)} reshape(bf16[8,1280,2,137]{3,2,1,0:T(2,128)(2,1)} %copy.52) | data formatting | bytes 11223040 | tf_op jit(solution)/shard_map/reshape | solution.py:18
  318.0 0.0 copy-done.2
  318.0 10.8 %fusion.4 = bf16[20480,137]{1,0:T(8,128)(2,1)} fusion(bf16[20480,137]{1,0:T(8,128)(2,1)} %reshape.143, bf16[137,137]{1,0:T(8,128)(2,1)S(1)} %copy-done.2), kind=kOutput, calls=%fused_computation.19 | convolution fusion | flops 768778240 | bytes 11260578 | tf_op jit(solution)/shard_map/dot_general | solution.py:19
  328.8 16.0 %reshape.144 = bf16[8,1280,274]{2,1,0:T(8,128)(2,1)} reshape(bf16[20480,137]{1,0:T(8,128)(2,1)} %fusion.4) | data formatting | bytes 11223040 | tf_op jit(solution)/shard_map/reshape | solution.py:20
  344.8 7.6 %select_convert_fusion = bf16[8,1280,274]{2,1,0:T(8,128)(2,1)} fusion(bf16[8,1280,274]{2,1,0:T(8,128)(2,1)} %reshape.144, pred[8,1280]{1,0:T(8,128)(4,1)S(1)} %add_compare_fusion), kind=kLoop, calls=%fused_computation | loop fusion | flops 2805760 | bytes 11233280 | tf_op jit(solution)/shard_map/convert_element_type | solution.py:21
  352.4 16.3 %fusion.5 = bf16[8,274,1280]{2,1,0:T(8,128)(2,1)} fusion(bf16[8,1280,274]{2,1,0:T(8,128)(2,1)} %select_convert_fusion, bf16[8,1280,1280]{2,1,0:T(8,128)(2,1)} %param.12), kind=kOutput, calls=%fused_computation.20 | convolution fusion | flops 7182745600 | bytes 37437440 | tf_op jit(solution)/shard_map/snj,snc->jsc/dot_general | solution.py:41
  368.8 6.5 %fusion = bf16[1280,8,274]{0,1,2:T(8,128)(2,1)} fusion(bf16[8,274,1280]{2,1,0:T(8,128)(2,1)} %fusion.5, pred[1280,8]{0,1:T(8,128)(4,1)S(1)} %broadcast_compare_fusion.1), kind=kLoop, calls=%fused_computation.4 | loop fusion | flops 2805760 | bytes 11233280 | tf_op jit(solution)/shard_map/convert_element_type | solution.py:42
  375.3 10.9 %copy.56 = bf16[1280,8,274]{2,1,0:T(8,128)(2,1)} copy(bf16[1280,8,274]{0,1,2:T(8,128)(2,1)} %fusion) | data formatting | bytes 11223040 | tf_op jit(solution)/shard_map/convert_element_type | solution.py:42
  386.2 4.9 all-to-all-start.1
  391.1 10.1 %copy.59 = bf16[8,1280,274]{1,0,2:T(8,128)(2,1)} copy(bf16[8,1280,274]{2,1,0:T(8,128)(2,1)} %select_convert_fusion) | data formatting | bytes 11223040
  401.2 161.1 %all-to-all-done.1 = bf16[1280,8,274]{2,1,0:T(8,128)(2,1)} async-done(((bf16[1280,8,274]{2,1,0:T(8,128)(2,1)}), bf16[1280,8,274]{2,1,0:T(8,128)(2,1)}, u32[]{:S(2)}, u32[]{:S(2)}) %all-to-all-start.1) | async-done | bytes 5611552 | tf_op jit(solution)/shard_map/all_to_all | solution.py:43
  562.2 0.0 copy-start.1
  562.3 7.9 %copy.74 = bf16[80,16,8,274]{3,2,1,0:T(8,128)(2,1)} copy(bf16[80,16,8,274]{3,2,0,1:T(8,128)(2,1)} %bitcast.9) | data formatting | bytes 11223040 | tf_op jit(solution)/shard_map/all_to_all | solution.py:43
  570.1 10.0 %copy.60 = bf16[80,128,274]{1,0,2:T(8,128)(2,1)} copy(bf16[80,128,274]{2,1,0:T(8,128)(2,1)} %bitcast.30) | data formatting | bytes 11223040
  580.2 0.0 copy-done.1
  (2 shorter events, 0.0 us)
Async XLA Ops:
  0.6 266.8 %copy-start = (bf16[137,137]{1,0:T(8,128)(2,1)S(1)}, bf16[137,137]{1,0:T(8,128)(2,1)}, u32[]{:S(2)}) copy-start(bf16[137,137]{1,0:T(8,128)(2,1)} %param.14) | copy-start | bytes 112618
  11.6 11.1 %copy-start.5 = (s32[128]{0:T(128)S(1)}, s32[128]{0:T(128)}, u32[]{:S(2)}) copy-start(s32[128]{0:T(128)} %param.11) | copy-start | bytes 1540
  11.6 11.1 %copy-start.3 = (s32[1280]{0:T(1024)S(1)}, s32[1280]{0:T(1024)}, u32[]{:S(2)}) copy-start(s32[1280]{0:T(1024)} %param.10) | copy-start | bytes 15364
  32.5 7.0 %copy-start.4 = (f32[137]{0:T(256)S(1)}, f32[137]{0:T(256)}, u32[]{:S(2)}) copy-start(f32[137]{0:T(256)} %param.13) | copy-start | bytes 1648
  32.5 177.8 %all-to-all-start = ((bf16[80,128,274]{2,0,1:T(8,128)(2,1)}), bf16[80,128,274]{2,0,1:T(8,128)(2,1)}, u32[]{:S(2)}, u32[]{:S(2)}) async-start(bf16[80,128,274]{2,0,1:T(8,128)(2,1)} %select_convert_fusion.1), calls=%async_computation | async-start | bytes 15728640 | tf_op jit(solution)/shard_map/all_to_all | solution.py:36
  299.1 18.9 %copy-start.2 = (bf16[137,137]{1,0:T(8,128)(2,1)S(1)}, bf16[137,137]{1,0:T(8,128)(2,1)}, u32[]{:S(2)}) copy-start(bf16[137,137]{1,0:T(8,128)(2,1)} %param.15) | copy-start | bytes 112618
  386.2 176.0 %all-to-all-start.1 = ((bf16[1280,8,274]{2,1,0:T(8,128)(2,1)}), bf16[1280,8,274]{2,1,0:T(8,128)(2,1)}, u32[]{:S(2)}, u32[]{:S(2)}) async-start(bf16[1280,8,274]{2,1,0:T(8,128)(2,1)} %copy.56), calls=%async_computation.1 | async-start | bytes 15728640 | tf_op jit(solution)/shard_map/all_to_all | solution.py:43
  562.2 17.9 %copy-start.1 = (bf16[137,137]{1,0:T(8,128)(2,1)S(1)}, bf16[137,137]{1,0:T(8,128)(2,1)}, u32[]{:S(2)}) copy-start(bf16[137,137]{1,0:T(8,128)(2,1)} %param.14) | copy-start | bytes 112618
where the time goes:
time: 584 us; the launch traced here: 580 us
  waiting for transfers between devices  329 us (56%)
  local copies, waits for them, and re-layouts  153 us (26%)
  matrix products  59.3 us (10%)
  other arithmetic  27.3 us (5%)
  starting transfers between devices  11.6 us (2%)
    all_to_all x1, waiting for transfers between devices, per_device(): lax.all_to_all(sym_here, 'wave', split_axis=1, concat_axis=0, tiled=True)  168 us
    all_to_all x1, waiting for transfers between devices, per_device(): lax.all_to_all(returned, 'wave', split_axis=0, concat_axis=1, tiled=True)  161 us
    unnamed x16, local copies, waits for them, and re-layouts  42.2 us
    all_to_all x2, local copies, waits for them, and re-layouts, per_device(): lax.all_to_all(sym_here, 'wave', split_axis=1, concat_axis=0, tiled=True)  27.8 us
    dot_general x1, matrix products, per_device(): jnp.einsum('snj,jsc->snc', legendre, columns, preferred_element_type=jnp....  25.7 us
    convert_element_type x1, local copies, waits for them, and re-layouts, vertical_step(): scaled = (modal_part / divisor).astype(jnp.bfloat16).reshape(-1, levels)  25.2 us
    reshape x1, local copies, waits for them, and re-layouts, vertical_step(): scaled = (modal_part / divisor).astype(jnp.bfloat16).reshape(-1, levels)  18.9 us
    dot_general x1, matrix products, per_device(): jnp.einsum('snj,snc->jsc', legendre, spec_state, preferred_element_type=j...  16.3 us
  transfers between devices with their start and end apart: 2, of which 2 were waited for; matrix products, arithmetic and copies ran while one was open for 2% of the time, Pallas kernels for 0%

commit v1 on v0

v1 whole, which is shorter than its diff:
```python
import functools

import jax
import jax.numpy as jnp
from jax import lax
from jax.experimental import pallas as pl
from jax.experimental.pallas import tpu as pltpu
from jax.sharding import PartitionSpec as P

NMAX = 2559
VMEM_BYTES = 56 * 1024 * 1024
GROUP = 16


def pack_body(north_ref, south_ref, counts_ref, twice_ref, out_ref):
    _, group, lat_dev, slots = north_ref.shape
    live = twice_ref[...] < counts_ref[...]
    summed = north_ref[0].astype(jnp.float32) + south_ref[0].astype(jnp.float32)
    summed = jnp.where(live[None], summed, 0.0).reshape(group * lat_dev, slots)
    out_ref[...] = summed.astype(jnp.bfloat16).T


def pack(part, north, south, counts, twice):
    _, levels, lat_dev, slots = north.shape
    rows = pl.BlockSpec((1, GROUP, lat_dev, slots), lambda i: (part, i, 0, 0))
    return pl.pallas_call(
        pack_body,
        grid=(pl.cdiv(levels, GROUP),),
        in_specs=[
            rows,
            rows,
            pl.BlockSpec((lat_dev, 1), lambda i: (0, 0)),
            pl.BlockSpec((1, slots), lambda i: (0, 0)),
        ],
        out_specs=pl.BlockSpec((slots, GROUP * lat_dev), lambda i: (0, i)),
        out_shape=jax.ShapeDtypeStruct((slots, levels * lat_dev), jnp.bfloat16),
        compiler_params=pltpu.CompilerParams(vmem_limit_bytes=VMEM_BYTES),
        cost_estimate=pl.CostEstimate(
            flops=2 * levels * lat_dev * slots,
            bytes_accessed=6 * levels * lat_dev * slots,
            transcendentals=0,
        ),
    )(north, south, counts, twice)


def unpack_body(in_ref, *refs):
    out_ref = refs[-1]
    _, group, lat_dev, slots = out_ref.shape
    rows = in_ref[...].T.astype(jnp.float32).reshape(group, lat_dev, slots)
    out_ref[0] = rows.astype(jnp.bfloat16)


def unpack(part, parts, levels, lat_dev, received, earlier):
    slots = received.shape[0]
    in_specs = [pl.BlockSpec((slots, GROUP * lat_dev), lambda i: (0, i))]
    operands = [received]
    aliases = {}
    if earlier is not None:
        in_specs.append(pl.BlockSpec(memory_space=pl.ANY))
        operands.append(earlier)
        aliases = {1: 0}
    return pl.pallas_call(
        unpack_body,
        grid=(pl.cdiv(levels, GROUP),),
        in_specs=in_specs,
        out_specs=pl.BlockSpec((1, GROUP, lat_dev, slots), lambda i: (part, i, 0, 0)),
        out_shape=jax.ShapeDtypeStruct((parts, levels, lat_dev, slots), jnp.bfloat16),
        input_output_aliases=aliases,
        compiler_params=pltpu.CompilerParams(vmem_limit_bytes=VMEM_BYTES),
        cost_estimate=pl.CostEstimate(
            flops=levels * lat_dev * slots,
            bytes_accessed=4 * levels * lat_dev * slots,
            transcendentals=0,
        ),
    )(*operands)


def step_body(waves_ref, sym_ref, legendre_ref, counts_ref, rates_ref, to_ref, from_ref, spec_ref, new_ref):
    wave = waves_ref[pl.program_id(0)]
    row_total = legendre_ref.shape[1]
    matrix = legendre_ref[0]
    direct = lax.dot_general(
        sym_ref[0], matrix, (((1,), (1,)), ((), ())), preferred_element_type=jnp.float32
    ).astype(jnp.bfloat16)
    modal = jnp.dot(to_ref[...], direct, preferred_element_type=jnp.float32)
    degree = wave + 2 * lax.broadcasted_iota(jnp.int32, (1, row_total), 1)
    degree_f = degree.astype(jnp.float32)
    scaled_degree = degree_f * (degree_f + 1.0) / float(NMAX * (NMAX + 1))
    scaled = (modal / (1.0 + rates_ref[...] * scaled_degree)).astype(jnp.bfloat16)
    state = jnp.dot(from_ref[...], scaled, preferred_element_type=jnp.float32)
    state = jnp.where(degree <= NMAX, state, 0.0).astype(jnp.bfloat16)
    spec_ref[0] = state
    rows = jnp.dot(state, matrix, preferred_element_type=jnp.float32)
    new_ref[0] = jnp.where(2 * wave < counts_ref[...], rows, 0.0).astype(jnp.bfloat16)


def spectral_step(symmetric, legendre, own_waves, counts, rates, to_modes_t, from_modes_t):
    slot_dev, levels, lat_total = symmetric.shape
    row_total = legendre.shape[1]
    whole = lambda shape: pl.BlockSpec(shape, lambda s, waves: (0,) * len(shape))
    spec_shape = jax.ShapeDtypeStruct((slot_dev, levels, row_total), jnp.bfloat16)
    new_shape = jax.ShapeDtypeStruct((slot_dev, levels, lat_total), jnp.bfloat16)
    per_slot = lambda a, b: pl.BlockSpec((1, a, b), lambda s, waves: (s, 0, 0))
    return pl.pallas_call(
        step_body,
        grid_spec=pltpu.PrefetchScalarGridSpec(
            num_scalar_prefetch=1,
            grid=(slot_dev,),
            in_specs=[
                per_slot(levels, lat_total),
                per_slot(row_total, lat_total),
                whole((1, lat_total)),
                whole((levels, 1)),
                whole((levels, levels)),
                whole((levels, levels)),
            ],
            out_specs=[per_slot(levels, row_total), per_slot(levels, lat_total)],
        ),
        out_shape=[spec_shape, new_shape],
        compiler_params=pltpu.CompilerParams(vmem_limit_bytes=VMEM_BYTES),
        cost_estimate=pl.CostEstimate(
            flops=4 * slot_dev * row_total * lat_total * levels,
            bytes_accessed=2 * slot_dev * lat_total * (row_total + 3 * levels),
            transcendentals=0,
        ),
    )(own_waves, symmetric, legendre, counts, rates, to_modes_t, from_modes_t)


def per_device(
    north_rows, south_rows, lon_counts, slot_wave, legendre, mode_rates, to_modes, from_modes
):
    lat_dev, slots, channels = north_rows.shape
    slot_dev, row_total, lat_total = legendre.shape
    levels = to_modes.shape[0]
    parts = channels // levels
    devices = slots // slot_dev
    my_index = lax.axis_index("wave")
    own_waves = lax.dynamic_slice_in_dim(slot_wave, my_index * slot_dev, slot_dev)
    local_counts = lax.dynamic_slice_in_dim(lon_counts, my_index * lat_dev, lat_dev)[:, None]
    twice = 2 * slot_wave[None, :]
    north = jnp.transpose(north_rows, (2, 0, 1)).reshape(parts, levels, lat_dev, slots)
    south = jnp.transpose(south_rows, (2, 0, 1)).reshape(parts, levels, lat_dev, slots)
    exchange = functools.partial(
        lax.all_to_all, axis_name="wave", split_axis=0, concat_axis=0, tiled=True
    )
    columns = [exchange(pack(part, north, south, local_counts, twice)) for part in range(parts)]
    states = []
    returned = []
    for part in range(parts):
        symmetric = columns[part].reshape(devices, slot_dev, levels, lat_dev)
        symmetric = jnp.transpose(symmetric, (1, 2, 0, 3)).reshape(slot_dev, levels, lat_total)
        state, rows = spectral_step(
            symmetric, legendre, own_waves, lon_counts[None, :], mode_rates[:, None],
            to_modes.T, from_modes.T,
        )
        states.append(state)
        rows = rows.reshape(slot_dev, levels, devices, lat_dev)
        rows = jnp.transpose(rows, (2, 0, 1, 3)).reshape(slots, levels * lat_dev)
        returned.append(exchange(rows))
    new_rows = None
    for part in range(parts):
        new_rows = unpack(part, parts, levels, lat_dev, returned[part], new_rows)
    new_rows = jnp.transpose(new_rows.reshape(channels, lat_dev, slots), (1, 2, 0))
    spec_state = jnp.transpose(jnp.concatenate(states, axis=1), (0, 2, 1))
    return (spec_state, new_rows)


def solution(mesh):
    in_specs = (
        P(("grp", "wave"), None, None),
        P(("grp", "wave"), None, None),
        P(),
        P(),
        P("wave", None, None),
        P(),
        P(),
        P(),
    )
    out_specs = (P(("grp", "wave"), None, None), P(("grp", "wave"), None, None))
    return jax.shard_map(
        per_device, mesh=mesh, in_specs=in_specs, out_specs=out_specs, check_vma=False
    )
```

time: 584 us -> 336 us (0.58)
  waiting for transfers between devices: 329 us -> 104 us
  Pallas kernels: 0 us -> 83.2 us
  matrix products: 59.3 us -> 0 us
  local copies, waits for them, and re-layouts: 153 us -> 115 us
  other arithmetic: 27.3 us -> 4.72 us
  starting transfers between devices: 11.6 us -> 23.5 us
    all_to_all x2 -> x4, waiting for transfers between devices: 329 us -> 104 us  [the longest x2 55 us: per_device(): exchange(pack(part, north, south, local_counts, twice))]
    pallas_call x0 -> x6, Pallas kernels: none -> 83.2 us  [the longest x2 53.7 us: spectral_step(): pl.pallas_call(step_body, grid_spec=pltpu.PrefetchScalarGridSpec(num_scal...]
    dot_general x4 -> x0, matrix products: 59.3 us -> none  [the longest x1 25.7 us: per_device(): jnp.einsum('snj,jsc->snc', legendre, columns, preferred_element_type=jnp....]
    convert_element_type x3 -> x0, local copies, waits for them, and re-layouts: 39.9 us -> none  [the longest x1 25.2 us: vertical_step(): scaled = (modal_part / divisor).astype(jnp.bfloat16).reshape(-1, levels)]
    unnamed x16 -> x17, local copies, waits for them, and re-layouts: 42.2 us -> 8.14 us
    reshape x2 -> x8, local copies, waits for them, and re-layouts: 34.9 us -> 66.3 us  [the longest x4 30.4 us: per_device(): jnp.transpose(symmetric, (1, 2, 0, 3)).reshape(slot_dev, levels, lat_total)]
    convert_element_type x3 -> x0, other arithmetic: 23.7 us -> none  [the longest x1 9.62 us: per_device(): jnp.where(live_here[:, :, None], summed, 0.0).astype(jnp.bfloat16)]
    all_to_all x3 -> x2, local copies, waits for them, and re-layouts: 35.6 us -> 15 us  [per_device(): returned.append(exchange(rows))]
  transfers between devices with their start and end apart: 2 -> 4, of which waited for: 2 -> 2; matrix products, arithmetic and copies ran while one was open for 2% -> 30% of each run, Pallas kernels for 0% -> 21%
where the time goes in v1:
time: 336 us; the launch traced here: 331 us
  local copies, waits for them, and re-layouts  115 us (34%)
  waiting for transfers between devices  104 us (31%)
  Pallas kernels  83.2 us (25%)
  starting transfers between devices  23.5 us (7%)
  other arithmetic  4.72 us (1%)
    all_to_all x2, waiting for transfers between devices, per_device(): exchange(pack(part, north, south, local_counts, twice))  55 us
    pallas_call x2, Pallas kernels, spectral_step(): pl.pallas_call(step_body, grid_spec=pltpu.PrefetchScalarGridSpec(num_scal...  53.7 us
    all_to_all x2, waiting for transfers between devices, per_device(): returned.append(exchange(rows))  48.9 us
    reshape x4, local copies, waits for them, and re-layouts, per_device(): jnp.transpose(symmetric, (1, 2, 0, 3)).reshape(slot_dev, levels, lat_total)  30.4 us
    reshape x2, local copies, waits for them, and re-layouts, per_device(): rows = rows.reshape(slot_dev, levels, devices, lat_dev)  18 us
    reshape x2, local copies, waits for them, and re-layouts, per_device(): symmetric = columns[part].reshape(devices, slot_dev, levels, lat_dev)  17.9 us
    pallas_call x2, Pallas kernels, pack(): pl.pallas_call(pack_body, grid=(pl.cdiv(levels, GROUP),), in_specs=[rows,...  15.7 us
    all_to_all x2, local copies, waits for them, and re-layouts, per_device(): returned.append(exchange(rows))  15 us
  transfers between devices with their start and end apart: 4, of which 2 were waited for; matrix products, arithmetic and copies ran while one was open for 30% of the time, Pallas kernels for 21%

profile of v1, /device:TPU:13, one launch (start us, length us, event | category | flops | bytes accessed | tf_op | source)
XLA Modules:
  0.0 330.7 jit_solution(6428856220733570196)
XLA Ops:
  0.6 1.2 multiply_bitcast_fusion.twice_ref
  1.8 0.8 dynamic-slice_bitcast_fusion
  2.6 0.7 copy.18.counts_ref
  3.3 7.8 %shard_map.95 = bf16[128,10960]{1,0:T(8,128)(2,1)} custom-call(bf16[2,137,80,128]{3,2,1,0:T(8,128)(2,1)} %bitcast.34, bf16[2,137,80,128]{3,2,1,0:T(8,128)(2,1)} %bitcast.36, s32[80,1]{1,0:T(8,128)} %copy.18.counts_ref, s32[1,128]{1,0:T(1,128)} %multiply_bitcast_fusion.twice_ref), custom_call_target="tpu_custom_call" | custom-call | flops 2805760 | bytes 8417280 | tf_op jit(solution)/shard_map/pallas_call | solution.py:26
  11.1 6.5 %all-to-all-start = ((bf16[16,8,10960]{2,1,0:T(8,128)(2,1)}), bf16[16,8,10960]{2,1,0:T(8,128)(2,1)S(1)}, u32[]{:S(2)}, u32[]{:S(2)}) async-start(bf16[16,8,10960]{2,1,0:T(8,128)(2,1)} %bitcast.45), calls=%async_computation | async-start | bytes 5636096 | tf_op jit(solution)/shard_map/all_to_all | solution.py:146
  17.7 7.9 %shard_map.97 = bf16[128,10960]{1,0:T(8,128)(2,1)} custom-call(bf16[2,137,80,128]{3,2,1,0:T(8,128)(2,1)} %bitcast.35, bf16[2,137,80,128]{3,2,1,0:T(8,128)(2,1)} %bitcast.37, s32[80,1]{1,0:T(8,128)} %copy.18.counts_ref, s32[1,128]{1,0:T(1,128)} %multiply_bitcast_fusion.twice_ref), custom_call_target="tpu_custom_call" | custom-call | flops 2805760 | bytes 8417280 | tf_op jit(solution)/shard_map/pallas_call | solution.py:26
  25.6 0.0 copy-start.4
  25.6 0.0 copy-start.6
  25.6 0.0 copy-start.5
  25.6 0.0 copy-start.2
  25.6 0.0 copy-start.3
  25.6 55.0 %all-to-all-done = bf16[16,8,10960]{2,1,0:T(8,128)(2,1)S(1)} async-done(((bf16[16,8,10960]{2,1,0:T(8,128)(2,1)}), bf16[16,8,10960]{2,1,0:T(8,128)(2,1)S(1)}, u32[]{:S(2)}, u32[]{:S(2)}) %all-to-all-start) | async-done | bytes 2805792 | tf_op jit(solution)/shard_map/all_to_all | solution.py:146
  80.6 0.0 copy-start
  80.6 1.6 copy-done
  82.1 4.9 %all-to-all-start.1 = ((bf16[16,8,10960]{2,1,0:T(8,128)(2,1)}), bf16[16,8,10960]{2,1,0:T(8,128)(2,1)S(1)}, u32[]{:S(2)}, u32[]{:S(2)}) async-start(bf16[16,8,10960]{2,1,0:T(8,128)(2,1)} %bitcast.43), calls=%async_computation.1 | async-start | bytes 5636096 | tf_op jit(solution)/shard_map/all_to_all | solution.py:146
  87.0 0.0 copy-done.4
  87.0 0.6 broadcast_in_dim.13.counts_ref
  87.6 0.0 copy-done.6
  87.6 0.6 dynamic_slice.6.waves_ref
  88.3 0.0 copy-done.5
  88.3 0.7 copy.23.rates_ref
  89.0 0.0 copy-done.2
  89.0 0.7 copy.20
  89.8 0.0 copy-done.3
  89.8 0.7 copy.21
  90.5 9.4 %reshape.48 = bf16[16,8,137,80]{3,2,1,0:T(8,128)(2,1)} reshape(bf16[16,8,10960]{2,1,0:T(8,128)(2,1)} %copy-done) | data formatting | bytes 5611520 | tf_op jit(solution)/shard_map/reshape | solution.py:150
  99.9 7.4 %copy.33 = bf16[8,137,16,80]{3,2,1,0:T(8,128)(2,1)} copy(bf16[8,137,16,80]{3,1,0,2:T(8,128)(2,1)} %bitcast.39) | data formatting | bytes 5611520 | tf_op jit(solution)/shard_map/reshape | solution.py:151
  107.3 7.9 %reshape.55.sym_ref = bf16[8,137,1280]{2,1,0:T(8,128)(2,1)} reshape(bf16[8,137,16,80]{3,2,1,0:T(8,128)(2,1)} %copy.33) | data formatting | bytes 5611520 | tf_op jit(solution)/shard_map/reshape | solution.py:151
  115.1 22.1 %shard_map.96 = (bf16[8,137,1280]{2,1,0:T(8,128)(2,1)}, bf16[8,137,1280]{2,1,0:T(8,128)(2,1)}) custom-call(s32[8]{0:T(128)} %dynamic_slice.6.waves_ref, bf16[8,137,1280]{2,1,0:T(8,128)(2,1)} %reshape.55.sym_ref, bf16[8,1280,1280]{2,1,0:T(8,128)(2,1)} %legendre_ref.3, s32[1,1280]{1,0:T(1,128)} %broadcast_in_dim.13.counts_ref, f32[137,1]{1,0:T(8,128)} %copy.23.rates_ref, ...), custom_call_target="tpu_custom_call" | custom-call | flops 7182745600 | bytes 34631680 | tf_op jit(solution)/shard_map/pallas_call | solution.py:104
  137.2 4.2 %copy.30 = bf16[8,137,1280]{2,0,1:T(8,128)(2,1)} copy(bf16[8,137,1280]{2,1,0:T(8,128)(2,1)} %get-tuple-element.9) | data formatting | bytes 5611520 | tf_op jit(solution)/shard_map/pallas_call | solution.py:104
  141.4 9.3 %reshape.53 = bf16[8,137,16,80]{3,2,0,1:T(8,128)(2,1)} reshape(bf16[8,137,1280]{2,0,1:T(8,128)(2,1)} %copy.30) | data formatting | bytes 5611520 | tf_op jit(solution)/shard_map/reshape | solution.py:157
  150.8 7.4 %copy.31 = bf16[16,8,137,80]{3,2,1,0:T(8,128)(2,1)} copy(bf16[16,8,137,80]{3,0,1,2:T(8,128)(2,1)} %bitcast.41) | data formatting | bytes 5611520 | tf_op jit(solution)/shard_map/transpose | solution.py:158
  158.2 7.5 %all_to_all.33 = bf16[16,8,10960]{2,1,0:T(8,128)(2,1)} reshape(bf16[16,8,137,80]{3,2,1,0:T(8,128)(2,1)} %copy.31) | data formatting | bytes 5611520 | tf_op jit(solution)/shard_map/all_to_all | solution.py:159
  165.7 0.0 all-to-all-done.1
  165.7 6.0 %all-to-all-start.3 = ((bf16[16,8,10960]{2,1,0:T(8,128)(2,1)}), bf16[16,8,10960]{2,1,0:T(8,128)(2,1)}, u32[]{:S(2)}, u32[]{:S(2)}) async-start(bf16[16,8,10960]{2,1,0:T(8,128)(2,1)} %all_to_all.33), calls=%async_computation.3 | async-start | bytes 5636096 | tf_op jit(solution)/shard_map/all_to_all | solution.py:159
  171.7 8.5 %reshape.50 = bf16[16,8,137,80]{3,2,1,0:T(8,128)(2,1)} reshape(bf16[16,8,10960]{2,1,0:T(8,128)(2,1)S(1)} %all-to-all-done.1) | data formatting | bytes 5611520 | tf_op jit(solution)/shard_map/reshape | solution.py:150
  180.1 7.4 %copy.34 = bf16[8,137,16,80]{3,2,1,0:T(8,128)(2,1)} copy(bf16[8,137,16,80]{3,1,0,2:T(8,128)(2,1)} %bitcast.40) | data formatting | bytes 5611520 | tf_op jit(solution)/shard_map/reshape | solution.py:151
  187.5 7.9 %reshape.56.sym_ref = bf16[8,137,1280]{2,1,0:T(8,128)(2,1)} reshape(bf16[8,137,16,80]{3,2,1,0:T(8,128)(2,1)} %copy.34) | data formatting | bytes 5611520 | tf_op jit(solution)/shard_map/reshape | solution.py:151
  195.4 31.6 %shard_map.98 = (bf16[8,137,1280]{2,1,0:T(8,128)(2,1)}, bf16[8,137,1280]{2,1,0:T(8,128)(2,1)}) custom-call(s32[8]{0:T(128)} %dynamic_slice.6.waves_ref, bf16[8,137,1280]{2,1,0:T(8,128)(2,1)} %reshape.56.sym_ref, bf16[8,1280,1280]{2,1,0:T(8,128)(2,1)} %legendre_ref.3, s32[1,1280]{1,0:T(1,128)} %broadcast_in_dim.13.counts_ref, f32[137,1]{1,0:T(8,128)} %copy.23.rates_ref, ...), custom_call_target="tpu_custom_call" | custom-call | flops 7182745600 | bytes 34631680 | tf_op jit(solution)/shard_map/pallas_call | solution.py:104
  227.0 2.7 copy.28
  229.6 8.6 %reshape.52 = bf16[8,137,16,80]{3,2,0,1:T(8,128)(2,1)} reshape(bf16[8,137,1280]{2,0,1:T(8,128)(2,1)S(1)} %copy.28) | data formatting | bytes 5611520 | tf_op jit(solution)/shard_map/reshape | solution.py:157
  238.3 7.4 %copy.29 = bf16[16,8,137,80]{3,2,1,0:T(8,128)(2,1)} copy(bf16[16,8,137,80]{3,0,1,2:T(8,128)(2,1)} %bitcast.42) | data formatting | bytes 5611520 | tf_op jit(solution)/shard_map/transpose | solution.py:158
  245.7 7.5 %all_to_all.30 = bf16[16,8,10960]{2,1,0:T(8,128)(2,1)} reshape(bf16[16,8,137,80]{3,2,1,0:T(8,128)(2,1)} %copy.29) | data formatting | bytes 5611520 | tf_op jit(solution)/shard_map/all_to_all | solution.py:159
  253.2 0.0 all-to-all-done.3
  253.2 6.0 %all-to-all-start.2 = ((bf16[16,8,10960]{2,1,0:T(8,128)(2,1)}), bf16[16,8,10960]{2,1,0:T(8,128)(2,1)S(1)}, u32[]{:S(2)}, u32[]{:S(2)}) async-start(bf16[16,8,10960]{2,1,0:T(8,128)(2,1)} %all_to_all.30), calls=%async_computation.2 | async-start | bytes 5636096 | tf_op jit(solution)/shard_map/all_to_all | solution.py:159
  259.2 3.5 %maximum_bitcast_fusion = bf16[8,1280,274]{1,2,0:T(8,128)(2,1)S(1)} fusion(bf16[8,137,1280]{2,1,0:T(8,128)(2,1)} %get-tuple-element.7, bf16[8,137,1280]{2,1,0:T(8,128)(2,1)} %get-tuple-element.6), kind=kLoop, calls=%fused_computation | loop fusion | flops 11223040 | bytes 11223040 | tf_op jit(solution)/shard_map/transpose | solution.py:164
  262.7 3.6 %copy.32 = bf16[8,1280,274]{1,0,2:T(8,128)(2,1)} copy(bf16[8,1280,274]{1,2,0:T(8,128)(2,1)S(1)} %maximum_bitcast_fusion) | data formatting | bytes 11223040
  266.3 6.9 %shard_map.99.refs_0_ = bf16[2,137,80,128]{3,2,1,0:T(8,128)(2,1)} custom-call(bf16[128,10960]{1,0:T(8,128)(2,1)} %bitcast.19.in_ref), custom_call_target="tpu_custom_call" | custom-call | flops 1402880 | bytes 5611520 | tf_op jit(solution)/shard_map/pallas_call | solution.py:62
  273.2 48.9 %all-to-all-done.2 = bf16[16,8,10960]{2,1,0:T(8,128)(2,1)S(1)} async-done(((bf16[16,8,10960]{2,1,0:T(8,128)(2,1)}), bf16[16,8,10960]{2,1,0:T(8,128)(2,1)S(1)}, u32[]{:S(2)}, u32[]{:S(2)}) %all-to-all-start.2) | async-done | bytes 2805792 | tf_op jit(solution)/shard_map/all_to_all | solution.py:159
  322.1 0.0 copy-start.1
  322.1 1.6 copy-done.1
  323.6 6.9 %shard_map.100 = bf16[2,137,80,128]{3,2,1,0:T(8,128)(2,1)} custom-call(bf16[128,10960]{1,0:T(8,128)(2,1)} %bitcast.44, bf16[2,137,80,128]{3,2,1,0:T(8,128)(2,1)} %shard_map.99.refs_0_), custom_call_target="tpu_custom_call", output_to_operand_aliasing={{}: (1, {})} | custom-call | flops 1402880 | bytes 5611520 | tf_op jit(solution)/shard_map/pallas_call | solution.py:62
Async XLA Ops:
  11.1 69.4 %all-to-all-start = ((bf16[16,8,10960]{2,1,0:T(8,128)(2,1)}), bf16[16,8,10960]{2,1,0:T(8,128)(2,1)S(1)}, u32[]{:S(2)}, u32[]{:S(2)}) async-start(bf16[16,8,10960]{2,1,0:T(8,128)(2,1)} %bitcast.45), calls=%async_computation | async-start | bytes 5636096 | tf_op jit(solution)/shard_map/all_to_all | solution.py:146
  25.6 61.5 %copy-start.4 = (s32[1280]{0:T(1024)S(1)}, s32[1280]{0:T(1024)}, u32[]{:S(2)}) copy-start(s32[1280]{0:T(1024)} %param.10) | copy-start | bytes 15364
  25.6 62.1 %copy-start.6 = (s32[128]{0:T(128)S(1)}, s32[128]{0:T(128)}, u32[]{:S(2)}) copy-start(s32[128]{0:T(128)} %param.11) | copy-start | bytes 1540
  25.6 62.7 %copy-start.5 = (f32[137]{0:T(256)S(1)}, f32[137]{0:T(256)}, u32[]{:S(2)}) copy-start(f32[137]{0:T(256)} %param.13) | copy-start | bytes 1648
  25.6 63.5 %copy-start.2 = (bf16[137,137]{1,0:T(8,128)(2,1)S(1)}, bf16[137,137]{1,0:T(8,128)(2,1)}, u32[]{:S(2)}) copy-start(bf16[137,137]{1,0:T(8,128)(2,1)} %param.14) | copy-start | bytes 112618
  25.6 64.2 %copy-start.3 = (bf16[137,137]{1,0:T(8,128)(2,1)S(1)}, bf16[137,137]{1,0:T(8,128)(2,1)}, u32[]{:S(2)}) copy-start(bf16[137,137]{1,0:T(8,128)(2,1)} %param.15) | copy-start | bytes 112618
  80.6 1.6 copy-start
  82.1 83.5 %all-to-all-start.1 = ((bf16[16,8,10960]{2,1,0:T(8,128)(2,1)}), bf16[16,8,10960]{2,1,0:T(8,128)(2,1)S(1)}, u32[]{:S(2)}, u32[]{:S(2)}) async-start(bf16[16,8,10960]{2,1,0:T(8,128)(2,1)} %bitcast.43), calls=%async_computation.1 | async-start | bytes 5636096 | tf_op jit(solution)/shard_map/all_to_all | solution.py:146
  165.7 87.5 %all-to-all-start.3 = ((bf16[16,8,10960]{2,1,0:T(8,128)(2,1)}), bf16[16,8,10960]{2,1,0:T(8,128)(2,1)}, u32[]{:S(2)}, u32[]{:S(2)}) async-start(bf16[16,8,10960]{2,1,0:T(8,128)(2,1)} %all_to_all.33), calls=%async_computation.3 | async-start | bytes 5636096 | tf_op jit(solution)/shard_map/all_to_all | solution.py:159
  253.2 68.9 %all-to-all-start.2 = ((bf16[16,8,10960]{2,1,0:T(8,128)(2,1)}), bf16[16,8,10960]{2,1,0:T(8,128)(2,1)S(1)}, u32[]{:S(2)}, u32[]{:S(2)}) async-start(bf16[16,8,10960]{2,1,0:T(8,128)(2,1)} %all_to_all.30), calls=%async_computation.2 | async-start | bytes 5636096 | tf_op jit(solution)/shard_map/all_to_all | solution.py:159
  322.1 1.6 copy-start.1

commit v2 on v1

--- a/solution.py
+++ b/solution.py
@@ -1,4 +1,5 @@
 import functools
+import math
 
 import jax
 import jax.numpy as jnp
@@ -10,6 +11,7 @@
 NMAX = 2559
 VMEM_BYTES = 56 * 1024 * 1024
 GROUP = 16
+LANES = 128
 
 
 def pack_body(north_ref, south_ref, counts_ref, twice_ref, out_ref):
@@ -33,7 +35,7 @@
             pl.BlockSpec((1, slots), lambda i: (0, 0)),
         ],
         out_specs=pl.BlockSpec((slots, GROUP * lat_dev), lambda i: (0, i)),
-        out_shape=jax.ShapeDtypeStruct((slots, levels * lat_dev), jnp.bfloat16),
+        out_shape=jax.ShapeDtypeStruct((slots, pl.cdiv(levels * lat_dev, LANES) * LANES), jnp.bfloat16),
         compiler_params=pltpu.CompilerParams(vmem_limit_bytes=VMEM_BYTES),
         cost_estimate=pl.CostEstimate(
             flops=2 * levels * lat_dev * slots,
@@ -75,12 +77,129 @@
     )(*operands)
 
 
-def step_body(waves_ref, sym_ref, legendre_ref, counts_ref, rates_ref, to_ref, from_ref, spec_ref, new_ref):
-    wave = waves_ref[pl.program_id(0)]
-    row_total = legendre_ref.shape[1]
+def lane_runs(lanes, source):
+    runs = []
+    for lane in range(LANES):
+        where = source(lanes + lane)
+        if where is None:
+            continue
+        tile = (where[0], where[1] // LANES)
+        shift = (lane - where[1]) % LANES
+        if runs and runs[-1][1:] == (tile, shift):
+            runs[-1] = (lane + 1, tile, shift)
+        else:
+            runs.append((lane + 1, tile, shift))
+    return runs
+
+
+def merge_runs(runs, load, cache, lane_index):
+    out = None
+    for end, tile, shift in reversed(runs):
+        if (tile, shift) not in cache:
+            value = load(*tile)
+            cache[tile, shift] = pltpu.roll(value, shift, 1) if shift else value
+        value = cache[tile, shift]
+        out = value if out is None else jnp.where(lane_index < end, value, out)
+    return out
+
+
+def group_size(lat_dev):
+    return LANES // math.gcd(lat_dev, LANES)
+
+
+def spread(recv_ref, rows_ref, first, group, lat_dev, slot_dev):
+    lat_total = rows_ref.shape[0] * LANES
+    base = pl.multiple_of(first * lat_dev, LANES)
+    lane_index = lax.broadcasted_iota(jnp.int32, (slot_dev, LANES), 1)
+    pairs = {}
+
+    def load(device, tile):
+        pair = device // 2
+        if (pair, tile) not in pairs:
+            pairs[pair, tile] = recv_ref[
+                2 * pair * slot_dev : 2 * (pair + 1) * slot_dev, pl.ds(base + tile * LANES, LANES)
+            ].astype(jnp.float32)
+        at = (device % 2) * slot_dev
+        return pairs[pair, tile][at : at + slot_dev]
+
+    cache = {}
+    for lanes in range(0, lat_total, LANES):
+        for i in range(group):
+            runs = lane_runs(lanes, lambda j: (j // lat_dev, i * lat_dev + j % lat_dev))
+            row = pl.multiple_of((first + i) * slot_dev, slot_dev)
+            rows_ref[lanes // LANES, pl.ds(row, slot_dev), :] = merge_runs(
+                runs, load, cache, lane_index
+            )
+
+
+def gather(rows_ref, send_ref, first, group, lat_dev, slot_dev):
+    devices = rows_ref.shape[0] * LANES // lat_dev
+    base = pl.multiple_of(first * lat_dev, LANES)
+    lane_index = lax.broadcasted_iota(jnp.int32, (slot_dev, LANES), 1)
+    cache = {}
+
+    def load(i, tile):
+        row = pl.multiple_of((first + i) * slot_dev, slot_dev)
+        return rows_ref[tile, pl.ds(row, slot_dev), :]
+
+    for pair in range(devices // 2):
+        for lanes in range(0, group * lat_dev, LANES):
+            tiles = []
+            for device in (2 * pair, 2 * pair + 1):
+                runs = lane_runs(
+                    lanes,
+                    lambda l: (l // lat_dev, device * lat_dev + l % lat_dev)
+                    if l < group * lat_dev
+                    else None,
+                )
+                tiles.append(merge_runs(runs, load, cache, lane_index))
+            send_ref[
+                2 * pair * slot_dev : 2 * (pair + 1) * slot_dev, pl.ds(base + lanes, LANES)
+            ] = jnp.concatenate(tiles, axis=0).astype(jnp.bfloat16)
+
+
+def join_tiles(ref, rows):
+    return jnp.concatenate([ref[tile, rows, :] for tile in range(ref.shape[0])], axis=1)
+
+
+def split_tiles(ref, rows, value):
+    for tile in range(ref.shape[0]):
+        ref[tile, rows, :] = value[:, tile * LANES : (tile + 1) * LANES]
+
+
+def all_groups(levels, lat_dev, body):
+    group = group_size(lat_dev)
+    full = levels // group
+
+    @pl.loop(0, full)
+    def _(g):
+        body(g * group, group)
+
+    if levels % group:
+        body(full * group, levels % group)
+
+
+def step_body(waves_ref, recv_ref, legendre_ref, counts_ref, rates_ref, to_ref, from_ref, *refs):
+    state_ref, send_ref, rows_ref, spec_ref = refs[-4:]
+    slot = pl.program_id(0)
+    wave = waves_ref[slot]
+    row_total, lat_total = legendre_ref.shape[1:]
+    _, levels, slot_dev, _ = state_ref.shape
+    lat_dev = lat_total // (recv_ref.shape[0] // slot_dev)
+
+    @pl.when(slot == 0)
+    def _():
+        all_groups(
+            levels, lat_dev, lambda c, n: spread(recv_ref, rows_ref, c, n, lat_dev, slot_dev)
+        )
+
+    own = pl.ds(slot, levels, stride=slot_dev)
     matrix = legendre_ref[0]
     direct = lax.dot_general(
-        sym_ref[0], matrix, (((1,), (1,)), ((), ())), preferred_element_type=jnp.float32
+        join_tiles(rows_ref, own).astype(jnp.bfloat16),
+        matrix,
+        (((1,), (1,)), ((), ())),
+        preferred_element_type=jnp.float32,
     ).astype(jnp.bfloat16)
     modal = jnp.dot(to_ref[...], direct, preferred_element_type=jnp.float32)
     degree = wave + 2 * lax.broadcasted_iota(jnp.int32, (1, row_total), 1)
@@ -88,42 +207,69 @@
     scaled_degree = degree_f * (degree_f + 1.0) / float(NMAX * (NMAX + 1))
     scaled = (modal / (1.0 + rates_ref[...] * scaled_degree)).astype(jnp.bfloat16)
     state = jnp.dot(from_ref[...], scaled, preferred_element_type=jnp.float32)
-    state = jnp.where(degree <= NMAX, state, 0.0).astype(jnp.bfloat16)
-    spec_ref[0] = state
-    rows = jnp.dot(state, matrix, preferred_element_type=jnp.float32)
-    new_ref[0] = jnp.where(2 * wave < counts_ref[...], rows, 0.0).astype(jnp.bfloat16)
-
-
-def spectral_step(symmetric, legendre, own_waves, counts, rates, to_modes_t, from_modes_t):
-    slot_dev, levels, lat_total = symmetric.shape
-    row_total = legendre.shape[1]
+    state = jnp.where(degree <= NMAX, state, 0.0)
+    split_tiles(spec_ref, own, state)
+    rows = jnp.dot(state.astype(jnp.bfloat16), matrix, preferred_element_type=jnp.float32)
+    split_tiles(rows_ref, own, jnp.where(2 * wave < counts_ref[...], rows, 0.0))
+
+    @pl.when(slot == slot_dev - 1)
+    def _():
+        all_groups(
+            levels, lat_dev, lambda c, n: gather(rows_ref, send_ref, c, n, lat_dev, slot_dev)
+        )
+
+        @pl.loop(0, levels)
+        def _(c):
+            at = pl.multiple_of(c * slot_dev, slot_dev)
+            state_ref[0, c] = join_tiles(spec_ref, pl.ds(at, slot_dev)).astype(jnp.bfloat16)
+
+
+def spectral_step(part, parts, received, legendre, own_waves, counts, rates, to_t, from_t, earlier):
+    slots, width = received.shape
+    slot_dev, row_total, lat_total = legendre.shape
+    levels = to_t.shape[0]
     whole = lambda shape: pl.BlockSpec(shape, lambda s, waves: (0,) * len(shape))
-    spec_shape = jax.ShapeDtypeStruct((slot_dev, levels, row_total), jnp.bfloat16)
-    new_shape = jax.ShapeDtypeStruct((slot_dev, levels, lat_total), jnp.bfloat16)
-    per_slot = lambda a, b: pl.BlockSpec((1, a, b), lambda s, waves: (s, 0, 0))
+    in_specs = [
+        whole((slots, width)),
+        pl.BlockSpec((1, row_total, lat_total), lambda s, waves: (s, 0, 0)),
+        whole((1, lat_total)),
+        whole((levels, 1)),
+        whole((levels, levels)),
+        whole((levels, levels)),
+    ]
+    operands = [own_waves, received, legendre, counts, rates, to_t, from_t]
+    aliases = {}
+    if earlier is not None:
+        in_specs.append(pl.BlockSpec(memory_space=pl.ANY))
+        aliases = {len(operands): 0}
+        operands.append(earlier)
     return pl.pallas_call(
         step_body,
         grid_spec=pltpu.PrefetchScalarGridSpec(
             num_scalar_prefetch=1,
             grid=(slot_dev,),
-            in_specs=[
-                per_slot(levels, lat_total),
-                per_slot(row_total, lat_total),
-                whole((1, lat_total)),
-                whole((levels, 1)),
-                whole((levels, levels)),
-                whole((levels, levels)),
+            in_specs=in_specs,
+            out_specs=[
+                pl.BlockSpec((1, levels, slot_dev, row_total), lambda s, waves: (part, 0, 0, 0)),
+                whole((slots, width)),
             ],
-            out_specs=[per_slot(levels, row_total), per_slot(levels, lat_total)],
+            scratch_shapes=[
+                pltpu.VMEM((lat_total // LANES, levels * slot_dev, LANES), jnp.float32),
+                pltpu.VMEM((row_total // LANES, levels * slot_dev, LANES), jnp.float32),
+            ],
         ),
-        out_shape=[spec_shape, new_shape],
+        out_shape=[
+            jax.ShapeDtypeStruct((parts, levels, slot_dev, row_total), jnp.bfloat16),
+            jax.ShapeDtypeStruct((slots, width), jnp.bfloat16),
+        ],
+        input_output_aliases=aliases,
         compiler_params=pltpu.CompilerParams(vmem_limit_bytes=VMEM_BYTES),
         cost_estimate=pl.CostEstimate(
             flops=4 * slot_dev * row_total * lat_total * levels,
             bytes_accessed=2 * slot_dev * lat_total * (row_total + 3 * levels),
             transcendentals=0,
         ),
-    )(own_waves, symmetric, legendre, counts, rates, to_modes_t, from_modes_t)
+    )(*operands)
 
 
 def per_device(
@@ -133,7 +279,6 @@
     slot_dev, row_total, lat_total = legendre.shape
     levels = to_modes.shape[0]
     parts = channels // levels
-    devices = slots // slot_dev
     my_index = lax.axis_index("wave")
     own_waves = lax.dynamic_slice_in_dim(slot_wave, my_index * slot_dev, slot_dev)
     local_counts = lax.dynamic_slice_in_dim(lon_counts, my_index * lat_dev, lat_dev)[:, None]
@@ -144,24 +289,19 @@
         lax.all_to_all, axis_name="wave", split_axis=0, concat_axis=0, tiled=True
     )
     columns = [exchange(pack(part, north, south, local_counts, twice)) for part in range(parts)]
-    states = []
+    spec_state = None
     returned = []
     for part in range(parts):
-        symmetric = columns[part].reshape(devices, slot_dev, levels, lat_dev)
-        symmetric = jnp.transpose(symmetric, (1, 2, 0, 3)).reshape(slot_dev, levels, lat_total)
-        state, rows = spectral_step(
-            symmetric, legendre, own_waves, lon_counts[None, :], mode_rates[:, None],
-            to_modes.T, from_modes.T,
+        spec_state, rows = spectral_step(
+            part, parts, columns[part], legendre, own_waves, lon_counts[None, :],
+            mode_rates[:, None], to_modes.T, from_modes.T, spec_state,
         )
-        states.append(state)
-        rows = rows.reshape(slot_dev, levels, devices, lat_dev)
-        rows = jnp.transpose(rows, (2, 0, 1, 3)).reshape(slots, levels * lat_dev)
         returned.append(exchange(rows))
     new_rows = None
     for part in range(parts):
         new_rows = unpack(part, parts, levels, lat_dev, returned[part], new_rows)
     new_rows = jnp.transpose(new_rows.reshape(channels, lat_dev, slots), (1, 2, 0))
-    spec_state = jnp.transpose(jnp.concatenate(states, axis=1), (0, 2, 1))
+    spec_state = jnp.transpose(spec_state.reshape(channels, slot_dev, row_total), (1, 2, 0))
     return (spec_state, new_rows)
 
 

time: 336 us -> 297 us (0.88); the launches traced: 331 us -> 296 us
  local copies, waits for them, and re-layouts: 115 us -> 9.56 us
  waiting for transfers between devices: 104 us -> 168 us
  Pallas kernels: 83.2 us -> 94.5 us
  other arithmetic: 4.72 us -> 1.17 us
    reshape x8 -> x0, local copies, waits for them, and re-layouts: 66.3 us -> none  [the longest x4 30.4 us: per_device(): jnp.transpose(symmetric, (1, 2, 0, 3)).reshape(slot_dev, levels, lat_total)]
    all_to_all x2, waiting for transfers between devices: 48.9 us -> 86.4 us  [per_device(): returned.append(exchange(rows))]
    all_to_all x2, waiting for transfers between devices: 55 us -> 82 us  [per_device(): exchange(pack(part, north, south, local_counts, twice))]
    all_to_all x2 -> x0, local copies, waits for them, and re-layouts: 15 us -> none  [per_device(): returned.append(exchange(rows))]
    transpose x2 -> x0, local copies, waits for them, and re-layouts: 14.8 us -> none  [per_device(): rows = jnp.transpose(rows, (2, 0, 1, 3)).reshape(slots, levels * lat_dev)]
    pallas_call x2, Pallas kernels: 53.7 us -> 64.9 us  [spectral_step(): pl.pallas_call(step_body, grid_spec=pltpu.PrefetchScalarGridSpec(num_scal...]
    pallas_call x2 -> x0, local copies, waits for them, and re-layouts: 6.89 us -> none  [spectral_step(): pl.pallas_call(step_body, grid_spec=pltpu.PrefetchScalarGridSpec(num_scal...]
    transpose x1 -> x0, other arithmetic: 3.53 us -> none  [per_device(): spec_state = jnp.transpose(jnp.concatenate(states, axis=1), (0, 2, 1))]
  transfers between devices with their start and end apart: 4 -> 4, of which waited for: 2 -> 4; matrix products, arithmetic and copies ran while one was open for 30% -> 1% of each run, Pallas kernels for 21% -> 27%
where the time goes in v2:
time: 297 us; the launch traced here: 296 us
  waiting for transfers between devices  168 us (57%)
  Pallas kernels  94.5 us (32%)
  starting transfers between devices  21.3 us (7%)
  local copies, waits for them, and re-layouts  9.56 us (3%)
    all_to_all x2, waiting for transfers between devices, per_device(): returned.append(exchange(rows))  86.4 us
    all_to_all x2, waiting for transfers between devices, per_device(): exchange(pack(part, north, south, local_counts, twice))  82 us
    pallas_call x2, Pallas kernels, spectral_step(): pl.pallas_call(step_body, grid_spec=pltpu.PrefetchScalarGridSpec(num_scal...  64.9 us
    pallas_call x2, Pallas kernels, pack(): pl.pallas_call(pack_body, grid=(pl.cdiv(levels, GROUP),), in_specs=[rows,...  15.7 us
    pallas_call x2, Pallas kernels, unpack(): pl.pallas_call(unpack_body, grid=(pl.cdiv(levels, GROUP),), in_specs=in_s...  13.8 us
    all_to_all x2, starting transfers between devices, per_device(): exchange(pack(part, north, south, local_counts, twice))  11.5 us
    all_to_all x2, starting transfers between devices, per_device(): returned.append(exchange(rows))  9.82 us
    unnamed x18, local copies, waits for them, and re-layouts  6.18 us
  transfers between devices with their start and end apart: 4, of which 4 were waited for; matrix products, arithmetic and copies ran while one was open for 1% of the time, Pallas kernels for 27%

profile of v2, /device:TPU:13, one launch (start us, length us, event | category | flops | bytes accessed | tf_op | source)
XLA Modules:
  0.0 295.6 jit_solution(9202178219479184395)
XLA Ops:
  0.6 1.2 multiply_bitcast_fusion.twice_ref
  1.8 0.8 dynamic-slice_bitcast_fusion
  2.6 0.7 copy.16.counts_ref
  3.3 7.8 %shard_map.96 = bf16[128,11008]{1,0:T(8,128)(2,1)} custom-call(bf16[2,137,80,128]{3,2,1,0:T(8,128)(2,1)} %bitcast.27, bf16[2,137,80,128]{3,2,1,0:T(8,128)(2,1)} %bitcast.29, s32[80,1]{1,0:T(8,128)} %copy.16.counts_ref, s32[1,128]{1,0:T(1,128)} %multiply_bitcast_fusion.twice_ref), custom_call_target="tpu_custom_call" | custom-call | flops 2805760 | bytes 8417280 | tf_op jit(solution)/shard_map/pallas_call | solution.py:28
  11.1 6.5 %all-to-all-start.1 = ((bf16[16,8,11008]{2,1,0:T(8,128)(2,1)}), bf16[16,8,11008]{2,1,0:T(8,128)(2,1)S(1)}, u32[]{:S(2)}, u32[]{:S(2)}) async-start(bf16[16,8,11008]{2,1,0:T(8,128)(2,1)} %bitcast.36), calls=%async_computation.1 | async-start | bytes 5636096 | tf_op jit(solution)/shard_map/all_to_all | solution.py:291
  17.7 7.9 %shard_map.95 = bf16[128,11008]{1,0:T(8,128)(2,1)} custom-call(bf16[2,137,80,128]{3,2,1,0:T(8,128)(2,1)} %bitcast.28, bf16[2,137,80,128]{3,2,1,0:T(8,128)(2,1)} %bitcast.30, s32[80,1]{1,0:T(8,128)} %copy.16.counts_ref, s32[1,128]{1,0:T(1,128)} %multiply_bitcast_fusion.twice_ref), custom_call_target="tpu_custom_call" | custom-call | flops 2805760 | bytes 8417280 | tf_op jit(solution)/shard_map/pallas_call | solution.py:28
  25.5 55.0 %all-to-all-done.1 = bf16[16,8,11008]{2,1,0:T(8,128)(2,1)S(1)} async-done(((bf16[16,8,11008]{2,1,0:T(8,128)(2,1)}), bf16[16,8,11008]{2,1,0:T(8,128)(2,1)S(1)}, u32[]{:S(2)}, u32[]{:S(2)}) %all-to-all-start.1) | async-done | bytes 2818080 | tf_op jit(solution)/shard_map/all_to_all | solution.py:291
  80.5 0.0 copy-start.2
  80.5 0.0 copy-start.5
  80.5 0.0 copy-start.7
  80.5 0.0 copy-start.6
  80.5 0.0 copy-start.3
  80.6 0.0 copy-start.4
  80.6 1.5 copy-done.2
  82.1 4.9 %all-to-all-start = ((bf16[16,8,11008]{2,1,0:T(8,128)(2,1)}), bf16[16,8,11008]{2,1,0:T(8,128)(2,1)S(1)}, u32[]{:S(2)}, u32[]{:S(2)}) async-start(bf16[16,8,11008]{2,1,0:T(8,128)(2,1)} %bitcast.35), calls=%async_computation | async-start | bytes 5636096 | tf_op jit(solution)/shard_map/all_to_all | solution.py:291
  87.0 0.0 copy-done.5
  87.0 0.6 broadcast_in_dim.13.counts_ref
  87.6 0.0 copy-done.7
  87.6 0.5 dynamic_slice.6.waves_ref
  88.2 0.0 copy-done.6
  88.2 0.7 copy.21.rates_ref
  88.9 0.0 copy-done.3
  88.9 0.7 copy.17
  89.7 0.0 copy-done.4
  89.7 0.7 copy.18
  90.4 32.5 %shard_map.97 = (bf16[2,137,8,1280]{3,2,1,0:T(8,128)(2,1)}, bf16[128,11008]{1,0:T(8,128)(2,1)}) custom-call(s32[8]{0:T(128)} %dynamic_slice.6.waves_ref, bf16[128,11008]{1,0:T(8,128)(2,1)} %bitcast.34, bf16[8,1280,1280]{2,1,0:T(8,128)(2,1)} %legendre_ref.3, s32[1,1280]{1,0:T(1,128)} %broadcast_in_dim.13.counts_ref, f32[137,1]{1,0:T(8,128)} %copy.21.rates_ref, ...), custom_call_target="tpu_custom_call" | custom-call | flops 7182745600 | bytes 34631680 | tf_op jit(solution)/shard_map/pallas_call | solution.py:246
  122.9 27.0 %all-to-all-done = bf16[16,8,11008]{2,1,0:T(8,128)(2,1)S(1)} async-done(((bf16[16,8,11008]{2,1,0:T(8,128)(2,1)}), bf16[16,8,11008]{2,1,0:T(8,128)(2,1)S(1)}, u32[]{:S(2)}, u32[]{:S(2)}) %all-to-all-start) | async-done | bytes 2818080 | tf_op jit(solution)/shard_map/all_to_all | solution.py:291
  149.9 0.0 copy-start.1
  149.9 1.6 copy-done.1
  151.4 4.9 %all-to-all-start.3 = ((bf16[16,8,11008]{2,1,0:T(8,128)(2,1)}), bf16[16,8,11008]{2,1,0:T(8,128)(2,1)S(1)}, u32[]{:S(2)}, u32[]{:S(2)}) async-start(bf16[16,8,11008]{2,1,0:T(8,128)(2,1)} %bitcast.38), calls=%async_computation.3 | async-start | bytes 5636096 | tf_op jit(solution)/shard_map/all_to_all | solution.py:299
  156.4 32.5 %shard_map.98 = (bf16[2,137,8,1280]{3,2,1,0:T(8,128)(2,1)}, bf16[128,11008]{1,0:T(8,128)(2,1)}) custom-call(s32[8]{0:T(128)} %dynamic_slice.6.waves_ref, bf16[128,11008]{1,0:T(8,128)(2,1)} %bitcast.33, bf16[8,1280,1280]{2,1,0:T(8,128)(2,1)} %legendre_ref.3, s32[1,1280]{1,0:T(1,128)} %broadcast_in_dim.13.counts_ref, ...), custom_call_target="tpu_custom_call", output_to_operand_aliasing={{0}: (7, {})} | custom-call | flops 7182745600 | bytes 34631680 | tf_op jit(solution)/shard_map/pallas_call | solution.py:246
  188.8 30.4 %all-to-all-done.3 = bf16[16,8,11008]{2,1,0:T(8,128)(2,1)S(1)} async-done(((bf16[16,8,11008]{2,1,0:T(8,128)(2,1)}), bf16[16,8,11008]{2,1,0:T(8,128)(2,1)S(1)}, u32[]{:S(2)}, u32[]{:S(2)}) %all-to-all-start.3) | async-done | bytes 2818080 | tf_op jit(solution)/shard_map/all_to_all | solution.py:299
  219.2 0.0 copy-start
  219.2 1.6 copy-done
  220.8 4.9 %all-to-all-start.2 = ((bf16[16,8,11008]{2,1,0:T(8,128)(2,1)}), bf16[16,8,11008]{2,1,0:T(8,128)(2,1)}, u32[]{:S(2)}, u32[]{:S(2)}) async-start(bf16[16,8,11008]{2,1,0:T(8,128)(2,1)} %bitcast.39), calls=%async_computation.2 | async-start | bytes 5636096 | tf_op jit(solution)/shard_map/all_to_all | solution.py:299
  225.7 6.9 %shard_map.99.refs_0_ = bf16[2,137,80,128]{3,2,1,0:T(8,128)(2,1)} custom-call(bf16[128,11008]{1,0:T(8,128)(2,1)} %bitcast.32), custom_call_target="tpu_custom_call" | custom-call | flops 1402880 | bytes 5611520 | tf_op jit(solution)/shard_map/pallas_call | solution.py:64
  232.6 56.0 %all-to-all-done.2 = bf16[16,8,11008]{2,1,0:T(8,128)(2,1)} async-done(((bf16[16,8,11008]{2,1,0:T(8,128)(2,1)}), bf16[16,8,11008]{2,1,0:T(8,128)(2,1)}, u32[]{:S(2)}, u32[]{:S(2)}) %all-to-all-start.2) | async-done | bytes 2818080 | tf_op jit(solution)/shard_map/all_to_all | solution.py:299
  288.7 6.9 %shard_map.100 = bf16[2,137,80,128]{3,2,1,0:T(8,128)(2,1)} custom-call(bf16[128,11008]{1,0:T(8,128)(2,1)} %bitcast.18.in_ref, bf16[2,137,80,128]{3,2,1,0:T(8,128)(2,1)} %shard_map.99.refs_0_), custom_call_target="tpu_custom_call", output_to_operand_aliasing={{}: (1, {})} | custom-call | flops 1402880 | bytes 5611520 | tf_op jit(solution)/shard_map/pallas_call | solution.py:64
Async XLA Ops:
  11.1 69.4 %all-to-all-start.1 = ((bf16[16,8,11008]{2,1,0:T(8,128)(2,1)}), bf16[16,8,11008]{2,1,0:T(8,128)(2,1)S(1)}, u32[]{:S(2)}, u32[]{:S(2)}) async-start(bf16[16,8,11008]{2,1,0:T(8,128)(2,1)} %bitcast.36), calls=%async_computation.1 | async-start | bytes 5636096 | tf_op jit(solution)/shard_map/all_to_all | solution.py:291
  80.5 1.6 copy-start.2
  80.5 6.5 %copy-start.5 = (s32[1280]{0:T(1024)S(1)}, s32[1280]{0:T(1024)}, u32[]{:S(2)}) copy-start(s32[1280]{0:T(1024)} %param.10) | copy-start | bytes 15364
  80.5 7.1 %copy-start.7 = (s32[128]{0:T(128)S(1)}, s32[128]{0:T(128)}, u32[]{:S(2)}) copy-start(s32[128]{0:T(128)} %param.11) | copy-start | bytes 1540
  80.5 7.6 %copy-start.6 = (f32[137]{0:T(256)S(1)}, f32[137]{0:T(256)}, u32[]{:S(2)}) copy-start(f32[137]{0:T(256)} %param.13) | copy-start | bytes 1648
  80.5 8.4 %copy-start.3 = (bf16[137,137]{1,0:T(8,128)(2,1)S(1)}, bf16[137,137]{1,0:T(8,128)(2,1)}, u32[]{:S(2)}) copy-start(bf16[137,137]{1,0:T(8,128)(2,1)} %param.14) | copy-start | bytes 112618
  80.6 9.1 %copy-start.4 = (bf16[137,137]{1,0:T(8,128)(2,1)S(1)}, bf16[137,137]{1,0:T(8,128)(2,1)}, u32[]{:S(2)}) copy-start(bf16[137,137]{1,0:T(8,128)(2,1)} %param.15) | copy-start | bytes 112618
  82.1 67.8 %all-to-all-start = ((bf16[16,8,11008]{2,1,0:T(8,128)(2,1)}), bf16[16,8,11008]{2,1,0:T(8,128)(2,1)S(1)}, u32[]{:S(2)}, u32[]{:S(2)}) async-start(bf16[16,8,11008]{2,1,0:T(8,128)(2,1)} %bitcast.35), calls=%async_computation | async-start | bytes 5636096 | tf_op jit(solution)/shard_map/all_to_all | solution.py:291
  149.9 1.6 copy-start.1
  151.4 67.8 %all-to-all-start.3 = ((bf16[16,8,11008]{2,1,0:T(8,128)(2,1)}), bf16[16,8,11008]{2,1,0:T(8,128)(2,1)S(1)}, u32[]{:S(2)}, u32[]{:S(2)}) async-start(bf16[16,8,11008]{2,1,0:T(8,128)(2,1)} %bitcast.38), calls=%async_computation.3 | async-start | bytes 5636096 | tf_op jit(solution)/shard_map/all_to_all | solution.py:299
  219.2 1.6 copy-start
  220.8 67.9 %all-to-all-start.2 = ((bf16[16,8,11008]{2,1,0:T(8,128)(2,1)}), bf16[16,8,11008]{2,1,0:T(8,128)(2,1)}, u32[]{:S(2)}, u32[]{:S(2)}) async-start(bf16[16,8,11008]{2,1,0:T(8,128)(2,1)} %bitcast.39), calls=%async_computation.2 | async-start | bytes 5636096 | tf_op jit(solution)/shard_map/all_to_all | solution.py:299

commit v3 on v2

--- a/solution.py
+++ b/solution.py
@@ -9,31 +9,30 @@
 from jax.sharding import PartitionSpec as P
 
 NMAX = 2559
-VMEM_BYTES = 56 * 1024 * 1024
-GROUP = 16
+VMEM_BYTES = 62 * 1024 * 1024
+GROUP = 48
 LANES = 128
 
 
-def pack_body(north_ref, south_ref, counts_ref, twice_ref, out_ref):
-    _, group, lat_dev, slots = north_ref.shape
-    live = twice_ref[...] < counts_ref[...]
+def flat_rows(value):
+    group, lat_dev, slots = value.shape
+    if lat_dev % 16:
+        value = value.astype(jnp.float32)
+    return value.reshape(group * lat_dev, slots).astype(jnp.bfloat16)
+
+
+def pack_body(north_ref, south_ref, out_ref):
     summed = north_ref[0].astype(jnp.float32) + south_ref[0].astype(jnp.float32)
-    summed = jnp.where(live[None], summed, 0.0).reshape(group * lat_dev, slots)
-    out_ref[...] = summed.astype(jnp.bfloat16).T
-
-
-def pack(part, north, south, counts, twice):
+    out_ref[...] = flat_rows(summed.astype(jnp.bfloat16)).T
+
+
+def pack(part, north, south):
     _, levels, lat_dev, slots = north.shape
     rows = pl.BlockSpec((1, GROUP, lat_dev, slots), lambda i: (part, i, 0, 0))
     return pl.pallas_call(
         pack_body,
         grid=(pl.cdiv(levels, GROUP),),
-        in_specs=[
-            rows,
-            rows,
-            pl.BlockSpec((lat_dev, 1), lambda i: (0, 0)),
-            pl.BlockSpec((1, slots), lambda i: (0, 0)),
-        ],
+        in_specs=[rows, rows],
         out_specs=pl.BlockSpec((slots, GROUP * lat_dev), lambda i: (0, i)),
         out_shape=jax.ShapeDtypeStruct((slots, pl.cdiv(levels * lat_dev, LANES) * LANES), jnp.bfloat16),
         compiler_params=pltpu.CompilerParams(vmem_limit_bytes=VMEM_BYTES),
@@ -42,14 +41,16 @@
             bytes_accessed=6 * levels * lat_dev * slots,
             transcendentals=0,
         ),
-    )(north, south, counts, twice)
+    )(north, south)
 
 
 def unpack_body(in_ref, *refs):
     out_ref = refs[-1]
     _, group, lat_dev, slots = out_ref.shape
-    rows = in_ref[...].T.astype(jnp.float32).reshape(group, lat_dev, slots)
-    out_ref[0] = rows.astype(jnp.bfloat16)
+    rows = in_ref[...].T
+    if lat_dev % 16:
+        rows = rows.astype(jnp.float32)
+    out_ref[0] = rows.reshape(group, lat_dev, slots).astype(jnp.bfloat16)
 
 
 def unpack(part, parts, levels, lat_dev, received, earlier):
@@ -195,8 +196,9 @@
 
     own = pl.ds(slot, levels, stride=slot_dev)
     matrix = legendre_ref[0]
+    live = 2 * wave < counts_ref[...]
     direct = lax.dot_general(
-        join_tiles(rows_ref, own).astype(jnp.bfloat16),
+        jnp.where(live, join_tiles(rows_ref, own), 0.0).astype(jnp.bfloat16),
         matrix,
         (((1,), (1,)), ((), ())),
         preferred_element_type=jnp.float32,
@@ -210,7 +212,7 @@
     state = jnp.where(degree <= NMAX, state, 0.0)
     split_tiles(spec_ref, own, state)
     rows = jnp.dot(state.astype(jnp.bfloat16), matrix, preferred_element_type=jnp.float32)
-    split_tiles(rows_ref, own, jnp.where(2 * wave < counts_ref[...], rows, 0.0))
+    split_tiles(rows_ref, own, jnp.where(live, rows, 0.0))
 
     @pl.when(slot == slot_dev - 1)
     def _():
@@ -281,14 +283,12 @@
     parts = channels // levels
     my_index = lax.axis_index("wave")
     own_waves = lax.dynamic_slice_in_dim(slot_wave, my_index * slot_dev, slot_dev)
-    local_counts = lax.dynamic_slice_in_dim(lon_counts, my_index * lat_dev, lat_dev)[:, None]
-    twice = 2 * slot_wave[None, :]
     north = jnp.transpose(north_rows, (2, 0, 1)).reshape(parts, levels, lat_dev, slots)
     south = jnp.transpose(south_rows, (2, 0, 1)).reshape(parts, levels, lat_dev, slots)
     exchange = functools.partial(
         lax.all_to_all, axis_name="wave", split_axis=0, concat_axis=0, tiled=True
     )
-    columns = [exchange(pack(part, north, south, local_counts, twice)) for part in range(parts)]
+    columns = [exchange(pack(part, north, south)) for part in range(parts)]
     spec_state = None
     returned = []
     for part in range(parts):

time: 297 us -> 284 us (0.956)
  Pallas kernels: 94.5 us -> 84.8 us
  local copies, waits for them, and re-layouts: 9.56 us -> 3.48 us
  waiting for transfers between devices: 168 us -> 173 us
    pallas_call x2, Pallas kernels: 15.7 us -> 10.5 us  [pack(): pl.pallas_call(pack_body, grid=(pl.cdiv(levels, GROUP),), in_specs=[rows,...]
    pallas_call x2, Pallas kernels: 13.8 us -> 9.06 us  [unpack(): pl.pallas_call(unpack_body, grid=(pl.cdiv(levels, GROUP),), in_specs=in_s...]
    unnamed x18 -> x12, local copies, waits for them, and re-layouts: 6.18 us -> 1.49 us
  transfers between devices with their start and end apart: 4 -> 4, of which waited for: 4 -> 4; matrix products, arithmetic and copies ran while one was open for 1% -> 1% of each run, Pallas kernels for 27% -> 26%
where the time goes in v3:
time: 284 us
  waiting for transfers between devices  173 us (61%)
  Pallas kernels  84.8 us (30%)
  starting transfers between devices  21.4 us (8%)
  local copies, waits for them, and re-layouts  3.48 us (1%)
    all_to_all x2, waiting for transfers between devices, per_device(): returned.append(exchange(rows))  88.7 us
    all_to_all x2, waiting for transfers between devices, per_device(): columns = [exchange(pack(part, north, south)) for part in range(parts)]  84.6 us
    pallas_call x2, Pallas kernels, spectral_step(): pl.pallas_call(step_body, grid_spec=pltpu.PrefetchScalarGridSpec(num_scal...  65.3 us
    all_to_all x2, starting transfers between devices, per_device(): columns = [exchange(pack(part, north, south)) for part in range(parts)]  11.6 us
    pallas_call x2, Pallas kernels, pack(): pl.pallas_call(pack_body, grid=(pl.cdiv(levels, GROUP),), in_specs=[rows,...  10.5 us
    all_to_all x2, starting transfers between devices, per_device(): returned.append(exchange(rows))  9.82 us
    pallas_call x2, Pallas kernels, unpack(): pl.pallas_call(unpack_body, grid=(pl.cdiv(levels, GROUP),), in_specs=in_s...  9.06 us
  transfers between devices with their start and end apart: 4, of which 4 were waited for; matrix products, arithmetic and copies ran while one was open for 1% of the time, Pallas kernels for 26%

profile of v3, /device:TPU:13, one launch (start us, length us, event | category | flops | bytes accessed | tf_op | source)
XLA Modules:
  0.0 283.7 jit_solution(13695299433826590294)
XLA Ops:
  0.6 5.2 %shard_map.96 = bf16[128,11008]{1,0:T(8,128)(2,1)} custom-call(bf16[2,137,80,128]{3,2,1,0:T(8,128)(2,1)} %bitcast.24, bf16[2,137,80,128]{3,2,1,0:T(8,128)(2,1)} %bitcast.26), custom_call_target="tpu_custom_call" | custom-call | flops 2805760 | bytes 8417280 | tf_op jit(solution)/shard_map/pallas_call | solution.py:32
  5.9 6.6 %all-to-all-start.1 = ((bf16[16,8,11008]{2,1,0:T(8,128)(2,1)}), bf16[16,8,11008]{2,1,0:T(8,128)(2,1)}, u32[]{:S(2)}, u32[]{:S(2)}) async-start(bf16[16,8,11008]{2,1,0:T(8,128)(2,1)} %bitcast.29), calls=%async_computation.1 | async-start | bytes 5636096 | tf_op jit(solution)/shard_map/all_to_all | solution.py:291
  12.4 5.2 %shard_map.95 = bf16[128,11008]{1,0:T(8,128)(2,1)} custom-call(bf16[2,137,80,128]{3,2,1,0:T(8,128)(2,1)} %bitcast.25, bf16[2,137,80,128]{3,2,1,0:T(8,128)(2,1)} %bitcast.27), custom_call_target="tpu_custom_call" | custom-call | flops 2805760 | bytes 8417280 | tf_op jit(solution)/shard_map/pallas_call | solution.py:32
  17.7 57.7 %all-to-all-done.1 = bf16[16,8,11008]{2,1,0:T(8,128)(2,1)} async-done(((bf16[16,8,11008]{2,1,0:T(8,128)(2,1)}), bf16[16,8,11008]{2,1,0:T(8,128)(2,1)}, u32[]{:S(2)}, u32[]{:S(2)}) %all-to-all-start.1) | async-done | bytes 2818080 | tf_op jit(solution)/shard_map/all_to_all | solution.py:291
  75.4 0.0 copy-start.2
  75.4 0.0 copy-start.3
  75.4 0.0 copy-start
  75.4 0.0 copy-start.1
  75.4 0.0 copy-start.4
  75.4 5.1 %all-to-all-start = ((bf16[16,8,11008]{2,1,0:T(8,128)(2,1)}), bf16[16,8,11008]{2,1,0:T(8,128)(2,1)}, u32[]{:S(2)}, u32[]{:S(2)}) async-start(bf16[16,8,11008]{2,1,0:T(8,128)(2,1)} %bitcast.28), calls=%async_computation | async-start | bytes 5636096 | tf_op jit(solution)/shard_map/all_to_all | solution.py:291
  80.5 0.0 copy-done.2
  80.5 0.6 broadcast_in_dim.8.counts_ref
  81.1 0.0 copy-done.3
  81.1 0.7 copy.17.rates_ref
  81.8 0.0 copy-done
  81.8 0.7 copy.14
  82.6 0.0 copy-done.1
  82.6 0.7 copy.15
  83.3 0.0 copy-done.4
  83.3 0.7 dynamic_slice.3.waves_ref
  84.0 32.6 %shard_map.97 = (bf16[2,137,8,1280]{3,2,1,0:T(8,128)(2,1)}, bf16[128,11008]{1,0:T(8,128)(2,1)}) custom-call(s32[8]{0:T(128)} %dynamic_slice.3.waves_ref, bf16[128,11008]{1,0:T(8,128)(2,1)} %bitcast.12.recv_ref, bf16[8,1280,1280]{2,1,0:T(8,128)(2,1)} %legendre_ref.3, s32[1,1280]{1,0:T(1,128)} %broadcast_in_dim.8.counts_ref, f32[137,1]{1,0:T(8,128)} %copy.17.rates_ref, ...), custom_call_target="tpu_custom_call" | custom-call | flops 7182745600 | bytes 34631680 | tf_op jit(solution)/shard_map/pallas_call | solution.py:248
  116.6 26.9 %all-to-all-done = bf16[16,8,11008]{2,1,0:T(8,128)(2,1)} async-done(((bf16[16,8,11008]{2,1,0:T(8,128)(2,1)}), bf16[16,8,11008]{2,1,0:T(8,128)(2,1)}, u32[]{:S(2)}, u32[]{:S(2)}) %all-to-all-start) | async-done | bytes 2818080 | tf_op jit(solution)/shard_map/all_to_all | solution.py:291
  143.4 4.9 %all-to-all-start.3 = ((bf16[16,8,11008]{2,1,0:T(8,128)(2,1)}), bf16[16,8,11008]{2,1,0:T(8,128)(2,1)}, u32[]{:S(2)}, u32[]{:S(2)}) async-start(bf16[16,8,11008]{2,1,0:T(8,128)(2,1)} %bitcast.31), calls=%async_computation.3 | async-start | bytes 5636096 | tf_op jit(solution)/shard_map/all_to_all | solution.py:299
  148.4 32.7 %shard_map.98 = (bf16[2,137,8,1280]{3,2,1,0:T(8,128)(2,1)}, bf16[128,11008]{1,0:T(8,128)(2,1)}) custom-call(s32[8]{0:T(128)} %dynamic_slice.3.waves_ref, bf16[128,11008]{1,0:T(8,128)(2,1)} %bitcast.5.recv_ref, bf16[8,1280,1280]{2,1,0:T(8,128)(2,1)} %legendre_ref.3, s32[1,1280]{1,0:T(1,128)} %broadcast_in_dim.8.counts_ref, ...), custom_call_target="tpu_custom_call", output_to_operand_aliasing={{0}: (7, {})} | custom-call | flops 7182745600 | bytes 34631680 | tf_op jit(solution)/shard_map/pallas_call | solution.py:248
  181.0 30.3 %all-to-all-done.3 = bf16[16,8,11008]{2,1,0:T(8,128)(2,1)} async-done(((bf16[16,8,11008]{2,1,0:T(8,128)(2,1)}), bf16[16,8,11008]{2,1,0:T(8,128)(2,1)}, u32[]{:S(2)}, u32[]{:S(2)}) %all-to-all-start.3) | async-done | bytes 2818080 | tf_op jit(solution)/shard_map/all_to_all | solution.py:299
  211.3 4.9 %all-to-all-start.2 = ((bf16[16,8,11008]{2,1,0:T(8,128)(2,1)}), bf16[16,8,11008]{2,1,0:T(8,128)(2,1)}, u32[]{:S(2)}, u32[]{:S(2)}) async-start(bf16[16,8,11008]{2,1,0:T(8,128)(2,1)} %bitcast.32), calls=%async_computation.2 | async-start | bytes 5636096 | tf_op jit(solution)/shard_map/all_to_all | solution.py:299
  216.2 4.5 %shard_map.99.refs_0_ = bf16[2,137,80,128]{3,2,1,0:T(8,128)(2,1)} custom-call(bf16[128,11008]{1,0:T(8,128)(2,1)} %bitcast.18.in_ref), custom_call_target="tpu_custom_call" | custom-call | flops 1402880 | bytes 5611520 | tf_op jit(solution)/shard_map/pallas_call | solution.py:65
  220.8 58.4 %all-to-all-done.2 = bf16[16,8,11008]{2,1,0:T(8,128)(2,1)} async-done(((bf16[16,8,11008]{2,1,0:T(8,128)(2,1)}), bf16[16,8,11008]{2,1,0:T(8,128)(2,1)}, u32[]{:S(2)}, u32[]{:S(2)}) %all-to-all-start.2) | async-done | bytes 2818080 | tf_op jit(solution)/shard_map/all_to_all | solution.py:299
  279.2 4.5 %shard_map.100 = bf16[2,137,80,128]{3,2,1,0:T(8,128)(2,1)} custom-call(bf16[128,11008]{1,0:T(8,128)(2,1)} %bitcast.16.in_ref, bf16[2,137,80,128]{3,2,1,0:T(8,128)(2,1)} %shard_map.99.refs_0_), custom_call_target="tpu_custom_call", output_to_operand_aliasing={{}: (1, {})} | custom-call | flops 1402880 | bytes 5611520 | tf_op jit(solution)/shard_map/pallas_call | solution.py:65
Async XLA Ops:
  5.9 69.5 %all-to-all-start.1 = ((bf16[16,8,11008]{2,1,0:T(8,128)(2,1)}), bf16[16,8,11008]{2,1,0:T(8,128)(2,1)}, u32[]{:S(2)}, u32[]{:S(2)}) async-start(bf16[16,8,11008]{2,1,0:T(8,128)(2,1)} %bitcast.29), calls=%async_computation.1 | async-start | bytes 5636096 | tf_op jit(solution)/shard_map/all_to_all | solution.py:291
  75.4 5.1 %copy-start.2 = (s32[1280]{0:T(1024)S(1)}, s32[1280]{0:T(1024)}, u32[]{:S(2)}) copy-start(s32[1280]{0:T(1024)} %param.10) | copy-start | bytes 15364
  75.4 5.7 %copy-start.3 = (f32[137]{0:T(256)S(1)}, f32[137]{0:T(256)}, u32[]{:S(2)}) copy-start(f32[137]{0:T(256)} %param.13) | copy-start | bytes 1648
  75.4 6.4 %copy-start = (bf16[137,137]{1,0:T(8,128)(2,1)S(1)}, bf16[137,137]{1,0:T(8,128)(2,1)}, u32[]{:S(2)}) copy-start(bf16[137,137]{1,0:T(8,128)(2,1)} %param.14) | copy-start | bytes 112618
  75.4 7.2 %copy-start.1 = (bf16[137,137]{1,0:T(8,128)(2,1)S(1)}, bf16[137,137]{1,0:T(8,128)(2,1)}, u32[]{:S(2)}) copy-start(bf16[137,137]{1,0:T(8,128)(2,1)} %param.15) | copy-start | bytes 112618
  75.4 7.9 %copy-start.4 = (s32[128]{0:T(128)S(1)}, s32[128]{0:T(128)}, u32[]{:S(2)}) copy-start(s32[128]{0:T(128)} %param.11) | copy-start | bytes 1540
  75.4 68.0 %all-to-all-start = ((bf16[16,8,11008]{2,1,0:T(8,128)(2,1)}), bf16[16,8,11008]{2,1,0:T(8,128)(2,1)}, u32[]{:S(2)}, u32[]{:S(2)}) async-start(bf16[16,8,11008]{2,1,0:T(8,128)(2,1)} %bitcast.28), calls=%async_computation | async-start | bytes 5636096 | tf_op jit(solution)/shard_map/all_to_all | solution.py:291
  143.4 67.9 %all-to-all-start.3 = ((bf16[16,8,11008]{2,1,0:T(8,128)(2,1)}), bf16[16,8,11008]{2,1,0:T(8,128)(2,1)}, u32[]{:S(2)}, u32[]{:S(2)}) async-start(bf16[16,8,11008]{2,1,0:T(8,128)(2,1)} %bitcast.31), calls=%async_computation.3 | async-start | bytes 5636096 | tf_op jit(solution)/shard_map/all_to_all | solution.py:299
  211.3 67.9 %all-to-all-start.2 = ((bf16[16,8,11008]{2,1,0:T(8,128)(2,1)}), bf16[16,8,11008]{2,1,0:T(8,128)(2,1)}, u32[]{:S(2)}, u32[]{:S(2)}) async-start(bf16[16,8,11008]{2,1,0:T(8,128)(2,1)} %bitcast.32), calls=%async_computation.2 | async-start | bytes 5636096 | tf_op jit(solution)/shard_map/all_to_all | solution.py:299

commit v4 on v3

--- a/solution.py
+++ b/solution.py
@@ -9,9 +9,10 @@
 from jax.sharding import PartitionSpec as P
 
 NMAX = 2559
-VMEM_BYTES = 62 * 1024 * 1024
+VMEM_BYTES = 255 * 256 * 1024
 GROUP = 48
 LANES = 128
+EARLY = 5
 
 
 def flat_rows(value):
@@ -21,20 +22,65 @@
     return value.reshape(group * lat_dev, slots).astype(jnp.bfloat16)
 
 
-def pack_body(north_ref, south_ref, out_ref):
+def partner(my_index, half, turn):
+    other = jnp.where(my_index < half, half, 0)
+    return other + lax.rem(lax.rem(my_index, half) + turn + half, half)
+
+
+def own_half(my_index, half):
+    return jnp.where(my_index < half, 0, half)
+
+
+def take_blocks(near_ref, far_refs, blocks_ref):
+    half = len(far_refs)
+    my_index = lax.axis_index("wave")
+    base = own_half(my_index, half)
+    for i in range(half):
+        blocks_ref[base + i] = near_ref[i]
+        blocks_ref[partner(my_index, half, -i)] = far_refs[i][...]
+
+
+def give_blocks(blocks_ref, near_ref, far_refs):
+    half = len(far_refs)
+    my_index = lax.axis_index("wave")
+    base = own_half(my_index, half)
+    for i in range(half):
+        near_ref[i] = blocks_ref[base + i]
+        far_refs[i][...] = blocks_ref[partner(my_index, half, i)]
+
+
+def pack_body(north_ref, south_ref, near_ref, *refs):
+    far_refs, blocks_ref = refs[:-1], refs[-1]
+    slot_dev = blocks_ref.shape[1]
     summed = north_ref[0].astype(jnp.float32) + south_ref[0].astype(jnp.float32)
-    out_ref[...] = flat_rows(summed.astype(jnp.bfloat16)).T
-
-
-def pack(part, north, south):
+    columns = flat_rows(summed.astype(jnp.bfloat16)).T
+    for device in range(blocks_ref.shape[0]):
+        blocks_ref[device] = columns[device * slot_dev : (device + 1) * slot_dev]
+    give_blocks(blocks_ref, near_ref, far_refs)
+
+
+def block_shapes(half, slot_dev, width):
+    near = jax.ShapeDtypeStruct((half, slot_dev, width), jnp.bfloat16)
+    return [near] + [jax.ShapeDtypeStruct((slot_dev, width), jnp.bfloat16)] * half
+
+
+def block_specs(half, slot_dev, lanes):
+    near = pl.BlockSpec((half, slot_dev, lanes), lambda i: (0, 0, i))
+    return [near] + [pl.BlockSpec((slot_dev, lanes), lambda i: (0, i))] * half
+
+
+def pack(part, half, north, south):
     _, levels, lat_dev, slots = north.shape
+    slot_dev = slots // (2 * half)
+    width = pl.cdiv(levels * lat_dev, LANES) * LANES
     rows = pl.BlockSpec((1, GROUP, lat_dev, slots), lambda i: (part, i, 0, 0))
     return pl.pallas_call(
         pack_body,
         grid=(pl.cdiv(levels, GROUP),),
         in_specs=[rows, rows],
-        out_specs=pl.BlockSpec((slots, GROUP * lat_dev), lambda i: (0, i)),
-        out_shape=jax.ShapeDtypeStruct((slots, pl.cdiv(levels * lat_dev, LANES) * LANES), jnp.bfloat16),
+        out_specs=block_specs(half, slot_dev, GROUP * lat_dev),
+        out_shape=block_shapes(half, slot_dev, width),
+        scratch_shapes=[pltpu.VMEM((2 * half, slot_dev, GROUP * lat_dev), jnp.bfloat16)],
         compiler_params=pltpu.CompilerParams(vmem_limit_bytes=VMEM_BYTES),
         cost_estimate=pl.CostEstimate(
             flops=2 * levels * lat_dev * slots,
@@ -44,30 +90,41 @@
     )(north, south)
 
 
-def unpack_body(in_ref, *refs):
-    out_ref = refs[-1]
+def unpack_body(near_ref, *refs, half, passed):
+    far_refs, out_ref, blocks_ref = refs[:half], refs[-2 - passed], refs[-1]
     _, group, lat_dev, slots = out_ref.shape
-    rows = in_ref[...].T
+    take_blocks(near_ref, far_refs, blocks_ref)
+    blocks = [blocks_ref[device].astype(jnp.float32) for device in range(2 * half)]
+    rows = jnp.concatenate(blocks, axis=0).astype(jnp.bfloat16).T
     if lat_dev % 16:
         rows = rows.astype(jnp.float32)
     out_ref[0] = rows.reshape(group, lat_dev, slots).astype(jnp.bfloat16)
 
 
-def unpack(part, parts, levels, lat_dev, received, earlier):
-    slots = received.shape[0]
-    in_specs = [pl.BlockSpec((slots, GROUP * lat_dev), lambda i: (0, i))]
-    operands = [received]
+def unpack(part, parts, levels, lat_dev, received, earlier, waiting):
+    half, slot_dev, _ = received[0].shape
+    slots = 2 * half * slot_dev
+    in_specs = block_specs(half, slot_dev, GROUP * lat_dev)
+    operands = list(received)
     aliases = {}
     if earlier is not None:
         in_specs.append(pl.BlockSpec(memory_space=pl.ANY))
+        aliases = {len(operands): 0}
         operands.append(earlier)
-        aliases = {1: 0}
-    return pl.pallas_call(
-        unpack_body,
+    anywhere = pl.BlockSpec(memory_space=pl.ANY)
+    for i, block in enumerate(waiting):
+        aliases[len(operands)] = 1 + i
+        operands.append(block)
+        in_specs.append(anywhere)
+    outs = pl.pallas_call(
+        functools.partial(unpack_body, half=half, passed=len(waiting)),
         grid=(pl.cdiv(levels, GROUP),),
         in_specs=in_specs,
-        out_specs=pl.BlockSpec((1, GROUP, lat_dev, slots), lambda i: (part, i, 0, 0)),
-        out_shape=jax.ShapeDtypeStruct((parts, levels, lat_dev, slots), jnp.bfloat16),
+        out_specs=[pl.BlockSpec((1, GROUP, lat_dev, slots), lambda i: (part, i, 0, 0))]
+        + [anywhere] * len(waiting),
+        out_shape=[jax.ShapeDtypeStruct((parts, levels, lat_dev, slots), jnp.bfloat16)]
+        + [jax.ShapeDtypeStruct(block.shape, block.dtype) for block in waiting],
+        scratch_shapes=[pltpu.VMEM((2 * half, slot_dev, GROUP * lat_dev), jnp.bfloat16)],
         input_output_aliases=aliases,
         compiler_params=pltpu.CompilerParams(vmem_limit_bytes=VMEM_BYTES),
         cost_estimate=pl.CostEstimate(
@@ -76,6 +133,7 @@
             transcendentals=0,
         ),
     )(*operands)
+    return outs[0], outs[1:]
 
 
 def lane_runs(lanes, source):
@@ -112,16 +170,9 @@
     lat_total = rows_ref.shape[0] * LANES
     base = pl.multiple_of(first * lat_dev, LANES)
     lane_index = lax.broadcasted_iota(jnp.int32, (slot_dev, LANES), 1)
-    pairs = {}
 
     def load(device, tile):
-        pair = device // 2
-        if (pair, tile) not in pairs:
-            pairs[pair, tile] = recv_ref[
-                2 * pair * slot_dev : 2 * (pair + 1) * slot_dev, pl.ds(base + tile * LANES, LANES)
-            ].astype(jnp.float32)
-        at = (device % 2) * slot_dev
-        return pairs[pair, tile][at : at + slot_dev]
+        return recv_ref[device, :, pl.ds(base + tile * LANES, LANES)].astype(jnp.float32)
 
     cache = {}
     for lanes in range(0, lat_total, LANES):
@@ -143,20 +194,16 @@
         row = pl.multiple_of((first + i) * slot_dev, slot_dev)
         return rows_ref[tile, pl.ds(row, slot_dev), :]
 
-    for pair in range(devices // 2):
+    for device in range(devices):
         for lanes in range(0, group * lat_dev, LANES):
-            tiles = []
-            for device in (2 * pair, 2 * pair + 1):
-                runs = lane_runs(
-                    lanes,
-                    lambda l: (l // lat_dev, device * lat_dev + l % lat_dev)
-                    if l < group * lat_dev
-                    else None,
-                )
-                tiles.append(merge_runs(runs, load, cache, lane_index))
-            send_ref[
-                2 * pair * slot_dev : 2 * (pair + 1) * slot_dev, pl.ds(base + lanes, LANES)
-            ] = jnp.concatenate(tiles, axis=0).astype(jnp.bfloat16)
+            runs = lane_runs(
+                lanes,
+                lambda l: (l // lat_dev, device * lat_dev + l % lat_dev)
+                if l < group * lat_dev
+                else None,
+            )
+            tile = merge_runs(runs, load, cache, lane_index).astype(jnp.bfloat16)
+            send_ref[device, :, pl.ds(base + lanes, LANES)] = tile
 
 
 def join_tiles(ref, rows):
@@ -180,18 +227,23 @@
         body(full * group, levels % group)
 
 
-def step_body(waves_ref, recv_ref, legendre_ref, counts_ref, rates_ref, to_ref, from_ref, *refs):
-    state_ref, send_ref, rows_ref, spec_ref = refs[-4:]
+def step_body(waves_ref, recv_ref, *refs, half, passed):
+    recv_refs, refs = refs[:half], refs[half:]
+    legendre_ref, counts_ref, rates_ref, to_ref, from_ref = refs[:5]
+    outs = refs[len(refs) - 5 - half - passed :]
+    state_ref, send_ref, send_refs = outs[0], outs[1], outs[2 : 2 + half]
+    rows_ref, spec_ref, blocks_ref = refs[-3:]
     slot = pl.program_id(0)
     wave = waves_ref[slot]
     row_total, lat_total = legendre_ref.shape[1:]
     _, levels, slot_dev, _ = state_ref.shape
-    lat_dev = lat_total // (recv_ref.shape[0] // slot_dev)
+    lat_dev = lat_total // (2 * half)
 
     @pl.when(slot == 0)
     def _():
+        take_blocks(recv_ref, recv_refs, blocks_ref)
         all_groups(
-            levels, lat_dev, lambda c, n: spread(recv_ref, rows_ref, c, n, lat_dev, slot_dev)
+            levels, lat_dev, lambda c, n: spread(blocks_ref, rows_ref, c, n, lat_dev, slot_dev)
         )
 
     own = pl.ds(slot, levels, stride=slot_dev)
@@ -217,8 +269,9 @@
     @pl.when(slot == slot_dev - 1)
     def _():
         all_groups(
-            levels, lat_dev, lambda c, n: gather(rows_ref, send_ref, c, n, lat_dev, slot_dev)
+            levels, lat_dev, lambda c, n: gather(rows_ref, blocks_ref, c, n, lat_dev, slot_dev)
         )
+        give_blocks(blocks_ref, send_ref, send_refs)
 
         @pl.loop(0, levels)
         def _(c):
@@ -226,52 +279,75 @@
             state_ref[0, c] = join_tiles(spec_ref, pl.ds(at, slot_dev)).astype(jnp.bfloat16)
 
 
-def spectral_step(part, parts, received, legendre, own_waves, counts, rates, to_t, from_t, earlier):
-    slots, width = received.shape
+def spectral_step(part, parts, received, legendre, own_waves, counts, rates, to_t, from_t, earlier, waiting):
+    half, _, width = received[0].shape
     slot_dev, row_total, lat_total = legendre.shape
     levels = to_t.shape[0]
     whole = lambda shape: pl.BlockSpec(shape, lambda s, waves: (0,) * len(shape))
-    in_specs = [
-        whole((slots, width)),
+    shapes = block_shapes(half, slot_dev, width)
+    in_specs = [whole(shape.shape) for shape in shapes] + [
         pl.BlockSpec((1, row_total, lat_total), lambda s, waves: (s, 0, 0)),
         whole((1, lat_total)),
         whole((levels, 1)),
         whole((levels, levels)),
         whole((levels, levels)),
     ]
-    operands = [own_waves, received, legendre, counts, rates, to_t, from_t]
+    operands = [own_waves, *received, legendre, counts, rates, to_t, from_t]
+    anywhere = pl.BlockSpec(memory_space=pl.ANY)
     aliases = {}
     if earlier is not None:
-        in_specs.append(pl.BlockSpec(memory_space=pl.ANY))
-        aliases = {len(operands): 0}
+        aliases[len(operands)] = 0
         operands.append(earlier)
-    return pl.pallas_call(
-        step_body,
+        in_specs.append(anywhere)
+    for i, block in enumerate(waiting):
+        aliases[len(operands)] = 1 + len(shapes) + i
+        operands.append(block)
+        in_specs.append(anywhere)
+    outs = pl.pallas_call(
+        functools.partial(step_body, half=half, passed=len(waiting)),
         grid_spec=pltpu.PrefetchScalarGridSpec(
             num_scalar_prefetch=1,
             grid=(slot_dev,),
             in_specs=in_specs,
             out_specs=[
                 pl.BlockSpec((1, levels, slot_dev, row_total), lambda s, waves: (part, 0, 0, 0)),
-                whole((slots, width)),
-            ],
+            ]
+            + [whole(shape.shape) for shape in shapes]
+            + [anywhere] * len(waiting),
             scratch_shapes=[
                 pltpu.VMEM((lat_total // LANES, levels * slot_dev, LANES), jnp.float32),
                 pltpu.VMEM((row_total // LANES, levels * slot_dev, LANES), jnp.float32),
+                pltpu.VMEM((2 * half, slot_dev, width), jnp.bfloat16),
             ],
         ),
         out_shape=[
             jax.ShapeDtypeStruct((parts, levels, slot_dev, row_total), jnp.bfloat16),
-            jax.ShapeDtypeStruct((slots, width), jnp.bfloat16),
+            *shapes,
+            *[jax.ShapeDtypeStruct(block.shape, block.dtype) for block in waiting],
         ],
         input_output_aliases=aliases,
         compiler_params=pltpu.CompilerParams(vmem_limit_bytes=VMEM_BYTES),
         cost_estimate=pl.CostEstimate(
-            flops=4 * slot_dev * row_total * lat_total * levels,
+            flops=16 * slot_dev * row_total * lat_total * levels,
             bytes_accessed=2 * slot_dev * lat_total * (row_total + 3 * levels),
             transcendentals=0,
         ),
     )(*operands)
+    return outs[0], outs[1 : 1 + len(shapes)], outs[1 + len(shapes) :]
+
+
+def exchange_near(block, half):
+    groups = [list(range(half)), list(range(half, 2 * half))]
+    return lax.all_to_all(
+        block, "wave", split_axis=0, concat_axis=0, tiled=True, axis_index_groups=groups
+    )
+
+
+def exchange_far(block, half, turn):
+    pairs = [
+        (i, (half if i < half else 0) + (i % half + turn) % half) for i in range(2 * half)
+    ]
+    return lax.ppermute(block, "wave", pairs)
 
 
 def per_device(
@@ -285,21 +361,27 @@
     own_waves = lax.dynamic_slice_in_dim(slot_wave, my_index * slot_dev, slot_dev)
     north = jnp.transpose(north_rows, (2, 0, 1)).reshape(parts, levels, lat_dev, slots)
     south = jnp.transpose(south_rows, (2, 0, 1)).reshape(parts, levels, lat_dev, slots)
-    exchange = functools.partial(
-        lax.all_to_all, axis_name="wave", split_axis=0, concat_axis=0, tiled=True
-    )
-    columns = [exchange(pack(part, north, south)) for part in range(parts)]
+    half = slots // slot_dev // 2
+    early = 1 + min(EARLY, half)
+    send = lambda blocks: [exchange_near(blocks[0], half)] + [
+        exchange_far(block, half, turn) for turn, block in enumerate(blocks[1:])
+    ]
+    sent = [list(pack(part, half, north, south)) for part in range(parts)]
+    returned = []
     spec_state = None
-    returned = []
     for part in range(parts):
-        spec_state, rows = spectral_step(
-            part, parts, columns[part], legendre, own_waves, lon_counts[None, :],
-            mode_rates[:, None], to_modes.T, from_modes.T, spec_state,
+        beside = sent[part + 1] if part + 1 < parts else (returned or [[]])[-1]
+        spec_state, blocks, beside[early:] = spectral_step(
+            part, parts, send(sent[part]), legendre, own_waves, lon_counts[None, :],
+            mode_rates[:, None], to_modes.T, from_modes.T, spec_state, beside[early:],
         )
-        returned.append(exchange(rows))
+        returned.append(list(blocks))
     new_rows = None
     for part in range(parts):
-        new_rows = unpack(part, parts, levels, lat_dev, returned[part], new_rows)
+        last = returned[part + 1] if part + 1 < parts else []
+        new_rows, last[:1] = unpack(
+            part, parts, levels, lat_dev, send(returned[part]), new_rows, last[:1]
+        )
     new_rows = jnp.transpose(new_rows.reshape(channels, lat_dev, slots), (1, 2, 0))
     spec_state = jnp.transpose(spec_state.reshape(channels, slot_dev, row_total), (1, 2, 0))
     return (spec_state, new_rows)

time: 284 us -> 298 us (1.049); the launches traced: 284 us -> 293 us
  starting transfers between devices: 21.4 us -> 80.4 us
  waiting for transfers between devices: 173 us -> 121 us
    all_to_all x4, waiting for transfers between devices: 173 us -> 0.01 us  [exchange_near(): lax.all_to_all(block, 'wave', split_axis=0, concat_axis=0, tiled=True, ax...]
    ppermute x0 -> x32, waiting for transfers between devices: none -> 121 us  [exchange_far(): return lax.ppermute(block, 'wave', pairs)]
    ppermute x0 -> x32, starting transfers between devices: none -> 56.9 us  [exchange_far(): return lax.ppermute(block, 'wave', pairs)]
  transfers between devices with their start and end apart: 4 -> 36, of which waited for: 4 -> 21; matrix products, arithmetic and copies ran while one was open for 1% -> 1% of each run, Pallas kernels for 26% -> 24%
where the time goes in v4:
time: 298 us; the launch traced here: 293 us
  waiting for transfers between devices  121 us (41%)
  Pallas kernels  86.3 us (29%)
  starting transfers between devices  80.4 us (27%)
  local copies, waits for them, and re-layouts  4.19 us (1%)
    ppermute x32, waiting for transfers between devices, exchange_far(): return lax.ppermute(block, 'wave', pairs)  121 us
    pallas_call x2, Pallas kernels, spectral_step(): pl.pallas_call(functools.partial(step_body, half=half, passed=len(waiting...  66.4 us
    ppermute x32, starting transfers between devices, exchange_far(): return lax.ppermute(block, 'wave', pairs)  56.9 us
    all_to_all x4, starting transfers between devices, exchange_near(): lax.all_to_all(block, 'wave', split_axis=0, concat_axis=0, tiled=True, ax...  23.5 us
    pallas_call x2, Pallas kernels, pack(): pl.pallas_call(pack_body, grid=(pl.cdiv(levels, GROUP),), in_specs=[rows,...  10.7 us
    pallas_call x2, Pallas kernels, unpack(): pl.pallas_call(functools.partial(unpack_body, half=half, passed=len(waiti...  9.21 us
  transfers between devices with their start and end apart: 36, of which 21 were waited for; matrix products, arithmetic and copies ran while one was open for 1% of the time, Pallas kernels for 24%

profile of v4, /device:TPU:13, one launch (start us, length us, event | category | flops | bytes accessed | tf_op | source)
XLA Modules:
  0.0 292.9 jit_solution(15499717416687838232)
XLA Ops:
  0.6 5.3 %shard_map.96 = (bf16[8,8,11008]{2,1,0:T(8,128)(2,1)}, bf16[8,11008]{1,0:T(8,128)(2,1)}, bf16[8,11008]{1,0:T(8,128)(2,1)}, bf16[8,11008]{1,0:T(8,128)(2,1)}, bf1...) custom-call(bf16[2,137,80,128]{3,2,1,0:T(8,128)(2,1)} %bitcast.15, ...), custom_call_target="tpu_custom_call" | custom-call | flops 2805760 | bytes 8417280 | tf_op jit(solution)/shard_map/pallas_call | solution.py:77
  6.0 0.0 copy-start.4
  6.0 0.0 copy-start.5
  6.0 0.0 copy-start.2
  6.0 0.0 copy-start.3
  6.1 0.0 copy-start.19
  6.1 4.7 %all-to-all-start.1 = ((bf16[8,8,11008]{2,1,0:T(8,128)(2,1)}), bf16[8,8,11008]{2,1,0:T(8,128)(2,1)}, u32[]{:S(2)}, u32[]{:S(2)}) async-start(bf16[8,8,11008]{2,1,0:T(8,128)(2,1)} %get-tuple-element.54), calls=%async_computation.1 | async-start | bytes 2818048 | tf_op jit(solution)/shard_map/all_to_all | solution.py:341
  10.7 2.7 collective-permute-start.5
  13.5 2.9 collective-permute-start.7
  16.3 0.4 collective-permute-start.9
  16.7 19.0 %collective-permute-done.5.refs_0_ = bf16[8,11008]{1,0:T(8,128)(2,1)} collective-permute-done((bf16[8,11008]{1,0:T(8,128)(2,1)S(1)}, bf16[8,11008]{1,0:T(8,128)(2,1)}, u32[]{:S(2)}, u32[]{:S(2)}) %collective-permute-start.5) | collective-permute-done | bytes 176160 | tf_op jit(solution)/shard_map/ppermute | solution.py:350
  35.7 4.7 %collective-permute-done.6.refs_1_ = bf16[8,11008]{1,0:T(8,128)(2,1)} collective-permute-done((bf16[8,11008]{1,0:T(8,128)(2,1)S(1)}, bf16[8,11008]{1,0:T(8,128)(2,1)}, u32[]{:S(2)}, u32[]{:S(2)}) %collective-permute-start.6) | collective-permute-done | bytes 176160 | tf_op jit(solution)/shard_map/ppermute | solution.py:350
  40.4 0.6 collective-permute-done.7.refs_2_
  41.0 2.6 collective-permute-start.12
  43.6 0.6 broadcast_in_dim.8.refs_9_
  44.2 0.7 copy.23.refs_10_
  45.0 0.7 copy.21
  45.7 0.7 copy.22
  46.5 0.6 dynamic_slice.3.waves_ref
  47.1 5.3 %shard_map.95 = (bf16[8,8,11008]{2,1,0:T(8,128)(2,1)}, bf16[8,11008]{1,0:T(8,128)(2,1)}, bf16[8,11008]{1,0:T(8,128)(2,1)}, bf16[8,11008]{1,0:T(8,128)(2,1)}, bf1...) custom-call(bf16[2,137,80,128]{3,2,1,0:T(8,128)(2,1)} %bitcast.16, ...), custom_call_target="tpu_custom_call" | custom-call | flops 2805760 | bytes 8417280 | tf_op jit(solution)/shard_map/pallas_call | solution.py:77
  52.4 7.2 %all-to-all-start = ((bf16[8,8,11008]{2,1,0:T(8,128)(2,1)}), bf16[8,8,11008]{2,1,0:T(8,128)(2,1)}, u32[]{:S(2)}, u32[]{:S(2)}) async-start(bf16[8,8,11008]{2,1,0:T(8,128)(2,1)} %get-tuple-element.48), calls=%async_computation | async-start | bytes 2818048 | tf_op jit(solution)/shard_map/all_to_all | solution.py:341
  59.6 1.1 collective-permute-done.8.refs_3_
  60.7 0.7 copy-done.12
  61.4 2.3 collective-permute-start
  63.7 1.3 collective-permute-done.9.refs_4_
  64.9 1.6 collective-permute-start.1
  66.5 3.2 %collective-permute-done.10.refs_5_ = bf16[8,11008]{1,0:T(8,128)(2,1)} collective-permute-done((bf16[8,11008]{1,0:T(8,128)(2,1)}, bf16[8,11008]{1,0:T(8,128)(2,1)}, u32[]{:S(2)}, u32[]{:S(2)}) %collective-permute-start.10) | collective-permute-done | bytes 176160 | tf_op jit(solution)/shard_map/ppermute | solution.py:350
  69.6 0.3 collective-permute-start.2
  70.0 5.0 %collective-permute-done.11.refs_6_ = bf16[8,11008]{1,0:T(8,128)(2,1)} collective-permute-done((bf16[8,11008]{1,0:T(8,128)(2,1)}, bf16[8,11008]{1,0:T(8,128)(2,1)}, u32[]{:S(2)}, u32[]{:S(2)}) %collective-permute-start.11) | collective-permute-done | bytes 176160 | tf_op jit(solution)/shard_map/ppermute | solution.py:350
  75.0 1.7 collective-permute-start.3
  76.8 0.6 collective-permute-done.12.refs_7_
  77.4 2.1 collective-permute-start.4
  79.5 33.2 %shard_map.97 = (bf16[2,137,8,1280]{3,2,1,0:T(8,128)(2,1)}, bf16[8,8,11008]{2,1,0:T(8,128)(2,1)}, bf16[8,11008]{1,0:T(8,128)(2,1)}, bf16[8,11008]{1,0:T(8,128)(2...) custom-call(s32[8]{0:T(128)} %dynamic_slice.3.waves_ref, ...), custom_call_target="tpu_custom_call", output_to_operand_aliasing={{10}: (15, {}), {11}: (16, {}), {12}: (17, {})} | custom-call | flops 28730982400 | bytes 34631680 | tf_op jit(solution)/shard_map/pallas_call | solution.py:306
  112.7 2.6 collective-permute-start.13
  115.3 18.7 %collective-permute-start.14 = (bf16[8,11008]{1,0:T(8,128)(2,1)}, bf16[8,11008]{1,0:T(8,128)(2,1)}, u32[]{:S(2)}, u32[]{:S(2)}) collective-permute-start(bf16[8,11008]{1,0:T(8,128)(2,1)} %get-tuple-element.67), channel_id=1, source_target_pairs={{0,14},{1,15},{2,8},{3,9},{4,10},{5,11},{6,12},{7,13},{8,6},{9,7},... | collective-permute-start | bytes 528392 | tf_op jit(solution)/shard_map/ppermute | solution.py:350
  134.0 5.6 %all-to-all-start.2 = ((bf16[8,8,11008]{2,1,0:T(8,128)(2,1)}), bf16[8,8,11008]{2,1,0:T(8,128)(2,1)}, u32[]{:S(2)}, u32[]{:S(2)}) async-start(bf16[8,8,11008]{2,1,0:T(8,128)(2,1)} %get-tuple-element.74), calls=%async_computation.2 | async-start | bytes 2818048 | tf_op jit(solution)/shard_map/all_to_all | solution.py:341
  139.6 2.6 collective-permute-start.16
  142.2 2.3 collective-permute-done.13.refs_5_
  144.5 0.4 collective-permute-start.18
  144.9 6.5 %collective-permute-done.14.refs_6_ = bf16[8,11008]{1,0:T(8,128)(2,1)} collective-permute-done((bf16[8,11008]{1,0:T(8,128)(2,1)}, bf16[8,11008]{1,0:T(8,128)(2,1)}, u32[]{:S(2)}, u32[]{:S(2)}) %collective-permute-start.14) | collective-permute-done | bytes 176160 | tf_op jit(solution)/shard_map/ppermute | solution.py:350
  151.4 1.3 collective-permute-done.15.refs_7_
  152.7 3.2 %collective-permute-start.20 = (bf16[8,11008]{1,0:T(8,128)(2,1)}, bf16[8,11008]{1,0:T(8,128)(2,1)}, u32[]{:S(2)}, u32[]{:S(2)}) collective-permute-start(bf16[8,11008]{1,0:T(8,128)(2,1)} %get-tuple-element.79), channel_id=1, source_target_pairs={{0,12},{1,13},{2,14},{3,15},{4,8},{5,9},{6,10},{7,11},{8,4},{9,5},... | collective-permute-start | bytes 528392 | tf_op jit(solution)/shard_map/ppermute | solution.py:350
  155.9 33.2 %shard_map.98 = (bf16[2,137,8,1280]{3,2,1,0:T(8,128)(2,1)}, bf16[8,8,11008]{2,1,0:T(8,128)(2,1)}, bf16[8,11008]{1,0:T(8,128)(2,1)}, bf16[8,11008]{1,0:T(8,128)(2...) custom-call(s32[8]{0:T(128)} %dynamic_slice.3.waves_ref, ...), custom_call_target="tpu_custom_call", output_to_operand_aliasing={{0}: (15, {}), {10}: (16, {}), {11}: (17, {}), {12}: (18, {})} | custom-call | flops 28730982400 | bytes 34631680 | tf_op jit(solution)/shard_map/pallas_call | solution.py:306
  189.1 3.6 %collective-permute-start.21 = (bf16[8,11008]{1,0:T(8,128)(2,1)}, bf16[8,11008]{1,0:T(8,128)(2,1)}, u32[]{:S(2)}, u32[]{:S(2)}) collective-permute-start(bf16[8,11008]{1,0:T(8,128)(2,1)} %get-tuple-element.80), channel_id=1, source_target_pairs={{0,13},{1,14},{2,15},{3,8},{4,9},{5,10},{6,11},{7,12},{8,5},{9,6},... | collective-permute-start | bytes 528392 | tf_op jit(solution)/shard_map/ppermute | solution.py:350
  192.8 0.5 collective-permute-start.23
  193.3 10.2 %collective-permute-done.21.refs_5_ = bf16[8,11008]{1,0:T(8,128)(2,1)} collective-permute-done((bf16[8,11008]{1,0:T(8,128)(2,1)}, bf16[8,11008]{1,0:T(8,128)(2,1)}, u32[]{:S(2)}, u32[]{:S(2)}) %collective-permute-start.21) | collective-permute-done | bytes 176160 | tf_op jit(solution)/shard_map/ppermute | solution.py:350
  203.6 6.7 %collective-permute-done.22.refs_6_ = bf16[8,11008]{1,0:T(8,128)(2,1)} collective-permute-done((bf16[8,11008]{1,0:T(8,128)(2,1)}, bf16[8,11008]{1,0:T(8,128)(2,1)}, u32[]{:S(2)}, u32[]{:S(2)}) %collective-permute-start.22) | collective-permute-done | bytes 176160 | tf_op jit(solution)/shard_map/ppermute | solution.py:350
  210.3 3.5 %collective-permute-done.23.refs_7_ = bf16[8,11008]{1,0:T(8,128)(2,1)} collective-permute-done((bf16[8,11008]{1,0:T(8,128)(2,1)}, bf16[8,11008]{1,0:T(8,128)(2,1)}, u32[]{:S(2)}, u32[]{:S(2)}) %collective-permute-start.23) | collective-permute-done | bytes 176160 | tf_op jit(solution)/shard_map/ppermute | solution.py:350
  213.8 4.6 %shard_map.99 = (bf16[2,137,80,128]{3,2,1,0:T(8,128)(2,1)}, bf16[8,8,11008]{2,1,0:T(8,128)(2,1)}) custom-call(bf16[8,8,11008]{2,1,0:T(8,128)(2,1)} %all-to-all-done.2.near_ref, bf16[8,11008]{1,0:T(8,128)(2,1)} %copy-done, bf16[8,11008]{1,0:T(8,128)(2,1)} %collective-permute-done.17.refs_1_, ...), custom_call_target="tpu_custom_call", output_to_operand_aliasing={{1}: (9, {})} | custom-call | flops 1402880 | bytes 5611520 | tf_op jit(solution)/shard_map/pallas_call | solution.py:119
  218.5 6.1 %all-to-all-start.3 = ((bf16[8,8,11008]{2,1,0:T(8,128)(2,1)}), bf16[8,8,11008]{2,1,0:T(8,128)(2,1)}, u32[]{:S(2)}, u32[]{:S(2)}) async-start(bf16[8,8,11008]{2,1,0:T(8,128)(2,1)} %get-tuple-element.84), calls=%async_computation.3 | async-start | bytes 2818048 | tf_op jit(solution)/shard_map/all_to_all | solution.py:341
  224.6 1.5 collective-permute-start.24
  226.0 0.1 collective-permute-start.25
  226.2 2.8 collective-permute-start.26
  228.9 0.4 collective-permute-start.27
  229.4 0.5 collective-permute-start.28
  229.9 18.4 %collective-permute-done.24.refs_0_ = bf16[8,11008]{1,0:T(8,128)(2,1)S(1)} collective-permute-done((bf16[8,11008]{1,0:T(8,128)(2,1)S(1)}, bf16[8,11008]{1,0:T(8,128)(2,1)S(1)}, u32[]{:S(2)}, u32[]{:S(2)}) %collective-permute-start.24) | collective-permute-done | bytes 176160 | tf_op jit(solution)/shard_map/ppermute | solution.py:350
  248.3 4.7 %collective-permute-done.25.refs_1_ = bf16[8,11008]{1,0:T(8,128)(2,1)} collective-permute-done((bf16[8,11008]{1,0:T(8,128)(2,1)S(1)}, bf16[8,11008]{1,0:T(8,128)(2,1)}, u32[]{:S(2)}, u32[]{:S(2)}) %collective-permute-start.25) | collective-permute-done | bytes 176160 | tf_op jit(solution)/shard_map/ppermute | solution.py:350
  253.0 3.2 %collective-permute-start.31 = (bf16[8,11008]{1,0:T(8,128)(2,1)S(1)}, bf16[8,11008]{1,0:T(8,128)(2,1)}, u32[]{:S(2)}, u32[]{:S(2)}) collective-permute-start(bf16[8,11008]{1,0:T(8,128)(2,1)S(1)} %copy-done.7), channel_id=1, source_target_pairs={{0,15},{1,8},{2,9},{3,10},{4,11},{5,12},{6,13},{7,14},{8,7},{9,0},... | collective-permute-start | bytes 528392 | tf_op jit(solution)/shard_map/ppermute | solution.py:350
  256.2 2.9 collective-permute-done.27.refs_3_
  259.1 18.8 %collective-permute-done.28.refs_4_ = bf16[8,11008]{1,0:T(8,128)(2,1)} collective-permute-done((bf16[8,11008]{1,0:T(8,128)(2,1)S(1)}, bf16[8,11008]{1,0:T(8,128)(2,1)}, u32[]{:S(2)}, u32[]{:S(2)}) %collective-permute-start.28) | collective-permute-done | bytes 176160 | tf_op jit(solution)/shard_map/ppermute | solution.py:350
  277.9 5.2 %collective-permute-done.29.refs_5_ = bf16[8,11008]{1,0:T(8,128)(2,1)} collective-permute-done((bf16[8,11008]{1,0:T(8,128)(2,1)S(1)}, bf16[8,11008]{1,0:T(8,128)(2,1)}, u32[]{:S(2)}, u32[]{:S(2)}) %collective-permute-start.29) | collective-permute-done | bytes 176160 | tf_op jit(solution)/shard_map/ppermute | solution.py:350
  283.2 1.3 collective-permute-done.30.refs_6_
  284.5 3.8 %collective-permute-done.31.refs_7_ = bf16[8,11008]{1,0:T(8,128)(2,1)} collective-permute-done((bf16[8,11008]{1,0:T(8,128)(2,1)S(1)}, bf16[8,11008]{1,0:T(8,128)(2,1)}, u32[]{:S(2)}, u32[]{:S(2)}) %collective-permute-start.31) | collective-permute-done | bytes 176160 | tf_op jit(solution)/shard_map/ppermute | solution.py:350
  288.3 4.6 %shard_map.100 = bf16[2,137,80,128]{3,2,1,0:T(8,128)(2,1)} custom-call(bf16[8,8,11008]{2,1,0:T(8,128)(2,1)} %all-to-all-done.3.near_ref, bf16[8,11008]{1,0:T(8,128)(2,1)} %copy-done.1, bf16[8,11008]{1,0:T(8,128)(2,1)} %collective-permute-done.25.refs_1_, bf16[8,11008]{1,0:T(8,128)(2,1)} %collective-permute-done.26.refs_2_, ...), custom_call_target="tpu_custom_call", output_to_operand_aliasing={{}: (9, {})} | custom-call | flops 1402880 | bytes 5611520 | tf_op jit(solution)/shard_map/pallas_call | solution.py:119
  (59 shorter events, 0.1 us)
Async XLA Ops:
  6.0 4.7 %copy-start.18 = (bf16[8,11008]{1,0:T(8,128)(2,1)S(1)}, bf16[8,11008]{1,0:T(8,128)(2,1)}, u32[]{:S(2)}) copy-start(bf16[8,11008]{1,0:T(8,128)(2,1)} %get-tuple-element.55) | copy-start | bytes 528388
  6.0 7.5 %copy-start.17 = (bf16[8,11008]{1,0:T(8,128)(2,1)S(1)}, bf16[8,11008]{1,0:T(8,128)(2,1)}, u32[]{:S(2)}) copy-start(bf16[8,11008]{1,0:T(8,128)(2,1)} %get-tuple-element.56) | copy-start | bytes 528388
  6.0 7.5 %copy-start.16 = (bf16[8,11008]{1,0:T(8,128)(2,1)S(1)}, bf16[8,11008]{1,0:T(8,128)(2,1)}, u32[]{:S(2)}) copy-start(bf16[8,11008]{1,0:T(8,128)(2,1)} %get-tuple-element.57) | copy-start | bytes 528388
  6.0 37.6 %copy-start.4 = (s32[1280]{0:T(1024)S(1)}, s32[1280]{0:T(1024)}, u32[]{:S(2)}) copy-start(s32[1280]{0:T(1024)} %param.10) | copy-start | bytes 15364
  6.0 38.2 %copy-start.5 = (f32[137]{0:T(256)S(1)}, f32[137]{0:T(256)}, u32[]{:S(2)}) copy-start(f32[137]{0:T(256)} %param.13) | copy-start | bytes 1648
  6.0 39.0 %copy-start.2 = (bf16[137,137]{1,0:T(8,128)(2,1)S(1)}, bf16[137,137]{1,0:T(8,128)(2,1)}, u32[]{:S(2)}) copy-start(bf16[137,137]{1,0:T(8,128)(2,1)} %param.14) | copy-start | bytes 112618
  6.0 39.7 %copy-start.3 = (bf16[137,137]{1,0:T(8,128)(2,1)S(1)}, bf16[137,137]{1,0:T(8,128)(2,1)}, u32[]{:S(2)}) copy-start(bf16[137,137]{1,0:T(8,128)(2,1)} %param.15) | copy-start | bytes 112618
  6.1 40.4 %copy-start.19 = (s32[128]{0:T(128)S(1)}, s32[128]{0:T(128)}, u32[]{:S(2)}) copy-start(s32[128]{0:T(128)} %param.11) | copy-start | bytes 1540
  6.1 46.4 %all-to-all-start.1 = ((bf16[8,8,11008]{2,1,0:T(8,128)(2,1)}), bf16[8,8,11008]{2,1,0:T(8,128)(2,1)}, u32[]{:S(2)}, u32[]{:S(2)}) async-start(bf16[8,8,11008]{2,1,0:T(8,128)(2,1)} %get-tuple-element.54), calls=%async_computation.1 | async-start | bytes 2818048 | tf_op jit(solution)/shard_map/all_to_all | solution.py:341
  10.7 25.0 %collective-permute-start.5 = (bf16[8,11008]{1,0:T(8,128)(2,1)S(1)}, bf16[8,11008]{1,0:T(8,128)(2,1)}, u32[]{:S(2)}, u32[]{:S(2)}) collective-permute-start(bf16[8,11008]{1,0:T(8,128)(2,1)S(1)} %copy-done.18), channel_id=1, source_target_pairs={{0,8},{1,9},{2,10},{3,11},{4,12},{5,13},{6,14},{7,15},{8,0},{9,1},... | collective-permute-start | bytes 528392 | tf_op jit(solution)/shard_map/ppermute | solution.py:350
  13.5 27.0 %collective-permute-start.6 = (bf16[8,11008]{1,0:T(8,128)(2,1)S(1)}, bf16[8,11008]{1,0:T(8,128)(2,1)}, u32[]{:S(2)}, u32[]{:S(2)}) collective-permute-start(bf16[8,11008]{1,0:T(8,128)(2,1)S(1)} %copy-done.17), channel_id=1, source_target_pairs={{0,9},{1,10},{2,11},{3,12},{4,13},{5,14},{6,15},{7,8},{8,1},{9,2},... | collective-permute-start | bytes 528392 | tf_op jit(solution)/shard_map/ppermute | solution.py:350
  13.5 27.5 %collective-permute-start.7 = (bf16[8,11008]{1,0:T(8,128)(2,1)S(1)}, bf16[8,11008]{1,0:T(8,128)(2,1)}, u32[]{:S(2)}, u32[]{:S(2)}) collective-permute-start(bf16[8,11008]{1,0:T(8,128)(2,1)S(1)} %copy-done.16), channel_id=1, source_target_pairs={{0,10},{1,11},{2,12},{3,13},{4,14},{5,15},{6,8},{7,9},{8,2},{9,3},... | collective-permute-start | bytes 528392 | tf_op jit(solution)/shard_map/ppermute | solution.py:350
  16.3 44.4 %collective-permute-start.8 = (bf16[8,11008]{1,0:T(8,128)(2,1)}, bf16[8,11008]{1,0:T(8,128)(2,1)S(1)}, u32[]{:S(2)}, u32[]{:S(2)}) collective-permute-start(bf16[8,11008]{1,0:T(8,128)(2,1)} %get-tuple-element.58), channel_id=1, source_target_pairs={{0,11},{1,12},{2,13},{3,14},{4,15},{5,8},{6,9},{7,10},{8,3},{9,4},... | collective-permute-start | bytes 528392 | tf_op jit(solution)/shard_map/ppermute | solution.py:350
  16.3 48.6 %collective-permute-start.9 = (bf16[8,11008]{1,0:T(8,128)(2,1)}, bf16[8,11008]{1,0:T(8,128)(2,1)}, u32[]{:S(2)}, u32[]{:S(2)}) collective-permute-start(bf16[8,11008]{1,0:T(8,128)(2,1)} %get-tuple-element.59), channel_id=1, source_target_pairs={{0,12},{1,13},{2,14},{3,15},{4,8},{5,9},{6,10},{7,11},{8,4},{9,5},... | collective-permute-start | bytes 528392 | tf_op jit(solution)/shard_map/ppermute | solution.py:350
  35.7 34.0 %collective-permute-start.10 = (bf16[8,11008]{1,0:T(8,128)(2,1)}, bf16[8,11008]{1,0:T(8,128)(2,1)}, u32[]{:S(2)}, u32[]{:S(2)}) collective-permute-start(bf16[8,11008]{1,0:T(8,128)(2,1)} %get-tuple-element.60), channel_id=1, source_target_pairs={{0,13},{1,14},{2,15},{3,8},{4,9},{5,10},{6,11},{7,12},{8,5},{9,6},... | collective-permute-start | bytes 528392 | tf_op jit(solution)/shard_map/ppermute | solution.py:350
  40.4 34.6 %collective-permute-start.11 = (bf16[8,11008]{1,0:T(8,128)(2,1)}, bf16[8,11008]{1,0:T(8,128)(2,1)}, u32[]{:S(2)}, u32[]{:S(2)}) collective-permute-start(bf16[8,11008]{1,0:T(8,128)(2,1)} %get-tuple-element.61), channel_id=1, source_target_pairs={{0,14},{1,15},{2,8},{3,9},{4,10},{5,11},{6,12},{7,13},{8,6},{9,7},... | collective-permute-start | bytes 528392 | tf_op jit(solution)/shard_map/ppermute | solution.py:350
  41.0 36.4 %collective-permute-start.12 = (bf16[8,11008]{1,0:T(8,128)(2,1)}, bf16[8,11008]{1,0:T(8,128)(2,1)}, u32[]{:S(2)}, u32[]{:S(2)}) collective-permute-start(bf16[8,11008]{1,0:T(8,128)(2,1)} %get-tuple-element.62), channel_id=1, source_target_pairs={{0,15},{1,8},{2,9},{3,10},{4,11},{5,12},{6,13},{7,14},{8,7},{9,0},... | collective-permute-start | bytes 528392 | tf_op jit(solution)/shard_map/ppermute | solution.py:350
  52.4 81.6 %all-to-all-start = ((bf16[8,8,11008]{2,1,0:T(8,128)(2,1)}), bf16[8,8,11008]{2,1,0:T(8,128)(2,1)}, u32[]{:S(2)}, u32[]{:S(2)}) async-start(bf16[8,8,11008]{2,1,0:T(8,128)(2,1)} %get-tuple-element.48), calls=%async_computation | async-start | bytes 2818048 | tf_op jit(solution)/shard_map/all_to_all | solution.py:341
  60.7 0.7 copy-start.12
  61.4 51.3 %collective-permute-start = (bf16[8,11008]{1,0:T(8,128)(2,1)}, bf16[8,11008]{1,0:T(8,128)(2,1)S(1)}, u32[]{:S(2)}, u32[]{:S(2)}) collective-permute-start(bf16[8,11008]{1,0:T(8,128)(2,1)} %get-tuple-element.49), channel_id=1, source_target_pairs={{0,8},{1,9},{2,10},{3,11},{4,12},{5,13},{6,14},{7,15},{8,0},{9,1},... | collective-permute-start | bytes 528392 | tf_op jit(solution)/shard_map/ppermute | solution.py:350
  64.9 50.4 %collective-permute-start.1 = (bf16[8,11008]{1,0:T(8,128)(2,1)}, bf16[8,11008]{1,0:T(8,128)(2,1)}, u32[]{:S(2)}, u32[]{:S(2)}) collective-permute-start(bf16[8,11008]{1,0:T(8,128)(2,1)} %get-tuple-element.50), channel_id=1, source_target_pairs={{0,9},{1,10},{2,11},{3,12},{4,13},{5,14},{6,15},{7,8},{8,1},{9,2},... | collective-permute-start | bytes 528392 | tf_op jit(solution)/shard_map/ppermute | solution.py:350
  69.6 64.3 %collective-permute-start.2 = (bf16[8,11008]{1,0:T(8,128)(2,1)}, bf16[8,11008]{1,0:T(8,128)(2,1)}, u32[]{:S(2)}, u32[]{:S(2)}) collective-permute-start(bf16[8,11008]{1,0:T(8,128)(2,1)} %get-tuple-element.51), channel_id=1, source_target_pairs={{0,10},{1,11},{2,12},{3,13},{4,14},{5,15},{6,8},{7,9},{8,2},{9,3},... | collective-permute-start | bytes 528392 | tf_op jit(solution)/shard_map/ppermute | solution.py:350
  75.0 64.6 %collective-permute-start.3 = (bf16[8,11008]{1,0:T(8,128)(2,1)}, bf16[8,11008]{1,0:T(8,128)(2,1)}, u32[]{:S(2)}, u32[]{:S(2)}) collective-permute-start(bf16[8,11008]{1,0:T(8,128)(2,1)} %get-tuple-element.52), channel_id=1, source_target_pairs={{0,11},{1,12},{2,13},{3,14},{4,15},{5,8},{6,9},{7,10},{8,3},{9,4},... | collective-permute-start | bytes 528392 | tf_op jit(solution)/shard_map/ppermute | solution.py:350
  77.4 64.8 %collective-permute-start.4 = (bf16[8,11008]{1,0:T(8,128)(2,1)}, bf16[8,11008]{1,0:T(8,128)(2,1)}, u32[]{:S(2)}, u32[]{:S(2)}) collective-permute-start(bf16[8,11008]{1,0:T(8,128)(2,1)} %get-tuple-element.53), channel_id=1, source_target_pairs={{0,12},{1,13},{2,14},{3,15},{4,8},{5,9},{6,10},{7,11},{8,4},{9,5},... | collective-permute-start | bytes 528392 | tf_op jit(solution)/shard_map/ppermute | solution.py:350
  112.7 21.3 %copy-start.6 = (bf16[8,11008]{1,0:T(8,128)(2,1)}, bf16[8,11008]{1,0:T(8,128)(2,1)S(1)}, u32[]{:S(2)}) copy-start(bf16[8,11008]{1,0:T(8,128)(2,1)S(1)} %collective-permute-done.refs_0_) | copy-start | bytes 528388
  112.7 31.8 %collective-permute-start.13 = (bf16[8,11008]{1,0:T(8,128)(2,1)}, bf16[8,11008]{1,0:T(8,128)(2,1)}, u32[]{:S(2)}, u32[]{:S(2)}) collective-permute-start(bf16[8,11008]{1,0:T(8,128)(2,1)} %get-tuple-element.66), channel_id=1, source_target_pairs={{0,13},{1,14},{2,15},{3,8},{4,9},{5,10},{6,11},{7,12},{8,5},{9,6},... | collective-permute-start | bytes 528392 | tf_op jit(solution)/shard_map/ppermute | solution.py:350
  115.3 36.1 %collective-permute-start.14 = (bf16[8,11008]{1,0:T(8,128)(2,1)}, bf16[8,11008]{1,0:T(8,128)(2,1)}, u32[]{:S(2)}, u32[]{:S(2)}) collective-permute-start(bf16[8,11008]{1,0:T(8,128)(2,1)} %get-tuple-element.67), channel_id=1, source_target_pairs={{0,14},{1,15},{2,8},{3,9},{4,10},{5,11},{6,12},{7,13},{8,6},{9,7},... | collective-permute-start | bytes 528392 | tf_op jit(solution)/shard_map/ppermute | solution.py:350
  134.0 18.7 %collective-permute-start.15 = (bf16[8,11008]{1,0:T(8,128)(2,1)}, bf16[8,11008]{1,0:T(8,128)(2,1)}, u32[]{:S(2)}, u32[]{:S(2)}) collective-permute-start(bf16[8,11008]{1,0:T(8,128)(2,1)} %get-tuple-element.68), channel_id=1, source_target_pairs={{0,15},{1,8},{2,9},{3,10},{4,11},{5,12},{6,13},{7,14},{8,7},{9,0},... | collective-permute-start | bytes 528392 | tf_op jit(solution)/shard_map/ppermute | solution.py:350
  134.0 79.8 %all-to-all-start.2 = ((bf16[8,8,11008]{2,1,0:T(8,128)(2,1)}), bf16[8,8,11008]{2,1,0:T(8,128)(2,1)}, u32[]{:S(2)}, u32[]{:S(2)}) async-start(bf16[8,8,11008]{2,1,0:T(8,128)(2,1)} %get-tuple-element.74), calls=%async_computation.2 | async-start | bytes 2818048 | tf_op jit(solution)/shard_map/all_to_all | solution.py:341
  139.6 49.5 %collective-permute-start.16 = (bf16[8,11008]{1,0:T(8,128)(2,1)}, bf16[8,11008]{1,0:T(8,128)(2,1)S(1)}, u32[]{:S(2)}, u32[]{:S(2)}) collective-permute-start(bf16[8,11008]{1,0:T(8,128)(2,1)} %get-tuple-element.75), channel_id=1, source_target_pairs={{0,8},{1,9},{2,10},{3,11},{4,12},{5,13},{6,14},{7,15},{8,0},{9,1},... | collective-permute-start | bytes 528392 | tf_op jit(solution)/shard_map/ppermute | solution.py:350
  142.2 50.6 %collective-permute-start.17 = (bf16[8,11008]{1,0:T(8,128)(2,1)}, bf16[8,11008]{1,0:T(8,128)(2,1)}, u32[]{:S(2)}, u32[]{:S(2)}) collective-permute-start(bf16[8,11008]{1,0:T(8,128)(2,1)} %get-tuple-element.76), channel_id=1, source_target_pairs={{0,9},{1,10},{2,11},{3,12},{4,13},{5,14},{6,15},{7,8},{8,1},{9,2},... | collective-permute-start | bytes 528392 | tf_op jit(solution)/shard_map/ppermute | solution.py:350
  144.5 48.3 %collective-permute-start.18 = (bf16[8,11008]{1,0:T(8,128)(2,1)}, bf16[8,11008]{1,0:T(8,128)(2,1)}, u32[]{:S(2)}, u32[]{:S(2)}) collective-permute-start(bf16[8,11008]{1,0:T(8,128)(2,1)} %get-tuple-element.77), channel_id=1, source_target_pairs={{0,10},{1,11},{2,12},{3,13},{4,14},{5,15},{6,8},{7,9},{8,2},{9,3},... | collective-permute-start | bytes 528392 | tf_op jit(solution)/shard_map/ppermute | solution.py:350
  151.4 41.9 %collective-permute-start.19 = (bf16[8,11008]{1,0:T(8,128)(2,1)}, bf16[8,11008]{1,0:T(8,128)(2,1)}, u32[]{:S(2)}, u32[]{:S(2)}) collective-permute-start(bf16[8,11008]{1,0:T(8,128)(2,1)} %get-tuple-element.78), channel_id=1, source_target_pairs={{0,11},{1,12},{2,13},{3,14},{4,15},{5,8},{6,9},{7,10},{8,3},{9,4},... | collective-permute-start | bytes 528392 | tf_op jit(solution)/shard_map/ppermute | solution.py:350
  152.7 40.6 %collective-permute-start.20 = (bf16[8,11008]{1,0:T(8,128)(2,1)}, bf16[8,11008]{1,0:T(8,128)(2,1)}, u32[]{:S(2)}, u32[]{:S(2)}) collective-permute-start(bf16[8,11008]{1,0:T(8,128)(2,1)} %get-tuple-element.79), channel_id=1, source_target_pairs={{0,12},{1,13},{2,14},{3,15},{4,8},{5,9},{6,10},{7,11},{8,4},{9,5},... | collective-permute-start | bytes 528392 | tf_op jit(solution)/shard_map/ppermute | solution.py:350
  189.1 24.7 %copy-start = (bf16[8,11008]{1,0:T(8,128)(2,1)}, bf16[8,11008]{1,0:T(8,128)(2,1)S(1)}, u32[]{:S(2)}) copy-start(bf16[8,11008]{1,0:T(8,128)(2,1)S(1)} %collective-permute-done.16.refs_0_) | copy-start | bytes 528388
  189.1 14.4 %collective-permute-start.21 = (bf16[8,11008]{1,0:T(8,128)(2,1)}, bf16[8,11008]{1,0:T(8,128)(2,1)}, u32[]{:S(2)}, u32[]{:S(2)}) collective-permute-start(bf16[8,11008]{1,0:T(8,128)(2,1)} %get-tuple-element.80), channel_id=1, source_target_pairs={{0,13},{1,14},{2,15},{3,8},{4,9},{5,10},{6,11},{7,12},{8,5},{9,6},... | collective-permute-start | bytes 528392 | tf_op jit(solution)/shard_map/ppermute | solution.py:350
  192.8 17.5 %collective-permute-start.22 = (bf16[8,11008]{1,0:T(8,128)(2,1)}, bf16[8,11008]{1,0:T(8,128)(2,1)}, u32[]{:S(2)}, u32[]{:S(2)}) collective-permute-start(bf16[8,11008]{1,0:T(8,128)(2,1)} %get-tuple-element.81), channel_id=1, source_target_pairs={{0,14},{1,15},{2,8},{3,9},{4,10},{5,11},{6,12},{7,13},{8,6},{9,7},... | collective-permute-start | bytes 528392 | tf_op jit(solution)/shard_map/ppermute | solution.py:350
  192.8 21.0 %collective-permute-start.23 = (bf16[8,11008]{1,0:T(8,128)(2,1)}, bf16[8,11008]{1,0:T(8,128)(2,1)}, u32[]{:S(2)}, u32[]{:S(2)}) collective-permute-start(bf16[8,11008]{1,0:T(8,128)(2,1)} %get-tuple-element.82), channel_id=1, source_target_pairs={{0,15},{1,8},{2,9},{3,10},{4,11},{5,12},{6,13},{7,14},{8,7},{9,0},... | collective-permute-start | bytes 528392 | tf_op jit(solution)/shard_map/ppermute | solution.py:350
  218.4 6.1 %copy-start.15 = (bf16[8,11008]{1,0:T(8,128)(2,1)S(1)}, bf16[8,11008]{1,0:T(8,128)(2,1)}, u32[]{:S(2)}) copy-start(bf16[8,11008]{1,0:T(8,128)(2,1)} %get-tuple-element.85) | copy-start | bytes 528388
  218.4 7.6 %copy-start.14 = (bf16[8,11008]{1,0:T(8,128)(2,1)S(1)}, bf16[8,11008]{1,0:T(8,128)(2,1)}, u32[]{:S(2)}) copy-start(bf16[8,11008]{1,0:T(8,128)(2,1)} %get-tuple-element.86) | copy-start | bytes 528388
  218.4 7.7 %copy-start.13 = (bf16[8,11008]{1,0:T(8,128)(2,1)S(1)}, bf16[8,11008]{1,0:T(8,128)(2,1)}, u32[]{:S(2)}) copy-start(bf16[8,11008]{1,0:T(8,128)(2,1)} %get-tuple-element.87) | copy-start | bytes 528388
  218.4 10.5 %copy-start.11 = (bf16[8,11008]{1,0:T(8,128)(2,1)S(1)}, bf16[8,11008]{1,0:T(8,128)(2,1)}, u32[]{:S(2)}) copy-start(bf16[8,11008]{1,0:T(8,128)(2,1)} %get-tuple-element.88) | copy-start | bytes 528388
  218.5 10.9 %copy-start.10 = (bf16[8,11008]{1,0:T(8,128)(2,1)S(1)}, bf16[8,11008]{1,0:T(8,128)(2,1)}, u32[]{:S(2)}) copy-start(bf16[8,11008]{1,0:T(8,128)(2,1)} %get-tuple-element.89) | copy-start | bytes 528388
  218.5 29.8 %copy-start.9 = (bf16[8,11008]{1,0:T(8,128)(2,1)S(1)}, bf16[8,11008]{1,0:T(8,128)(2,1)}, u32[]{:S(2)}) copy-start(bf16[8,11008]{1,0:T(8,128)(2,1)} %get-tuple-element.90) | copy-start | bytes 528388
  218.5 34.5 %copy-start.8 = (bf16[8,11008]{1,0:T(8,128)(2,1)S(1)}, bf16[8,11008]{1,0:T(8,128)(2,1)}, u32[]{:S(2)}) copy-start(bf16[8,11008]{1,0:T(8,128)(2,1)} %get-tuple-element.91) | copy-start | bytes 528388
  218.5 34.5 %copy-start.7 = (bf16[8,11008]{1,0:T(8,128)(2,1)S(1)}, bf16[8,11008]{1,0:T(8,128)(2,1)}, u32[]{:S(2)}) copy-start(bf16[8,11008]{1,0:T(8,128)(2,1)} %get-tuple-element.92) | copy-start | bytes 528388
  218.5 69.8 %all-to-all-start.3 = ((bf16[8,8,11008]{2,1,0:T(8,128)(2,1)}), bf16[8,8,11008]{2,1,0:T(8,128)(2,1)}, u32[]{:S(2)}, u32[]{:S(2)}) async-start(bf16[8,8,11008]{2,1,0:T(8,128)(2,1)} %get-tuple-element.84), calls=%async_computation.3 | async-start | bytes 2818048 | tf_op jit(solution)/shard_map/all_to_all | solution.py:341
  224.6 23.7 %collective-permute-start.24 = (bf16[8,11008]{1,0:T(8,128)(2,1)S(1)}, bf16[8,11008]{1,0:T(8,128)(2,1)S(1)}, u32[]{:S(2)}, u32[]{:S(2)}) collective-permute-start(bf16[8,11008]{1,0:T(8,128)(2,1)S(1)} %copy-done.15), channel_id=1, source_target_pairs={{0,8},{1,9},{2,10},{3,11},{4,12},{5,13},{6,14},{7,15},{8,0},{9,1},... | collective-permute-start | bytes 528392 | tf_op jit(solution)/shard_map/ppermute | solution.py:350
  226.0 27.0 %collective-permute-start.25 = (bf16[8,11008]{1,0:T(8,128)(2,1)S(1)}, bf16[8,11008]{1,0:T(8,128)(2,1)}, u32[]{:S(2)}, u32[]{:S(2)}) collective-permute-start(bf16[8,11008]{1,0:T(8,128)(2,1)S(1)} %copy-done.14), channel_id=1, source_target_pairs={{0,9},{1,10},{2,11},{3,12},{4,13},{5,14},{6,15},{7,8},{8,1},{9,2},... | collective-permute-start | bytes 528392 | tf_op jit(solution)/shard_map/ppermute | solution.py:350
  226.2 26.8 %collective-permute-start.26 = (bf16[8,11008]{1,0:T(8,128)(2,1)S(1)}, bf16[8,11008]{1,0:T(8,128)(2,1)}, u32[]{:S(2)}, u32[]{:S(2)}) collective-permute-start(bf16[8,11008]{1,0:T(8,128)(2,1)S(1)} %copy-done.13), channel_id=1, source_target_pairs={{0,10},{1,11},{2,12},{3,13},{4,14},{5,15},{6,8},{7,9},{8,2},{9,3},... | collective-permute-start | bytes 528392 | tf_op jit(solution)/shard_map/ppermute | solution.py:350
  228.9 30.1 %collective-permute-start.27 = (bf16[8,11008]{1,0:T(8,128)(2,1)S(1)}, bf16[8,11008]{1,0:T(8,128)(2,1)}, u32[]{:S(2)}, u32[]{:S(2)}) collective-permute-start(bf16[8,11008]{1,0:T(8,128)(2,1)S(1)} %copy-done.11), channel_id=1, source_target_pairs={{0,11},{1,12},{2,13},{3,14},{4,15},{5,8},{6,9},{7,10},{8,3},{9,4},... | collective-permute-start | bytes 528392 | tf_op jit(solution)/shard_map/ppermute | solution.py:350
  229.4 48.6 %collective-permute-start.28 = (bf16[8,11008]{1,0:T(8,128)(2,1)S(1)}, bf16[8,11008]{1,0:T(8,128)(2,1)}, u32[]{:S(2)}, u32[]{:S(2)}) collective-permute-start(bf16[8,11008]{1,0:T(8,128)(2,1)S(1)} %copy-done.10), channel_id=1, source_target_pairs={{0,12},{1,13},{2,14},{3,15},{4,8},{5,9},{6,10},{7,11},{8,4},{9,5},... | collective-permute-start | bytes 528392 | tf_op jit(solution)/shard_map/ppermute | solution.py:350
  248.3 40.0 %copy-start.1 = (bf16[8,11008]{1,0:T(8,128)(2,1)}, bf16[8,11008]{1,0:T(8,128)(2,1)S(1)}, u32[]{:S(2)}) copy-start(bf16[8,11008]{1,0:T(8,128)(2,1)S(1)} %collective-permute-done.24.refs_0_) | copy-start | bytes 528388
  248.3 34.9 %collective-permute-start.29 = (bf16[8,11008]{1,0:T(8,128)(2,1)S(1)}, bf16[8,11008]{1,0:T(8,128)(2,1)}, u32[]{:S(2)}, u32[]{:S(2)}) collective-permute-start(bf16[8,11008]{1,0:T(8,128)(2,1)S(1)} %copy-done.9), channel_id=1, source_target_pairs={{0,13},{1,14},{2,15},{3,8},{4,9},{5,10},{6,11},{7,12},{8,5},{9,6},... | collective-permute-start | bytes 528392 | tf_op jit(solution)/shard_map/ppermute | solution.py:350
  253.0 31.5 %collective-permute-start.30 = (bf16[8,11008]{1,0:T(8,128)(2,1)S(1)}, bf16[8,11008]{1,0:T(8,128)(2,1)}, u32[]{:S(2)}, u32[]{:S(2)}) collective-permute-start(bf16[8,11008]{1,0:T(8,128)(2,1)S(1)} %copy-done.8), channel_id=1, source_target_pairs={{0,14},{1,15},{2,8},{3,9},{4,10},{5,11},{6,12},{7,13},{8,6},{9,7},... | collective-permute-start | bytes 528392 | tf_op jit(solution)/shard_map/ppermute | solution.py:350
  253.0 35.2 %collective-permute-start.31 = (bf16[8,11008]{1,0:T(8,128)(2,1)S(1)}, bf16[8,11008]{1,0:T(8,128)(2,1)}, u32[]{:S(2)}, u32[]{:S(2)}) collective-permute-start(bf16[8,11008]{1,0:T(8,128)(2,1)S(1)} %copy-done.7), channel_id=1, source_target_pairs={{0,15},{1,8},{2,9},{3,10},{4,11},{5,12},{6,13},{7,14},{8,7},{9,0},... | collective-permute-start | bytes 528392 | tf_op jit(solution)/shard_map/ppermute | solution.py:350

commit v5 on v3

--- a/solution.py
+++ b/solution.py
@@ -9,9 +9,10 @@
 from jax.sharding import PartitionSpec as P
 
 NMAX = 2559
-VMEM_BYTES = 62 * 1024 * 1024
+VMEM_BYTES = 255 * 256 * 1024
 GROUP = 48
 LANES = 128
+NEAR = 2
 
 
 def flat_rows(value):
@@ -21,53 +22,111 @@
     return value.reshape(group * lat_dev, slots).astype(jnp.bfloat16)
 
 
-def pack_body(north_ref, south_ref, out_ref):
+def take_blocks(in_refs, blocks_ref):
+    partners = len(in_refs)
+    if partners == 1:
+        return in_refs[0]
+    my_index = lax.axis_index("wave")
+    for k in range(partners):
+        blocks_ref[lax.rem(my_index + (partners - k), partners)] = in_refs[k][...]
+    return blocks_ref
+
+
+def give_blocks(blocks_ref, out_refs):
+    partners = len(out_refs)
+    if partners == 1:
+        out_refs[0][...] = blocks_ref[...]
+        return
+    my_index = lax.axis_index("wave")
+    for k in range(partners):
+        out_refs[k][...] = blocks_ref[lax.rem(my_index + k, partners)]
+
+
+def gate(blocks, after):
+    if not after:
+        return blocks
+    anywhere = pl.BlockSpec(memory_space=pl.ANY)
+    return pl.pallas_call(
+        lambda *refs: None,
+        in_specs=[anywhere] * (len(blocks) + len(after)),
+        out_specs=[anywhere] * len(blocks),
+        out_shape=[jax.ShapeDtypeStruct(block.shape, block.dtype) for block in blocks],
+        input_output_aliases={i: i for i in range(len(blocks))},
+        compiler_params=pltpu.CompilerParams(vmem_limit_bytes=VMEM_BYTES),
+    )(*blocks, *after)
+
+
+def block_shapes(ring, partners, slot_dev, width):
+    if ring:
+        return [jax.ShapeDtypeStruct((slot_dev, width), jnp.bfloat16)] * partners
+    return [jax.ShapeDtypeStruct((partners, slot_dev, width), jnp.bfloat16)]
+
+
+def block_specs(ring, partners, slot_dev, lanes):
+    if ring:
+        return [pl.BlockSpec((slot_dev, lanes), lambda i: (0, i))] * partners
+    return [pl.BlockSpec((partners, slot_dev, lanes), lambda i: (0, 0, i))]
+
+
+def pack_body(north_ref, south_ref, *refs, after):
+    out_refs, blocks_ref = refs[after:-1], refs[-1]
+    partners, slot_dev, _ = blocks_ref.shape
     summed = north_ref[0].astype(jnp.float32) + south_ref[0].astype(jnp.float32)
-    out_ref[...] = flat_rows(summed.astype(jnp.bfloat16)).T
-
-
-def pack(part, north, south):
+    columns = flat_rows(summed.astype(jnp.bfloat16)).T
+    for device in range(partners):
+        blocks_ref[device] = columns[device * slot_dev : (device + 1) * slot_dev]
+    give_blocks(blocks_ref, out_refs)
+
+
+def pack(part, ring, partners, north, south, after):
     _, levels, lat_dev, slots = north.shape
+    slot_dev = slots // partners
+    width = pl.cdiv(levels * lat_dev, LANES) * LANES
     rows = pl.BlockSpec((1, GROUP, lat_dev, slots), lambda i: (part, i, 0, 0))
     return pl.pallas_call(
-        pack_body,
+        functools.partial(pack_body, after=len(after)),
         grid=(pl.cdiv(levels, GROUP),),
-        in_specs=[rows, rows],
-        out_specs=pl.BlockSpec((slots, GROUP * lat_dev), lambda i: (0, i)),
-        out_shape=jax.ShapeDtypeStruct((slots, pl.cdiv(levels * lat_dev, LANES) * LANES), jnp.bfloat16),
+        in_specs=[rows, rows] + [pl.BlockSpec(memory_space=pl.ANY)] * len(after),
+        out_specs=block_specs(ring, partners, slot_dev, GROUP * lat_dev),
+        out_shape=block_shapes(ring, partners, slot_dev, width),
+        scratch_shapes=[pltpu.VMEM((partners, slot_dev, GROUP * lat_dev), jnp.bfloat16)],
         compiler_params=pltpu.CompilerParams(vmem_limit_bytes=VMEM_BYTES),
         cost_estimate=pl.CostEstimate(
             flops=2 * levels * lat_dev * slots,
             bytes_accessed=6 * levels * lat_dev * slots,
             transcendentals=0,
         ),
-    )(north, south)
-
-
-def unpack_body(in_ref, *refs):
-    out_ref = refs[-1]
+    )(north, south, *after)
+
+
+def unpack_body(*refs, arrays):
+    out_ref, blocks_ref = refs[-2:]
     _, group, lat_dev, slots = out_ref.shape
-    rows = in_ref[...].T
+    taken_ref = take_blocks(refs[:arrays], blocks_ref)
+    blocks = [taken_ref[device].astype(jnp.float32) for device in range(blocks_ref.shape[0])]
+    rows = jnp.concatenate(blocks, axis=0).astype(jnp.bfloat16).T
     if lat_dev % 16:
         rows = rows.astype(jnp.float32)
     out_ref[0] = rows.reshape(group, lat_dev, slots).astype(jnp.bfloat16)
 
 
-def unpack(part, parts, levels, lat_dev, received, earlier):
-    slots = received.shape[0]
-    in_specs = [pl.BlockSpec((slots, GROUP * lat_dev), lambda i: (0, i))]
-    operands = [received]
+def unpack(part, parts, levels, lat_dev, slots, received, earlier):
+    slot_dev = received[0].shape[-2]
+    partners = slots // slot_dev
+    in_specs = block_specs(len(received) > 1, partners, slot_dev, GROUP * lat_dev)
+    operands = list(received)
     aliases = {}
     if earlier is not None:
         in_specs.append(pl.BlockSpec(memory_space=pl.ANY))
+        aliases = {len(operands): 0}
         operands.append(earlier)
-        aliases = {1: 0}
     return pl.pallas_call(
-        unpack_body,
+        functools.partial(unpack_body, arrays=len(received)),
         grid=(pl.cdiv(levels, GROUP),),
         in_specs=in_specs,
         out_specs=pl.BlockSpec((1, GROUP, lat_dev, slots), lambda i: (part, i, 0, 0)),
         out_shape=jax.ShapeDtypeStruct((parts, levels, lat_dev, slots), jnp.bfloat16),
+        scratch_shapes=[pltpu.VMEM((partners, slot_dev, GROUP * lat_dev), jnp.bfloat16)],
         input_output_aliases=aliases,
         compiler_params=pltpu.CompilerParams(vmem_limit_bytes=VMEM_BYTES),
         cost_estimate=pl.CostEstimate(
@@ -112,16 +171,9 @@
     lat_total = rows_ref.shape[0] * LANES
     base = pl.multiple_of(first * lat_dev, LANES)
     lane_index = lax.broadcasted_iota(jnp.int32, (slot_dev, LANES), 1)
-    pairs = {}
 
     def load(device, tile):
-        pair = device // 2
-        if (pair, tile) not in pairs:
-            pairs[pair, tile] = recv_ref[
-                2 * pair * slot_dev : 2 * (pair + 1) * slot_dev, pl.ds(base + tile * LANES, LANES)
-            ].astype(jnp.float32)
-        at = (device % 2) * slot_dev
-        return pairs[pair, tile][at : at + slot_dev]
+        return recv_ref[device, :, pl.ds(base + tile * LANES, LANES)].astype(jnp.float32)
 
     cache = {}
     for lanes in range(0, lat_total, LANES):
@@ -143,20 +195,16 @@
         row = pl.multiple_of((first + i) * slot_dev, slot_dev)
         return rows_ref[tile, pl.ds(row, slot_dev), :]
 
-    for pair in range(devices // 2):
+    for device in range(devices):
         for lanes in range(0, group * lat_dev, LANES):
-            tiles = []
-            for device in (2 * pair, 2 * pair + 1):
-                runs = lane_runs(
-                    lanes,
-                    lambda l: (l // lat_dev, device * lat_dev + l % lat_dev)
-                    if l < group * lat_dev
-                    else None,
-                )
-                tiles.append(merge_runs(runs, load, cache, lane_index))
-            send_ref[
-                2 * pair * slot_dev : 2 * (pair + 1) * slot_dev, pl.ds(base + lanes, LANES)
-            ] = jnp.concatenate(tiles, axis=0).astype(jnp.bfloat16)
+            runs = lane_runs(
+                lanes,
+                lambda l: (l // lat_dev, device * lat_dev + l % lat_dev)
+                if l < group * lat_dev
+                else None,
+            )
+            tile = merge_runs(runs, load, cache, lane_index).astype(jnp.bfloat16)
+            send_ref[device, :, pl.ds(base + lanes, LANES)] = tile
 
 
 def join_tiles(ref, rows):
@@ -180,16 +228,20 @@
         body(full * group, levels % group)
 
 
-def step_body(waves_ref, recv_ref, legendre_ref, counts_ref, rates_ref, to_ref, from_ref, *refs):
-    state_ref, send_ref, rows_ref, spec_ref = refs[-4:]
+def step_body(waves_ref, *refs, taken, given):
+    recv_refs, refs = refs[:taken], refs[taken:]
+    legendre_ref, counts_ref, rates_ref, to_ref, from_ref = refs[:5]
+    rows_ref, spec_ref, blocks_ref = refs[-3:]
+    state_ref, *send_refs = refs[-4 - given : -3]
     slot = pl.program_id(0)
     wave = waves_ref[slot]
     row_total, lat_total = legendre_ref.shape[1:]
     _, levels, slot_dev, _ = state_ref.shape
-    lat_dev = lat_total // (recv_ref.shape[0] // slot_dev)
+    lat_dev = lat_total // blocks_ref.shape[0]
 
     @pl.when(slot == 0)
     def _():
+        recv_ref = take_blocks(recv_refs, blocks_ref)
         all_groups(
             levels, lat_dev, lambda c, n: spread(recv_ref, rows_ref, c, n, lat_dev, slot_dev)
         )
@@ -216,9 +268,12 @@
 
     @pl.when(slot == slot_dev - 1)
     def _():
+        send_ref = blocks_ref if given > 1 else send_refs[0]
         all_groups(
             levels, lat_dev, lambda c, n: gather(rows_ref, send_ref, c, n, lat_dev, slot_dev)
         )
+        if given > 1:
+            give_blocks(blocks_ref, send_refs)
 
         @pl.loop(0, levels)
         def _(c):
@@ -226,52 +281,65 @@
             state_ref[0, c] = join_tiles(spec_ref, pl.ds(at, slot_dev)).astype(jnp.bfloat16)
 
 
-def spectral_step(part, parts, received, legendre, own_waves, counts, rates, to_t, from_t, earlier):
-    slots, width = received.shape
+def spectral_step(part, parts, ring, partners, received, legendre, own_waves, counts, rates, to_t, from_t, earlier):
+    width = received[0].shape[-1]
     slot_dev, row_total, lat_total = legendre.shape
     levels = to_t.shape[0]
     whole = lambda shape: pl.BlockSpec(shape, lambda s, waves: (0,) * len(shape))
-    in_specs = [
-        whole((slots, width)),
+    shapes = block_shapes(ring, partners, slot_dev, width)
+    in_specs = [whole(block.shape) for block in received] + [
         pl.BlockSpec((1, row_total, lat_total), lambda s, waves: (s, 0, 0)),
         whole((1, lat_total)),
         whole((levels, 1)),
         whole((levels, levels)),
         whole((levels, levels)),
     ]
-    operands = [own_waves, received, legendre, counts, rates, to_t, from_t]
+    operands = [own_waves, *received, legendre, counts, rates, to_t, from_t]
     aliases = {}
     if earlier is not None:
+        aliases[len(operands)] = 0
+        operands.append(earlier)
         in_specs.append(pl.BlockSpec(memory_space=pl.ANY))
-        aliases = {len(operands): 0}
-        operands.append(earlier)
-    return pl.pallas_call(
-        step_body,
+    state, *blocks = pl.pallas_call(
+        functools.partial(step_body, taken=len(received), given=len(shapes)),
         grid_spec=pltpu.PrefetchScalarGridSpec(
             num_scalar_prefetch=1,
             grid=(slot_dev,),
             in_specs=in_specs,
             out_specs=[
                 pl.BlockSpec((1, levels, slot_dev, row_total), lambda s, waves: (part, 0, 0, 0)),
-                whole((slots, width)),
-            ],
+            ]
+            + [whole(shape.shape) for shape in shapes],
             scratch_shapes=[
                 pltpu.VMEM((lat_total // LANES, levels * slot_dev, LANES), jnp.float32),
                 pltpu.VMEM((row_total // LANES, levels * slot_dev, LANES), jnp.float32),
+                pltpu.VMEM((partners, slot_dev, width), jnp.bfloat16),
             ],
         ),
         out_shape=[
             jax.ShapeDtypeStruct((parts, levels, slot_dev, row_total), jnp.bfloat16),
-            jax.ShapeDtypeStruct((slots, width), jnp.bfloat16),
+            *shapes,
         ],
         input_output_aliases=aliases,
         compiler_params=pltpu.CompilerParams(vmem_limit_bytes=VMEM_BYTES),
         cost_estimate=pl.CostEstimate(
-            flops=4 * slot_dev * row_total * lat_total * levels,
+            flops=16 * slot_dev * row_total * lat_total * levels,
             bytes_accessed=2 * slot_dev * lat_total * (row_total + 3 * levels),
             transcendentals=0,
         ),
     )(*operands)
+    return state, blocks
+
+
+def exchange(blocks):
+    partners = len(blocks)
+    if partners == 1:
+        return [lax.all_to_all(blocks[0], "wave", split_axis=0, concat_axis=0, tiled=True)]
+    received = list(blocks)
+    for k in sorted(range(1, partners), key=lambda k: -min(k, partners - k)):
+        pairs = [(i, (i + k) % partners) for i in range(partners)]
+        received[k] = lax.ppermute(blocks[k], "wave", pairs)
+    return received
 
 
 def per_device(
@@ -281,25 +349,27 @@
     slot_dev, row_total, lat_total = legendre.shape
     levels = to_modes.shape[0]
     parts = channels // levels
+    partners = slots // slot_dev
     my_index = lax.axis_index("wave")
     own_waves = lax.dynamic_slice_in_dim(slot_wave, my_index * slot_dev, slot_dev)
     north = jnp.transpose(north_rows, (2, 0, 1)).reshape(parts, levels, lat_dev, slots)
     south = jnp.transpose(south_rows, (2, 0, 1)).reshape(parts, levels, lat_dev, slots)
-    exchange = functools.partial(
-        lax.all_to_all, axis_name="wave", split_axis=0, concat_axis=0, tiled=True
-    )
-    columns = [exchange(pack(part, north, south)) for part in range(parts)]
+    columns = []
+    for part in range(parts):
+        before = columns[-1] if columns else []
+        blocks = pack(part, part == 0, partners, north, south, before[partners // 2 :][:1])
+        columns.append(exchange(gate(blocks, before[NEAR + 1 : partners - NEAR])))
     spec_state = None
     returned = []
     for part in range(parts):
-        spec_state, rows = spectral_step(
-            part, parts, columns[part], legendre, own_waves, lon_counts[None, :],
-            mode_rates[:, None], to_modes.T, from_modes.T, spec_state,
+        spec_state, blocks = spectral_step(
+            part, parts, part == parts - 1, partners, columns[part], legendre, own_waves,
+            lon_counts[None, :], mode_rates[:, None], to_modes.T, from_modes.T, spec_state,
         )
-        returned.append(exchange(rows))
+        returned.append(exchange(blocks))
     new_rows = None
     for part in range(parts):
-        new_rows = unpack(part, parts, levels, lat_dev, returned[part], new_rows)
+        new_rows = unpack(part, parts, levels, lat_dev, slots, returned[part], new_rows)
     new_rows = jnp.transpose(new_rows.reshape(channels, lat_dev, slots), (1, 2, 0))
     spec_state = jnp.transpose(spec_state.reshape(channels, slot_dev, row_total), (1, 2, 0))
     return (spec_state, new_rows)

time: 284 us -> 321 us (1.13)
  starting transfers between devices: 21.4 us -> 62.8 us
  waiting for transfers between devices: 173 us -> 164 us
    all_to_all x4 -> x2, waiting for transfers between devices: 173 us -> 0.01 us  [exchange(): lax.all_to_all(blocks[0], 'wave', split_axis=0, concat_axis=0, tiled=True)]
    ppermute x0 -> x30, waiting for transfers between devices: none -> 164 us  [exchange(): received[k] = lax.ppermute(blocks[k], 'wave', pairs)]
    ppermute x0 -> x30, starting transfers between devices: none -> 47 us  [exchange(): received[k] = lax.ppermute(blocks[k], 'wave', pairs)]
    all_to_all x4 -> x2, starting transfers between devices: 21.4 us -> 15.8 us  [exchange(): lax.all_to_all(blocks[0], 'wave', split_axis=0, concat_axis=0, tiled=True)]
    pallas_call x6 -> x7, Pallas kernels: 84.8 us -> 86.1 us  [the longest x2 66.2 us: spectral_step(): pl.pallas_call(functools.partial(step_body, taken=len(received), given=le...]
  transfers between devices with their start and end apart: 4 -> 32, of which waited for: 4 -> 16; matrix products, arithmetic and copies ran while one was open for 1% -> 1% of each run, Pallas kernels for 26% -> 24%
where the time goes in v5:
time: 321 us; the launch traced here: 318 us
  waiting for transfers between devices  164 us (51%)
  Pallas kernels  86.1 us (27%)
  starting transfers between devices  62.8 us (20%)
  local copies, waits for them, and re-layouts  4.17 us (1%)
    ppermute x30, waiting for transfers between devices, exchange(): received[k] = lax.ppermute(blocks[k], 'wave', pairs)  164 us
    pallas_call x2, Pallas kernels, spectral_step(): pl.pallas_call(functools.partial(step_body, taken=len(received), given=le...  66.2 us
    ppermute x30, starting transfers between devices, exchange(): received[k] = lax.ppermute(blocks[k], 'wave', pairs)  47 us
    all_to_all x2, starting transfers between devices, exchange(): lax.all_to_all(blocks[0], 'wave', split_axis=0, concat_axis=0, tiled=True)  15.8 us
    pallas_call x2, Pallas kernels, pack(): pl.pallas_call(functools.partial(pack_body, after=len(after)), grid=(pl.c...  10.5 us
    pallas_call x2, Pallas kernels, unpack(): pl.pallas_call(functools.partial(unpack_body, arrays=len(received)), grid...  9.31 us
  transfers between devices with their start and end apart: 32, of which 16 were waited for; matrix products, arithmetic and copies ran while one was open for 1% of the time, Pallas kernels for 24%

profile of v5, /device:TPU:13, one launch (start us, length us, event | category | flops | bytes accessed | tf_op | source)
XLA Modules:
  0.0 318.2 jit_solution(8879704381927957245)
XLA Ops:
  0.6 5.3 %shard_map.95 = (bf16[8,11008]{1,0:T(8,128)(2,1)}, bf16[8,11008]{1,0:T(8,128)(2,1)}, bf16[8,11008]{1,0:T(8,128)(2,1)}, bf16[8,11008]{1,0:T(8,128)(2,1)}, bf16[8,...) custom-call(bf16[2,137,80,128]{3,2,1,0:T(8,128)(2,1)} %bitcast.15, ...), custom_call_target="tpu_custom_call" | custom-call | flops 2805760 | bytes 8417280 | tf_op jit(solution)/shard_map/pallas_call | solution.py:86
  5.9 2.4 collective-permute-start
  8.3 0.0 collective-permute-start.1
  8.3 1.2 collective-permute-start.2
  9.5 2.8 collective-permute-start.3
  12.3 1.6 collective-permute-start.4
  13.9 2.6 collective-permute-done.refs_0_.refs_6_.refs_8_
  16.5 3.5 %collective-permute-start.5 = (bf16[8,11008]{1,0:T(8,128)(2,1)}, bf16[8,11008]{1,0:T(8,128)(2,1)}, u32[]{:S(2)}, u32[]{:S(2)}) collective-permute-start(bf16[8,11008]{1,0:T(8,128)(2,1)} %get-tuple-element.42), channel_id=1, source_target_pairs={{0,7},{1,8},{2,9},{3,10},{4,11},{5,12},{6,13},{7,14},{8,15},{9,0},... | collective-permute-start | bytes 528392 | tf_op jit(solution)/shard_map/ppermute | solution.py:341
  20.0 0.9 collective-permute-done.1.refs_1_.refs_3_
  20.8 13.9 %collective-permute-start.6 = (bf16[8,11008]{1,0:T(8,128)(2,1)}, bf16[8,11008]{1,0:T(8,128)(2,1)}, u32[]{:S(2)}, u32[]{:S(2)}) collective-permute-start(bf16[8,11008]{1,0:T(8,128)(2,1)} %get-tuple-element.43), channel_id=1, source_target_pairs={{0,9},{1,10},{2,11},{3,12},{4,13},{5,14},{6,15},{7,0},{8,1},{9,2},... | collective-permute-start | bytes 528392 | tf_op jit(solution)/shard_map/ppermute | solution.py:341
  34.8 0.0 collective-permute-done.2.refs_2_.refs_4_
  34.8 5.3 %collective-permute-start.7 = (bf16[8,11008]{1,0:T(8,128)(2,1)}, bf16[8,11008]{1,0:T(8,128)(2,1)}, u32[]{:S(2)}, u32[]{:S(2)}) collective-permute-start(bf16[8,11008]{1,0:T(8,128)(2,1)} %get-tuple-element.44), channel_id=1, source_target_pairs={{0,10},{1,11},{2,12},{3,13},{4,14},{5,15},{6,0},{7,1},{8,2},{9,3},... | collective-permute-start | bytes 528392 | tf_op jit(solution)/shard_map/ppermute | solution.py:341
  40.1 0.0 collective-permute-done.3.refs_3_.refs_5_
  40.1 2.5 collective-permute-start.8
  42.5 19.3 %collective-permute-done.5.refs_5_.refs_7_ = bf16[8,11008]{1,0:T(8,128)(2,1)} collective-permute-done((bf16[8,11008]{1,0:T(8,128)(2,1)}, bf16[8,11008]{1,0:T(8,128)(2,1)}, u32[]{:S(2)}, u32[]{:S(2)}) %collective-permute-start.5) | collective-permute-done | bytes 176160 | tf_op jit(solution)/shard_map/ppermute | solution.py:341
  61.8 0.0 collective-permute-start.10
  61.8 5.2 %shard_map.96.refs_0_ = bf16[16,8,11008]{2,1,0:T(8,128)(2,1)} custom-call(bf16[2,137,80,128]{3,2,1,0:T(8,128)(2,1)} %bitcast.16, bf16[2,137,80,128]{3,2,1,0:T(8,128)(2,1)} %bitcast.18, bf16[8,11008]{1,0:T(8,128)(2,1)} %copy-done), custom_call_target="tpu_custom_call" | custom-call | flops 2805760 | bytes 8417280 | tf_op jit(solution)/shard_map/pallas_call | solution.py:86
  67.0 0.0 copy-start.3
  67.1 0.0 copy-start.14
  67.1 0.0 collective-permute-done.6.refs_7_.refs_9_
  67.1 0.0 collective-permute-done.9.refs_10_.refs_12_
  67.1 0.2 collective-permute-done.10.refs_11_.refs_13_
  67.3 11.4 %all-to-all-start = ((bf16[16,8,11008]{2,1,0:T(8,128)(2,1)}), bf16[16,8,11008]{2,1,0:T(8,128)(2,1)}, u32[]{:S(2)}, u32[]{:S(2)}) async-start(bf16[16,8,11008]{2,1,0:T(8,128)(2,1)} %shard_map.97), calls=%async_computation | async-start | bytes 5636096 | tf_op jit(solution)/shard_map/all_to_all | solution.py:337
  78.7 1.5 collective-permute-start.11
  80.2 1.2 collective-permute-start.12
  81.4 0.3 collective-permute-start.13
  81.7 0.0 collective-permute-start.14
  81.7 0.6 broadcast_in_dim.8.refs_17_.refs_2_
  82.3 0.7 copy.18.refs_18_.refs_3_
  83.1 0.7 copy.15
  83.8 0.7 copy.16
  84.5 0.6 dynamic_slice.3.waves_ref
  85.2 58.0 %collective-permute-done.11.refs_1_ = bf16[8,11008]{1,0:T(8,128)(2,1)S(1)} collective-permute-done((bf16[8,11008]{1,0:T(8,128)(2,1)S(1)}, bf16[8,11008]{1,0:T(8,128)(2,1)S(1)}, u32[]{:S(2)}, u32[]{:S(2)}) %collective-permute-start.11) | collective-permute-done | bytes 176160 | tf_op jit(solution)/shard_map/ppermute | solution.py:341
  143.2 2.4 collective-permute-done.12.refs_2_
  145.6 0.0 collective-permute-done.13.refs_14_
  145.6 1.7 collective-permute-done.14.refs_15_
  147.3 0.7 copy-done.13
  147.9 33.1 %shard_map.98 = (bf16[2,137,8,1280]{3,2,1,0:T(8,128)(2,1)}, bf16[16,8,11008]{2,1,0:T(8,128)(2,1)}) custom-call(s32[8]{0:T(128)} %dynamic_slice.3.waves_ref, bf16[8,11008]{1,0:T(8,128)(2,1)} %get-tuple-element.48.refs_0_, bf16[8,11008]{1,0:T(8,128)(2,1)} %copy-done.10, bf16[8,11008]{1,0:T(8,128)(2,1)} %copy-done.11, ...), custom_call_target="tpu_custom_call" | custom-call | flops 28730982400 | bytes 34631680 | tf_op jit(solution)/shard_map/pallas_call | solution.py:303
  181.1 4.4 %all-to-all-start.1 = ((bf16[16,8,11008]{2,1,0:T(8,128)(2,1)}), bf16[16,8,11008]{2,1,0:T(8,128)(2,1)}, u32[]{:S(2)}, u32[]{:S(2)}) async-start(bf16[16,8,11008]{2,1,0:T(8,128)(2,1)} %get-tuple-element.71), calls=%async_computation.1 | async-start | bytes 5636096 | tf_op jit(solution)/shard_map/all_to_all | solution.py:337
  185.5 33.1 %shard_map.99 = (bf16[2,137,8,1280]{3,2,1,0:T(8,128)(2,1)}, bf16[8,11008]{1,0:T(8,128)(2,1)}, bf16[8,11008]{1,0:T(8,128)(2,1)}, bf16[8,11008]{1,0:T(8,128)(2,1)}...) custom-call(s32[8]{0:T(128)} %dynamic_slice.3.waves_ref, ...), custom_call_target="tpu_custom_call", output_to_operand_aliasing={{0}: (7, {})} | custom-call | flops 28730982400 | bytes 34631680 | tf_op jit(solution)/shard_map/pallas_call | solution.py:303
  218.6 1.1 collective-permute-start.15
  219.7 1.2 collective-permute-start.16
  220.8 0.4 collective-permute-start.17
  221.3 0.8 collective-permute-start.18
  222.0 2.9 collective-permute-start.19
  224.9 30.8 %collective-permute-done.15.refs_1_ = bf16[8,11008]{1,0:T(8,128)(2,1)S(1)} collective-permute-done((bf16[8,11008]{1,0:T(8,128)(2,1)}, bf16[8,11008]{1,0:T(8,128)(2,1)S(1)}, u32[]{:S(2)}, u32[]{:S(2)}) %collective-permute-start.15) | collective-permute-done | bytes 176160 | tf_op jit(solution)/shard_map/ppermute | solution.py:341
  255.7 3.8 %collective-permute-done.16.refs_2_ = bf16[8,11008]{1,0:T(8,128)(2,1)} collective-permute-done((bf16[8,11008]{1,0:T(8,128)(2,1)}, bf16[8,11008]{1,0:T(8,128)(2,1)}, u32[]{:S(2)}, u32[]{:S(2)}) %collective-permute-start.16) | collective-permute-done | bytes 176160 | tf_op jit(solution)/shard_map/ppermute | solution.py:341
  259.5 0.0 collective-permute-start.21
  259.5 11.3 %collective-permute-done.17.refs_3_ = bf16[8,11008]{1,0:T(8,128)(2,1)} collective-permute-done((bf16[8,11008]{1,0:T(8,128)(2,1)}, bf16[8,11008]{1,0:T(8,128)(2,1)}, u32[]{:S(2)}, u32[]{:S(2)}) %collective-permute-start.17) | collective-permute-done | bytes 176160 | tf_op jit(solution)/shard_map/ppermute | solution.py:341
  270.8 3.8 %collective-permute-done.18.refs_4_ = bf16[8,11008]{1,0:T(8,128)(2,1)} collective-permute-done((bf16[8,11008]{1,0:T(8,128)(2,1)}, bf16[8,11008]{1,0:T(8,128)(2,1)}, u32[]{:S(2)}, u32[]{:S(2)}) %collective-permute-start.18) | collective-permute-done | bytes 176160 | tf_op jit(solution)/shard_map/ppermute | solution.py:341
  274.6 13.1 %collective-permute-done.19.refs_5_ = bf16[8,11008]{1,0:T(8,128)(2,1)} collective-permute-done((bf16[8,11008]{1,0:T(8,128)(2,1)}, bf16[8,11008]{1,0:T(8,128)(2,1)}, u32[]{:S(2)}, u32[]{:S(2)}) %collective-permute-start.19) | collective-permute-done | bytes 176160 | tf_op jit(solution)/shard_map/ppermute | solution.py:341
  287.7 0.0 collective-permute-start.24
  287.7 3.9 %collective-permute-done.20.refs_6_ = bf16[8,11008]{1,0:T(8,128)(2,1)} collective-permute-done((bf16[8,11008]{1,0:T(8,128)(2,1)}, bf16[8,11008]{1,0:T(8,128)(2,1)}, u32[]{:S(2)}, u32[]{:S(2)}) %collective-permute-start.20) | collective-permute-done | bytes 176160 | tf_op jit(solution)/shard_map/ppermute | solution.py:341
  291.6 2.0 collective-permute-start.25
  293.6 3.7 %collective-permute-done.21.refs_7_ = bf16[8,11008]{1,0:T(8,128)(2,1)} collective-permute-done((bf16[8,11008]{1,0:T(8,128)(2,1)}, bf16[8,11008]{1,0:T(8,128)(2,1)}, u32[]{:S(2)}, u32[]{:S(2)}) %collective-permute-start.21) | collective-permute-done | bytes 176160 | tf_op jit(solution)/shard_map/ppermute | solution.py:341
  297.2 5.7 %collective-permute-done.22.refs_8_ = bf16[8,11008]{1,0:T(8,128)(2,1)} collective-permute-done((bf16[8,11008]{1,0:T(8,128)(2,1)}, bf16[8,11008]{1,0:T(8,128)(2,1)}, u32[]{:S(2)}, u32[]{:S(2)}) %collective-permute-start.22) | collective-permute-done | bytes 176160 | tf_op jit(solution)/shard_map/ppermute | solution.py:341
  302.9 0.0 collective-permute-start.27
  302.9 0.0 collective-permute-done.23.refs_9_
  302.9 0.4 collective-permute-start.28
  303.3 2.3 collective-permute-start.29
  305.5 0.0 all-to-all-done.1.refs_0_
  305.5 4.5 %shard_map.100.refs_16_ = bf16[2,137,80,128]{3,2,1,0:T(8,128)(2,1)} custom-call(bf16[16,8,11008]{2,1,0:T(8,128)(2,1)} %all-to-all-done.1.refs_0_), custom_call_target="tpu_custom_call" | custom-call | flops 1402880 | bytes 5611520 | tf_op jit(solution)/shard_map/pallas_call | solution.py:123
  310.1 3.3 %collective-permute-done.29.refs_15_ = bf16[8,11008]{1,0:T(8,128)(2,1)} collective-permute-done((bf16[8,11008]{1,0:T(8,128)(2,1)}, bf16[8,11008]{1,0:T(8,128)(2,1)}, u32[]{:S(2)}, u32[]{:S(2)}) %collective-permute-start.29) | collective-permute-done | bytes 176160 | tf_op jit(solution)/shard_map/ppermute | solution.py:341
  313.4 4.8 %shard_map.101 = bf16[2,137,80,128]{3,2,1,0:T(8,128)(2,1)} custom-call(bf16[8,11008]{1,0:T(8,128)(2,1)} %get-tuple-element.55.refs_0_, bf16[8,11008]{1,0:T(8,128)(2,1)} %copy-done.1, bf16[8,11008]{1,0:T(8,128)(2,1)} %collective-permute-done.16.refs_2_, bf16[8,11008]{1,0:T(8,128)(2,1)} %collective-permute-done.17.refs_3_, ...), custom_call_target="tpu_custom_call", output_to_operand_aliasing={{}: (16, {})} | custom-call | flops 1402880 | bytes 5611520 | tf_op jit(solution)/shard_map/pallas_call | solution.py:123
  (42 shorter events, 0.1 us)
Async XLA Ops:
  5.9 10.6 %collective-permute-start = (bf16[8,11008]{1,0:T(8,128)(2,1)}, bf16[8,11008]{1,0:T(8,128)(2,1)S(1)}, u32[]{:S(2)}, u32[]{:S(2)}) collective-permute-start(bf16[8,11008]{1,0:T(8,128)(2,1)} %get-tuple-element.37), channel_id=1, source_target_pairs={{0,8},{1,9},{2,10},{3,11},{4,12},{5,13},{6,14},{7,15},{8,0},{9,1},... | collective-permute-start | bytes 528392 | tf_op jit(solution)/shard_map/ppermute | solution.py:341
  8.3 12.5 %collective-permute-start.1 = (bf16[8,11008]{1,0:T(8,128)(2,1)}, bf16[8,11008]{1,0:T(8,128)(2,1)}, u32[]{:S(2)}, u32[]{:S(2)}) collective-permute-start(bf16[8,11008]{1,0:T(8,128)(2,1)} %get-tuple-element.38), channel_id=1, source_target_pairs={{0,3},{1,4},{2,5},{3,6},{4,7},{5,8},{6,9},{7,10},{8,11},{9,12},{10... | collective-permute-start | bytes 528392 | tf_op jit(solution)/shard_map/ppermute | solution.py:341
  8.3 26.4 %collective-permute-start.2 = (bf16[8,11008]{1,0:T(8,128)(2,1)}, bf16[8,11008]{1,0:T(8,128)(2,1)}, u32[]{:S(2)}, u32[]{:S(2)}) collective-permute-start(bf16[8,11008]{1,0:T(8,128)(2,1)} %get-tuple-element.39), channel_id=1, source_target_pairs={{0,4},{1,5},{2,6},{3,7},{4,8},{5,9},{6,10},{7,11},{8,12},{9,13},{1... | collective-permute-start | bytes 528392 | tf_op jit(solution)/shard_map/ppermute | solution.py:341
  9.5 30.6 %collective-permute-start.3 = (bf16[8,11008]{1,0:T(8,128)(2,1)}, bf16[8,11008]{1,0:T(8,128)(2,1)}, u32[]{:S(2)}, u32[]{:S(2)}) collective-permute-start(bf16[8,11008]{1,0:T(8,128)(2,1)} %get-tuple-element.40), channel_id=1, source_target_pairs={{0,5},{1,6},{2,7},{3,8},{4,9},{5,10},{6,11},{7,12},{8,13},{9,14},{... | collective-permute-start | bytes 528392 | tf_op jit(solution)/shard_map/ppermute | solution.py:341
  12.3 30.2 %collective-permute-start.4 = (bf16[8,11008]{1,0:T(8,128)(2,1)}, bf16[8,11008]{1,0:T(8,128)(2,1)}, u32[]{:S(2)}, u32[]{:S(2)}) collective-permute-start(bf16[8,11008]{1,0:T(8,128)(2,1)} %get-tuple-element.41), channel_id=1, source_target_pairs={{0,6},{1,7},{2,8},{3,9},{4,10},{5,11},{6,12},{7,13},{8,14},{9,15},... | collective-permute-start | bytes 528392 | tf_op jit(solution)/shard_map/ppermute | solution.py:341
  16.5 45.3 %copy-start = (bf16[8,11008]{1,0:T(8,128)(2,1)}, bf16[8,11008]{1,0:T(8,128)(2,1)S(1)}, u32[]{:S(2)}) copy-start(bf16[8,11008]{1,0:T(8,128)(2,1)S(1)} %collective-permute-done.refs_0_.refs_6_.refs_8_) | copy-start | bytes 528388
  16.5 45.3 %collective-permute-start.5 = (bf16[8,11008]{1,0:T(8,128)(2,1)}, bf16[8,11008]{1,0:T(8,128)(2,1)}, u32[]{:S(2)}, u32[]{:S(2)}) collective-permute-start(bf16[8,11008]{1,0:T(8,128)(2,1)} %get-tuple-element.42), channel_id=1, source_target_pairs={{0,7},{1,8},{2,9},{3,10},{4,11},{5,12},{6,13},{7,14},{8,15},{9,0},... | collective-permute-start | bytes 528392 | tf_op jit(solution)/shard_map/ppermute | solution.py:341
  20.8 46.2 %collective-permute-start.6 = (bf16[8,11008]{1,0:T(8,128)(2,1)}, bf16[8,11008]{1,0:T(8,128)(2,1)}, u32[]{:S(2)}, u32[]{:S(2)}) collective-permute-start(bf16[8,11008]{1,0:T(8,128)(2,1)} %get-tuple-element.43), channel_id=1, source_target_pairs={{0,9},{1,10},{2,11},{3,12},{4,13},{5,14},{6,15},{7,0},{8,1},{9,2},... | collective-permute-start | bytes 528392 | tf_op jit(solution)/shard_map/ppermute | solution.py:341
  34.8 32.3 %collective-permute-start.7 = (bf16[8,11008]{1,0:T(8,128)(2,1)}, bf16[8,11008]{1,0:T(8,128)(2,1)}, u32[]{:S(2)}, u32[]{:S(2)}) collective-permute-start(bf16[8,11008]{1,0:T(8,128)(2,1)} %get-tuple-element.44), channel_id=1, source_target_pairs={{0,10},{1,11},{2,12},{3,13},{4,14},{5,15},{6,0},{7,1},{8,2},{9,3},... | collective-permute-start | bytes 528392 | tf_op jit(solution)/shard_map/ppermute | solution.py:341
  40.1 27.0 %collective-permute-start.8 = (bf16[8,11008]{1,0:T(8,128)(2,1)}, bf16[8,11008]{1,0:T(8,128)(2,1)}, u32[]{:S(2)}, u32[]{:S(2)}) collective-permute-start(bf16[8,11008]{1,0:T(8,128)(2,1)} %get-tuple-element.45), channel_id=1, source_target_pairs={{0,11},{1,12},{2,13},{3,14},{4,15},{5,0},{6,1},{7,2},{8,3},{9,4},{... | collective-permute-start | bytes 528392 | tf_op jit(solution)/shard_map/ppermute | solution.py:341
  42.5 24.6 %collective-permute-start.9 = (bf16[8,11008]{1,0:T(8,128)(2,1)}, bf16[8,11008]{1,0:T(8,128)(2,1)}, u32[]{:S(2)}, u32[]{:S(2)}) collective-permute-start(bf16[8,11008]{1,0:T(8,128)(2,1)} %get-tuple-element.46), channel_id=1, source_target_pairs={{0,12},{1,13},{2,14},{3,15},{4,0},{5,1},{6,2},{7,3},{8,4},{9,5},{1... | collective-permute-start | bytes 528392 | tf_op jit(solution)/shard_map/ppermute | solution.py:341
  61.8 5.5 %collective-permute-start.10 = (bf16[8,11008]{1,0:T(8,128)(2,1)}, bf16[8,11008]{1,0:T(8,128)(2,1)}, u32[]{:S(2)}, u32[]{:S(2)}) collective-permute-start(bf16[8,11008]{1,0:T(8,128)(2,1)} %get-tuple-element.47), channel_id=1, source_target_pairs={{0,13},{1,14},{2,15},{3,0},{4,1},{5,2},{6,3},{7,4},{8,5},{9,6},{10... | collective-permute-start | bytes 528392 | tf_op jit(solution)/shard_map/ppermute | solution.py:341
  67.0 14.7 %copy-start.4 = (s32[1280]{0:T(1024)S(1)}, s32[1280]{0:T(1024)}, u32[]{:S(2)}) copy-start(s32[1280]{0:T(1024)} %param.10) | copy-start | bytes 15364
  67.0 15.3 %copy-start.5 = (f32[137]{0:T(256)S(1)}, f32[137]{0:T(256)}, u32[]{:S(2)}) copy-start(f32[137]{0:T(256)} %param.13) | copy-start | bytes 1648
  67.0 16.0 %copy-start.2 = (bf16[137,137]{1,0:T(8,128)(2,1)S(1)}, bf16[137,137]{1,0:T(8,128)(2,1)}, u32[]{:S(2)}) copy-start(bf16[137,137]{1,0:T(8,128)(2,1)} %param.14) | copy-start | bytes 112618
  67.0 16.8 %copy-start.3 = (bf16[137,137]{1,0:T(8,128)(2,1)S(1)}, bf16[137,137]{1,0:T(8,128)(2,1)}, u32[]{:S(2)}) copy-start(bf16[137,137]{1,0:T(8,128)(2,1)} %param.15) | copy-start | bytes 112618
  67.1 17.5 %copy-start.14 = (s32[128]{0:T(128)S(1)}, s32[128]{0:T(128)}, u32[]{:S(2)}) copy-start(s32[128]{0:T(128)} %param.11) | copy-start | bytes 1540
  67.3 11.5 %copy-start.9 = (bf16[8,11008]{1,0:T(8,128)(2,1)S(1)}, bf16[8,11008]{1,0:T(8,128)(2,1)}, u32[]{:S(2)}) copy-start(bf16[8,11008]{1,0:T(8,128)(2,1)} %get-tuple-element.49) | copy-start | bytes 528388
  67.3 12.9 %copy-start.8 = (bf16[8,11008]{1,0:T(8,128)(2,1)S(1)}, bf16[8,11008]{1,0:T(8,128)(2,1)}, u32[]{:S(2)}) copy-start(bf16[8,11008]{1,0:T(8,128)(2,1)} %get-tuple-element.50) | copy-start | bytes 528388
  67.3 14.1 %copy-start.7 = (bf16[8,11008]{1,0:T(8,128)(2,1)S(1)}, bf16[8,11008]{1,0:T(8,128)(2,1)}, u32[]{:S(2)}) copy-start(bf16[8,11008]{1,0:T(8,128)(2,1)} %get-tuple-element.51) | copy-start | bytes 528388
  67.3 14.4 %copy-start.6 = (bf16[8,11008]{1,0:T(8,128)(2,1)S(1)}, bf16[8,11008]{1,0:T(8,128)(2,1)}, u32[]{:S(2)}) copy-start(bf16[8,11008]{1,0:T(8,128)(2,1)} %get-tuple-element.52) | copy-start | bytes 528388
  67.3 113.8 %all-to-all-start = ((bf16[16,8,11008]{2,1,0:T(8,128)(2,1)}), bf16[16,8,11008]{2,1,0:T(8,128)(2,1)}, u32[]{:S(2)}, u32[]{:S(2)}) async-start(bf16[16,8,11008]{2,1,0:T(8,128)(2,1)} %shard_map.97), calls=%async_computation | async-start | bytes 5636096 | tf_op jit(solution)/shard_map/all_to_all | solution.py:337
  78.7 64.4 %collective-permute-start.11 = (bf16[8,11008]{1,0:T(8,128)(2,1)S(1)}, bf16[8,11008]{1,0:T(8,128)(2,1)S(1)}, u32[]{:S(2)}, u32[]{:S(2)}) collective-permute-start(bf16[8,11008]{1,0:T(8,128)(2,1)S(1)} %copy-done.9), channel_id=1, source_target_pairs={{0,1},{1,2},{2,3},{3,4},{4,5},{5,6},{6,7},{7,8},{8,9},{9,10},{10,1... | collective-permute-start | bytes 528392 | tf_op jit(solution)/shard_map/ppermute | solution.py:341
  80.2 65.3 %collective-permute-start.12 = (bf16[8,11008]{1,0:T(8,128)(2,1)S(1)}, bf16[8,11008]{1,0:T(8,128)(2,1)S(1)}, u32[]{:S(2)}, u32[]{:S(2)}) collective-permute-start(bf16[8,11008]{1,0:T(8,128)(2,1)S(1)} %copy-done.8), channel_id=1, source_target_pairs={{0,2},{1,3},{2,4},{3,5},{4,6},{5,7},{6,8},{7,9},{8,10},{9,11},{10,... | collective-permute-start | bytes 528392 | tf_op jit(solution)/shard_map/ppermute | solution.py:341
  81.4 64.1 %collective-permute-start.13 = (bf16[8,11008]{1,0:T(8,128)(2,1)S(1)}, bf16[8,11008]{1,0:T(8,128)(2,1)S(1)}, u32[]{:S(2)}, u32[]{:S(2)}) collective-permute-start(bf16[8,11008]{1,0:T(8,128)(2,1)S(1)} %copy-done.7), channel_id=1, source_target_pairs={{0,14},{1,15},{2,0},{3,1},{4,2},{5,3},{6,4},{7,5},{8,6},{9,7},{10,... | collective-permute-start | bytes 528392 | tf_op jit(solution)/shard_map/ppermute | solution.py:341
  81.7 65.6 %collective-permute-start.14 = (bf16[8,11008]{1,0:T(8,128)(2,1)S(1)}, bf16[8,11008]{1,0:T(8,128)(2,1)S(1)}, u32[]{:S(2)}, u32[]{:S(2)}) collective-permute-start(bf16[8,11008]{1,0:T(8,128)(2,1)S(1)} %copy-done.6), channel_id=1, source_target_pairs={{0,15},{1,0},{2,1},{3,2},{4,3},{5,4},{6,5},{7,6},{8,7},{9,8},{10,9... | collective-permute-start | bytes 528392 | tf_op jit(solution)/shard_map/ppermute | solution.py:341
  143.2 4.1 %copy-start.10 = (bf16[8,11008]{1,0:T(8,128)(2,1)}, bf16[8,11008]{1,0:T(8,128)(2,1)S(1)}, u32[]{:S(2)}) copy-start(bf16[8,11008]{1,0:T(8,128)(2,1)S(1)} %collective-permute-done.11.refs_1_) | copy-start | bytes 528388
  145.6 1.7 copy-start.11
  145.6 1.7 copy-start.12
  147.3 0.7 copy-start.13
  181.1 124.5 %all-to-all-start.1 = ((bf16[16,8,11008]{2,1,0:T(8,128)(2,1)}), bf16[16,8,11008]{2,1,0:T(8,128)(2,1)}, u32[]{:S(2)}, u32[]{:S(2)}) async-start(bf16[16,8,11008]{2,1,0:T(8,128)(2,1)} %get-tuple-element.71), calls=%async_computation.1 | async-start | bytes 5636096 | tf_op jit(solution)/shard_map/all_to_all | solution.py:337
  218.6 37.1 %collective-permute-start.15 = (bf16[8,11008]{1,0:T(8,128)(2,1)}, bf16[8,11008]{1,0:T(8,128)(2,1)S(1)}, u32[]{:S(2)}, u32[]{:S(2)}) collective-permute-start(bf16[8,11008]{1,0:T(8,128)(2,1)} %get-tuple-element.56), channel_id=1, source_target_pairs={{0,1},{1,2},{2,3},{3,4},{4,5},{5,6},{6,7},{7,8},{8,9},{9,10},{10,1... | collective-permute-start | bytes 528392 | tf_op jit(solution)/shard_map/ppermute | solution.py:341
  219.7 39.8 %collective-permute-start.16 = (bf16[8,11008]{1,0:T(8,128)(2,1)}, bf16[8,11008]{1,0:T(8,128)(2,1)}, u32[]{:S(2)}, u32[]{:S(2)}) collective-permute-start(bf16[8,11008]{1,0:T(8,128)(2,1)} %get-tuple-element.57), channel_id=1, source_target_pairs={{0,2},{1,3},{2,4},{3,5},{4,6},{5,7},{6,8},{7,9},{8,10},{9,11},{10,... | collective-permute-start | bytes 528392 | tf_op jit(solution)/shard_map/ppermute | solution.py:341
  220.8 50.0 %collective-permute-start.17 = (bf16[8,11008]{1,0:T(8,128)(2,1)}, bf16[8,11008]{1,0:T(8,128)(2,1)}, u32[]{:S(2)}, u32[]{:S(2)}) collective-permute-start(bf16[8,11008]{1,0:T(8,128)(2,1)} %get-tuple-element.58), channel_id=1, source_target_pairs={{0,3},{1,4},{2,5},{3,6},{4,7},{5,8},{6,9},{7,10},{8,11},{9,12},{10... | collective-permute-start | bytes 528392 | tf_op jit(solution)/shard_map/ppermute | solution.py:341
  221.3 53.3 %collective-permute-start.18 = (bf16[8,11008]{1,0:T(8,128)(2,1)}, bf16[8,11008]{1,0:T(8,128)(2,1)}, u32[]{:S(2)}, u32[]{:S(2)}) collective-permute-start(bf16[8,11008]{1,0:T(8,128)(2,1)} %get-tuple-element.59), channel_id=1, source_target_pairs={{0,4},{1,5},{2,6},{3,7},{4,8},{5,9},{6,10},{7,11},{8,12},{9,13},{1... | collective-permute-start | bytes 528392 | tf_op jit(solution)/shard_map/ppermute | solution.py:341
  222.0 65.6 %collective-permute-start.19 = (bf16[8,11008]{1,0:T(8,128)(2,1)}, bf16[8,11008]{1,0:T(8,128)(2,1)}, u32[]{:S(2)}, u32[]{:S(2)}) collective-permute-start(bf16[8,11008]{1,0:T(8,128)(2,1)} %get-tuple-element.60), channel_id=1, source_target_pairs={{0,5},{1,6},{2,7},{3,8},{4,9},{5,10},{6,11},{7,12},{8,13},{9,14},{... | collective-permute-start | bytes 528392 | tf_op jit(solution)/shard_map/ppermute | solution.py:341
  255.7 57.7 %copy-start.1 = (bf16[8,11008]{1,0:T(8,128)(2,1)}, bf16[8,11008]{1,0:T(8,128)(2,1)S(1)}, u32[]{:S(2)}) copy-start(bf16[8,11008]{1,0:T(8,128)(2,1)S(1)} %collective-permute-done.15.refs_1_) | copy-start | bytes 528388
  255.7 35.9 %collective-permute-start.20 = (bf16[8,11008]{1,0:T(8,128)(2,1)}, bf16[8,11008]{1,0:T(8,128)(2,1)}, u32[]{:S(2)}, u32[]{:S(2)}) collective-permute-start(bf16[8,11008]{1,0:T(8,128)(2,1)} %get-tuple-element.61), channel_id=1, source_target_pairs={{0,6},{1,7},{2,8},{3,9},{4,10},{5,11},{6,12},{7,13},{8,14},{9,15},... | collective-permute-start | bytes 528392 | tf_op jit(solution)/shard_map/ppermute | solution.py:341
  259.5 37.7 %collective-permute-start.21 = (bf16[8,11008]{1,0:T(8,128)(2,1)}, bf16[8,11008]{1,0:T(8,128)(2,1)}, u32[]{:S(2)}, u32[]{:S(2)}) collective-permute-start(bf16[8,11008]{1,0:T(8,128)(2,1)} %get-tuple-element.62), channel_id=1, source_target_pairs={{0,7},{1,8},{2,9},{3,10},{4,11},{5,12},{6,13},{7,14},{8,15},{9,0},... | collective-permute-start | bytes 528392 | tf_op jit(solution)/shard_map/ppermute | solution.py:341
  270.8 32.1 %collective-permute-start.22 = (bf16[8,11008]{1,0:T(8,128)(2,1)}, bf16[8,11008]{1,0:T(8,128)(2,1)}, u32[]{:S(2)}, u32[]{:S(2)}) collective-permute-start(bf16[8,11008]{1,0:T(8,128)(2,1)} %get-tuple-element.63), channel_id=1, source_target_pairs={{0,8},{1,9},{2,10},{3,11},{4,12},{5,13},{6,14},{7,15},{8,0},{9,1},... | collective-permute-start | bytes 528392 | tf_op jit(solution)/shard_map/ppermute | solution.py:341
  274.6 28.3 %collective-permute-start.23 = (bf16[8,11008]{1,0:T(8,128)(2,1)}, bf16[8,11008]{1,0:T(8,128)(2,1)}, u32[]{:S(2)}, u32[]{:S(2)}) collective-permute-start(bf16[8,11008]{1,0:T(8,128)(2,1)} %get-tuple-element.64), channel_id=1, source_target_pairs={{0,9},{1,10},{2,11},{3,12},{4,13},{5,14},{6,15},{7,0},{8,1},{9,2},... | collective-permute-start | bytes 528392 | tf_op jit(solution)/shard_map/ppermute | solution.py:341
  287.7 15.6 %collective-permute-start.24 = (bf16[8,11008]{1,0:T(8,128)(2,1)}, bf16[8,11008]{1,0:T(8,128)(2,1)}, u32[]{:S(2)}, u32[]{:S(2)}) collective-permute-start(bf16[8,11008]{1,0:T(8,128)(2,1)} %get-tuple-element.65), channel_id=1, source_target_pairs={{0,10},{1,11},{2,12},{3,13},{4,14},{5,15},{6,0},{7,1},{8,2},{9,3},... | collective-permute-start | bytes 528392 | tf_op jit(solution)/shard_map/ppermute | solution.py:341
  291.6 18.5 %collective-permute-start.25 = (bf16[8,11008]{1,0:T(8,128)(2,1)}, bf16[8,11008]{1,0:T(8,128)(2,1)}, u32[]{:S(2)}, u32[]{:S(2)}) collective-permute-start(bf16[8,11008]{1,0:T(8,128)(2,1)} %get-tuple-element.66), channel_id=1, source_target_pairs={{0,11},{1,12},{2,13},{3,14},{4,15},{5,0},{6,1},{7,2},{8,3},{9,4},{... | collective-permute-start | bytes 528392 | tf_op jit(solution)/shard_map/ppermute | solution.py:341
  297.2 12.8 %collective-permute-start.26 = (bf16[8,11008]{1,0:T(8,128)(2,1)}, bf16[8,11008]{1,0:T(8,128)(2,1)}, u32[]{:S(2)}, u32[]{:S(2)}) collective-permute-start(bf16[8,11008]{1,0:T(8,128)(2,1)} %get-tuple-element.67), channel_id=1, source_target_pairs={{0,12},{1,13},{2,14},{3,15},{4,0},{5,1},{6,2},{7,3},{8,4},{9,5},{1... | collective-permute-start | bytes 528392 | tf_op jit(solution)/shard_map/ppermute | solution.py:341
  302.9 7.2 %collective-permute-start.27 = (bf16[8,11008]{1,0:T(8,128)(2,1)}, bf16[8,11008]{1,0:T(8,128)(2,1)}, u32[]{:S(2)}, u32[]{:S(2)}) collective-permute-start(bf16[8,11008]{1,0:T(8,128)(2,1)} %get-tuple-element.68), channel_id=1, source_target_pairs={{0,13},{1,14},{2,15},{3,0},{4,1},{5,2},{6,3},{7,4},{8,5},{9,6},{10... | collective-permute-start | bytes 528392 | tf_op jit(solution)/shard_map/ppermute | solution.py:341
  302.9 7.2 %collective-permute-start.28 = (bf16[8,11008]{1,0:T(8,128)(2,1)}, bf16[8,11008]{1,0:T(8,128)(2,1)}, u32[]{:S(2)}, u32[]{:S(2)}) collective-permute-start(bf16[8,11008]{1,0:T(8,128)(2,1)} %get-tuple-element.69), channel_id=1, source_target_pairs={{0,14},{1,15},{2,0},{3,1},{4,2},{5,3},{6,4},{7,5},{8,6},{9,7},{10,... | collective-permute-start | bytes 528392 | tf_op jit(solution)/shard_map/ppermute | solution.py:341
  303.3 10.1 %collective-permute-start.29 = (bf16[8,11008]{1,0:T(8,128)(2,1)}, bf16[8,11008]{1,0:T(8,128)(2,1)}, u32[]{:S(2)}, u32[]{:S(2)}) collective-permute-start(bf16[8,11008]{1,0:T(8,128)(2,1)} %get-tuple-element.70), channel_id=1, source_target_pairs={{0,15},{1,0},{2,1},{3,2},{4,3},{5,4},{6,5},{7,6},{8,7},{9,8},{10,9... | collective-permute-start | bytes 528392 | tf_op jit(solution)/shard_map/ppermute | solution.py:341

commit v6 on v5

--- a/solution.py
+++ b/solution.py
@@ -12,7 +12,7 @@
 VMEM_BYTES = 255 * 256 * 1024
 GROUP = 48
 LANES = 128
-NEAR = 2
+EARLY = 5
 
 
 def flat_rows(value):
@@ -42,6 +42,10 @@
         out_refs[k][...] = blocks_ref[lax.rem(my_index + k, partners)]
 
 
+def like(blocks):
+    return [jax.ShapeDtypeStruct(block.shape, block.dtype) for block in blocks]
+
+
 def gate(blocks, after):
     if not after:
         return blocks
@@ -50,7 +54,7 @@
         lambda *refs: None,
         in_specs=[anywhere] * (len(blocks) + len(after)),
         out_specs=[anywhere] * len(blocks),
-        out_shape=[jax.ShapeDtypeStruct(block.shape, block.dtype) for block in blocks],
+        out_shape=like(blocks),
         input_output_aliases={i: i for i in range(len(blocks))},
         compiler_params=pltpu.CompilerParams(vmem_limit_bytes=VMEM_BYTES),
     )(*blocks, *after)
@@ -68,8 +72,8 @@
     return [pl.BlockSpec((partners, slot_dev, lanes), lambda i: (0, 0, i))]
 
 
-def pack_body(north_ref, south_ref, *refs, after):
-    out_refs, blocks_ref = refs[after:-1], refs[-1]
+def pack_body(north_ref, south_ref, *refs):
+    out_refs, blocks_ref = refs[:-1], refs[-1]
     partners, slot_dev, _ = blocks_ref.shape
     summed = north_ref[0].astype(jnp.float32) + south_ref[0].astype(jnp.float32)
     columns = flat_rows(summed.astype(jnp.bfloat16)).T
@@ -78,15 +82,15 @@
     give_blocks(blocks_ref, out_refs)
 
 
-def pack(part, ring, partners, north, south, after):
+def pack(part, ring, partners, north, south):
     _, levels, lat_dev, slots = north.shape
     slot_dev = slots // partners
     width = pl.cdiv(levels * lat_dev, LANES) * LANES
     rows = pl.BlockSpec((1, GROUP, lat_dev, slots), lambda i: (part, i, 0, 0))
     return pl.pallas_call(
-        functools.partial(pack_body, after=len(after)),
+        pack_body,
         grid=(pl.cdiv(levels, GROUP),),
-        in_specs=[rows, rows] + [pl.BlockSpec(memory_space=pl.ANY)] * len(after),
+        in_specs=[rows, rows],
         out_specs=block_specs(ring, partners, slot_dev, GROUP * lat_dev),
         out_shape=block_shapes(ring, partners, slot_dev, width),
         scratch_shapes=[pltpu.VMEM((partners, slot_dev, GROUP * lat_dev), jnp.bfloat16)],
@@ -96,11 +100,11 @@
             bytes_accessed=6 * levels * lat_dev * slots,
             transcendentals=0,
         ),
-    )(north, south, *after)
-
-
-def unpack_body(*refs, arrays):
-    out_ref, blocks_ref = refs[-2:]
+    )(north, south)
+
+
+def unpack_body(*refs, arrays, passed):
+    out_ref, blocks_ref = refs[-2 - passed], refs[-1]
     _, group, lat_dev, slots = out_ref.shape
     taken_ref = take_blocks(refs[:arrays], blocks_ref)
     blocks = [taken_ref[device].astype(jnp.float32) for device in range(blocks_ref.shape[0])]
@@ -110,7 +114,7 @@
     out_ref[0] = rows.reshape(group, lat_dev, slots).astype(jnp.bfloat16)
 
 
-def unpack(part, parts, levels, lat_dev, slots, received, earlier):
+def unpack(part, parts, levels, lat_dev, slots, received, earlier, waiting):
     slot_dev = received[0].shape[-2]
     partners = slots // slot_dev
     in_specs = block_specs(len(received) > 1, partners, slot_dev, GROUP * lat_dev)
@@ -120,12 +124,21 @@
         in_specs.append(pl.BlockSpec(memory_space=pl.ANY))
         aliases = {len(operands): 0}
         operands.append(earlier)
-    return pl.pallas_call(
-        functools.partial(unpack_body, arrays=len(received)),
+    anywhere = pl.BlockSpec(memory_space=pl.ANY)
+    for i, block in enumerate(waiting):
+        aliases[len(operands)] = 1 + i
+        operands.append(block)
+        in_specs.append(anywhere)
+    rows, *waiting = pl.pallas_call(
+        functools.partial(unpack_body, arrays=len(received), passed=len(waiting)),
         grid=(pl.cdiv(levels, GROUP),),
         in_specs=in_specs,
-        out_specs=pl.BlockSpec((1, GROUP, lat_dev, slots), lambda i: (part, i, 0, 0)),
-        out_shape=jax.ShapeDtypeStruct((parts, levels, lat_dev, slots), jnp.bfloat16),
+        out_specs=[pl.BlockSpec((1, GROUP, lat_dev, slots), lambda i: (part, i, 0, 0))]
+        + [anywhere] * len(waiting),
+        out_shape=[
+            jax.ShapeDtypeStruct((parts, levels, lat_dev, slots), jnp.bfloat16),
+            *like(waiting),
+        ],
         scratch_shapes=[pltpu.VMEM((partners, slot_dev, GROUP * lat_dev), jnp.bfloat16)],
         input_output_aliases=aliases,
         compiler_params=pltpu.CompilerParams(vmem_limit_bytes=VMEM_BYTES),
@@ -135,6 +148,7 @@
             transcendentals=0,
         ),
     )(*operands)
+    return rows, waiting
 
 
 def lane_runs(lanes, source):
@@ -228,11 +242,11 @@
         body(full * group, levels % group)
 
 
-def step_body(waves_ref, *refs, taken, given):
+def step_body(waves_ref, *refs, taken, given, passed):
     recv_refs, refs = refs[:taken], refs[taken:]
     legendre_ref, counts_ref, rates_ref, to_ref, from_ref = refs[:5]
     rows_ref, spec_ref, blocks_ref = refs[-3:]
-    state_ref, *send_refs = refs[-4 - given : -3]
+    state_ref, *send_refs = refs[len(refs) - 4 - given - passed :][: 1 + given]
     slot = pl.program_id(0)
     wave = waves_ref[slot]
     row_total, lat_total = legendre_ref.shape[1:]
@@ -281,7 +295,9 @@
             state_ref[0, c] = join_tiles(spec_ref, pl.ds(at, slot_dev)).astype(jnp.bfloat16)
 
 
-def spectral_step(part, parts, ring, partners, received, legendre, own_waves, counts, rates, to_t, from_t, earlier):
+def spectral_step(
+    part, parts, ring, partners, received, legendre, own_waves, counts, rates, to_t, from_t, earlier, waiting
+):
     width = received[0].shape[-1]
     slot_dev, row_total, lat_total = legendre.shape
     levels = to_t.shape[0]
@@ -300,8 +316,13 @@
         aliases[len(operands)] = 0
         operands.append(earlier)
         in_specs.append(pl.BlockSpec(memory_space=pl.ANY))
+    anywhere = pl.BlockSpec(memory_space=pl.ANY)
+    for i, block in enumerate(waiting):
+        aliases[len(operands)] = 1 + len(shapes) + i
+        operands.append(block)
+        in_specs.append(anywhere)
     state, *blocks = pl.pallas_call(
-        functools.partial(step_body, taken=len(received), given=len(shapes)),
+        functools.partial(step_body, taken=len(received), given=len(shapes), passed=len(waiting)),
         grid_spec=pltpu.PrefetchScalarGridSpec(
             num_scalar_prefetch=1,
             grid=(slot_dev,),
@@ -309,7 +330,8 @@
             out_specs=[
                 pl.BlockSpec((1, levels, slot_dev, row_total), lambda s, waves: (part, 0, 0, 0)),
             ]
-            + [whole(shape.shape) for shape in shapes],
+            + [whole(shape.shape) for shape in shapes]
+            + [anywhere] * len(waiting),
             scratch_shapes=[
                 pltpu.VMEM((lat_total // LANES, levels * slot_dev, LANES), jnp.float32),
                 pltpu.VMEM((row_total // LANES, levels * slot_dev, LANES), jnp.float32),
@@ -319,6 +341,7 @@
         out_shape=[
             jax.ShapeDtypeStruct((parts, levels, slot_dev, row_total), jnp.bfloat16),
             *shapes,
+            *like(waiting),
         ],
         input_output_aliases=aliases,
         compiler_params=pltpu.CompilerParams(vmem_limit_bytes=VMEM_BYTES),
@@ -328,7 +351,11 @@
             transcendentals=0,
         ),
     )(*operands)
-    return state, blocks
+    return state, blocks[: len(shapes)], blocks[len(shapes) :]
+
+
+def far_first(partners):
+    return sorted(range(1, partners), key=lambda k: -min(k, partners - k))
 
 
 def exchange(blocks):
@@ -336,7 +363,7 @@
     if partners == 1:
         return [lax.all_to_all(blocks[0], "wave", split_axis=0, concat_axis=0, tiled=True)]
     received = list(blocks)
-    for k in sorted(range(1, partners), key=lambda k: -min(k, partners - k)):
+    for k in far_first(partners):
         pairs = [(i, (i + k) % partners) for i in range(partners)]
         received[k] = lax.ppermute(blocks[k], "wave", pairs)
     return received
@@ -354,22 +381,36 @@
     own_waves = lax.dynamic_slice_in_dim(slot_wave, my_index * slot_dev, slot_dev)
     north = jnp.transpose(north_rows, (2, 0, 1)).reshape(parts, levels, lat_dev, slots)
     south = jnp.transpose(south_rows, (2, 0, 1)).reshape(parts, levels, lat_dev, slots)
-    columns = []
+    late = far_first(partners)[EARLY:]
+    packed = [list(pack(part, part % 2 == 1, partners, north, south)) for part in range(parts)]
+    returned = []
+    spec_state = None
+    arrived = []
     for part in range(parts):
-        before = columns[-1] if columns else []
-        blocks = pack(part, part == 0, partners, north, south, before[partners // 2 :][:1])
-        columns.append(exchange(gate(blocks, before[NEAR + 1 : partners - NEAR])))
-    spec_state = None
-    returned = []
-    for part in range(parts):
-        spec_state, blocks = spectral_step(
-            part, parts, part == parts - 1, partners, columns[part], legendre, own_waves,
-            lon_counts[None, :], mode_rates[:, None], to_modes.T, from_modes.T, spec_state,
+        if part % 2 == 0:
+            packed[part] = gate(packed[part], arrived)
+        arrived = exchange(packed[part])
+        beside = packed[part + 1] if part % 2 == 0 and part + 1 < parts else []
+        waiting = [beside[k] for k in late] if beside else []
+        spec_state, blocks, waiting = spectral_step(
+            part, parts, part % 2 == 1, partners, arrived, legendre, own_waves,
+            lon_counts[None, :], mode_rates[:, None], to_modes.T, from_modes.T, spec_state, waiting,
         )
-        returned.append(exchange(blocks))
+        for k, block in zip(late, waiting):
+            beside[k] = block
+        returned.append(list(blocks))
     new_rows = None
     for part in range(parts):
-        new_rows = unpack(part, parts, levels, lat_dev, slots, returned[part], new_rows)
+        if part % 2 == 0:
+            returned[part] = gate(returned[part], arrived)
+        arrived = exchange(returned[part])
+        beside = returned[part + 1] if part % 2 == 0 and part + 1 < parts else []
+        waiting = [beside[k] for k in late] if beside else []
+        new_rows, waiting = unpack(
+            part, parts, levels, lat_dev, slots, arrived, new_rows, waiting
+        )
+        for k, block in zip(late, waiting):
+            beside[k] = block
     new_rows = jnp.transpose(new_rows.reshape(channels, lat_dev, slots), (1, 2, 0))
     spec_state = jnp.transpose(spec_state.reshape(channels, slot_dev, row_total), (1, 2, 0))
     return (spec_state, new_rows)

time: 321 us -> 310 us (0.966)
  the two profiles are of different devices: /device:TPU:13 before, /device:TPU:17 now
where the time goes in v6:
time: 310 us
  waiting for transfers between devices  147 us (47%)
  Pallas kernels  86.1 us (28%)
  starting transfers between devices  69.9 us (23%)
  local copies, waits for them, and re-layouts  5.23 us (2%)
    all_to_all x2, waiting for transfers between devices, exchange(): lax.all_to_all(blocks[0], 'wave', split_axis=0, concat_axis=0, tiled=True)  103 us
    pallas_call x2, Pallas kernels, spectral_step(): pl.pallas_call(functools.partial(step_body, taken=len(received), given=le...  66.2 us
    ppermute x30, starting transfers between devices, exchange(): received[k] = lax.ppermute(blocks[k], 'wave', pairs)  58.7 us
    ppermute x30, waiting for transfers between devices, exchange(): received[k] = lax.ppermute(blocks[k], 'wave', pairs)  44 us
    all_to_all x2, starting transfers between devices, exchange(): lax.all_to_all(blocks[0], 'wave', split_axis=0, concat_axis=0, tiled=True)  11.2 us
    pallas_call x2, Pallas kernels, pack(): pl.pallas_call(pack_body, grid=(pl.cdiv(levels, GROUP),), in_specs=[rows,...  10.6 us
    pallas_call x2, Pallas kernels, unpack(): pl.pallas_call(functools.partial(unpack_body, arrays=len(received), passe...  9.31 us
  transfers between devices with their start and end apart: 32, of which 9 were waited for; matrix products, arithmetic and copies ran while one was open for 2% of the time, Pallas kernels for 25%

profile of v6, /device:TPU:17, one launch (start us, length us, event | category | flops | bytes accessed | tf_op | source)
XLA Modules:
  0.0 309.5 jit_solution(2977631482284949182)
XLA Ops:
  0.6 5.2 %shard_map.96 = bf16[16,8,11008]{2,1,0:T(8,128)(2,1)} custom-call(bf16[2,137,80,128]{3,2,1,0:T(8,128)(2,1)} %bitcast.15, bf16[2,137,80,128]{3,2,1,0:T(8,128)(2,1)} %bitcast.17), custom_call_target="tpu_custom_call" | custom-call | flops 2805760 | bytes 8417280 | tf_op jit(solution)/shard_map/pallas_call | solution.py:90
  5.9 6.5 %all-to-all-start = ((bf16[16,8,11008]{2,1,0:T(8,128)(2,1)}), bf16[16,8,11008]{2,1,0:T(8,128)(2,1)}, u32[]{:S(2)}, u32[]{:S(2)}) async-start(bf16[16,8,11008]{2,1,0:T(8,128)(2,1)} %shard_map.96), calls=%async_computation | async-start | bytes 5636096 | tf_op jit(solution)/shard_map/all_to_all | solution.py:364
  12.4 0.0 copy-start.3
  12.4 0.0 copy-start.4
  12.4 5.4 %shard_map.95 = (bf16[8,11008]{1,0:T(8,128)(2,1)}, bf16[8,11008]{1,0:T(8,128)(2,1)}, bf16[8,11008]{1,0:T(8,128)(2,1)}, bf16[8,11008]{1,0:T(8,128)(2,1)}, bf16[8,...) custom-call(bf16[2,137,80,128]{3,2,1,0:T(8,128)(2,1)} %bitcast.16, ...), custom_call_target="tpu_custom_call" | custom-call | flops 2805760 | bytes 8417280 | tf_op jit(solution)/shard_map/pallas_call | solution.py:90
  17.8 2.1 collective-permute-start.5
  19.9 0.8 collective-permute-start.6
  20.7 2.1 collective-permute-start.7
  22.8 1.2 collective-permute-start.8
  24.0 1.5 collective-permute-start.9
  25.5 0.6 broadcast_in_dim.8.refs_2_.refs_17_
  26.1 0.7 copy.37.refs_3_.refs_18_
  26.9 1.6 copy.35
  28.5 1.6 copy.36
  30.1 0.7 dynamic_slice.3.waves_ref
  30.8 63.2 %all-to-all-done.refs_0_ = bf16[16,8,11008]{2,1,0:T(8,128)(2,1)} async-done(((bf16[16,8,11008]{2,1,0:T(8,128)(2,1)}), bf16[16,8,11008]{2,1,0:T(8,128)(2,1)}, u32[]{:S(2)}, u32[]{:S(2)}) %all-to-all-start) | async-done | bytes 2818080 | tf_op jit(solution)/shard_map/all_to_all | solution.py:364
  93.9 32.7 %shard_map.97 = (bf16[2,137,8,1280]{3,2,1,0:T(8,128)(2,1)}, bf16[16,8,11008]{2,1,0:T(8,128)(2,1)}, bf16[8,11008]{1,0:T(8,128)(2,1)}, bf16[8,11008]{1,0:T(8,128)(...) custom-call(s32[8]{0:T(128)} %dynamic_slice.3.waves_ref, ...), custom_call_target="tpu_custom_call", output_to_operand_aliasing={{2}: (7, {}), {3}: (8, {}), {4}: (9, {}), {5}: (10, {}), {6... | custom-call | flops 28730982400 | bytes 34631680 | tf_op jit(solution)/shard_map/pallas_call | solution.py:324
  126.6 0.0 collective-permute-done.5.refs_6_.refs_7_
  126.6 0.1 collective-permute-start
  126.7 0.0 collective-permute-done.6.refs_7_.refs_8_
  126.7 0.1 collective-permute-start.1
  126.8 0.0 collective-permute-done.7.refs_8_.refs_9_
  126.8 0.1 collective-permute-start.2
  126.9 0.0 collective-permute-done.8.refs_9_.refs_10_
  126.9 0.1 collective-permute-start.3
  126.9 0.0 collective-permute-done.9.refs_10_.refs_11_
  126.9 7.5 %collective-permute-start.4 = (bf16[8,11008]{1,0:T(8,128)(2,1)}, bf16[8,11008]{1,0:T(8,128)(2,1)}, u32[]{:S(2)}, u32[]{:S(2)}) collective-permute-start(bf16[8,11008]{1,0:T(8,128)(2,1)} %get-tuple-element.73), channel_id=1, source_target_pairs={{0,5},{1,6},{2,7},{3,8},{4,9},{5,10},{6,11},{7,12},{8,13},{9,14},{... | collective-permute-start | bytes 528392 | tf_op jit(solution)/shard_map/ppermute | solution.py:368
  134.4 0.0 collective-permute-done.refs_1_.refs_2_
  134.4 0.0 collective-permute-start.10
  134.4 4.1 %collective-permute-done.1.refs_2_.refs_3_ = bf16[8,11008]{1,0:T(8,128)(2,1)} collective-permute-done((bf16[8,11008]{1,0:T(8,128)(2,1)}, bf16[8,11008]{1,0:T(8,128)(2,1)}, u32[]{:S(2)}, u32[]{:S(2)}) %collective-permute-start.1) | collective-permute-done | bytes 176160 | tf_op jit(solution)/shard_map/ppermute | solution.py:368
  138.5 0.0 collective-permute-start.11
  138.5 1.2 collective-permute-done.2.refs_3_.refs_4_
  139.7 0.0 collective-permute-start.12
  139.7 0.0 collective-permute-done.3.refs_4_.refs_5_
  139.7 17.2 %collective-permute-start.13 = (bf16[8,11008]{1,0:T(8,128)(2,1)}, bf16[8,11008]{1,0:T(8,128)(2,1)}, u32[]{:S(2)}, u32[]{:S(2)}) collective-permute-start(bf16[8,11008]{1,0:T(8,128)(2,1)} %get-tuple-element.82), channel_id=1, source_target_pairs={{0,14},{1,15},{2,0},{3,1},{4,2},{5,3},{6,4},{7,5},{8,6},{9,7},{10,... | collective-permute-start | bytes 528392 | tf_op jit(solution)/shard_map/ppermute | solution.py:368
  156.9 0.0 collective-permute-start.14
  156.9 0.0 collective-permute-done.10.refs_11_.refs_12_
  157.0 0.0 collective-permute-done.12.refs_13_.refs_14_
  157.0 4.1 %collective-permute-done.13.refs_14_.refs_15_ = bf16[8,11008]{1,0:T(8,128)(2,1)} collective-permute-done((bf16[8,11008]{1,0:T(8,128)(2,1)}, bf16[8,11008]{1,0:T(8,128)(2,1)}, u32[]{:S(2)}, u32[]{:S(2)}) %collective-permute-start.13) | collective-permute-done | bytes 176160 | tf_op jit(solution)/shard_map/ppermute | solution.py:368
  161.1 4.1 %collective-permute-done.14.refs_15_.refs_16_ = bf16[8,11008]{1,0:T(8,128)(2,1)} collective-permute-done((bf16[8,11008]{1,0:T(8,128)(2,1)}, bf16[8,11008]{1,0:T(8,128)(2,1)}, u32[]{:S(2)}, u32[]{:S(2)}) %collective-permute-start.14) | collective-permute-done | bytes 176160 | tf_op jit(solution)/shard_map/ppermute | solution.py:368
  165.2 4.7 %all-to-all-start.1 = ((bf16[16,8,11008]{2,1,0:T(8,128)(2,1)}), bf16[16,8,11008]{2,1,0:T(8,128)(2,1)}, u32[]{:S(2)}, u32[]{:S(2)}) async-start(bf16[16,8,11008]{2,1,0:T(8,128)(2,1)} %shard_map.99), calls=%async_computation.1 | async-start | bytes 5636096 | tf_op jit(solution)/shard_map/all_to_all | solution.py:364
  169.9 33.5 %shard_map.98 = (bf16[2,137,8,1280]{3,2,1,0:T(8,128)(2,1)}, bf16[8,11008]{1,0:T(8,128)(2,1)}, bf16[8,11008]{1,0:T(8,128)(2,1)}, bf16[8,11008]{1,0:T(8,128)(2,1)}...) custom-call(s32[8]{0:T(128)} %dynamic_slice.3.waves_ref, ...), custom_call_target="tpu_custom_call", output_to_operand_aliasing={{0}: (22, {})} | custom-call | flops 28730982400 | bytes 34631680 | tf_op jit(solution)/shard_map/pallas_call | solution.py:324
  203.5 2.1 collective-permute-start.20
  205.6 0.8 collective-permute-start.21
  206.4 2.1 collective-permute-start.22
  208.5 1.2 collective-permute-start.23
  209.7 1.5 collective-permute-start.24
  211.2 40.3 %all-to-all-done.1.refs_0_ = bf16[16,8,11008]{2,1,0:T(8,128)(2,1)} async-done(((bf16[16,8,11008]{2,1,0:T(8,128)(2,1)}), bf16[16,8,11008]{2,1,0:T(8,128)(2,1)}, u32[]{:S(2)}, u32[]{:S(2)}) %all-to-all-start.1) | async-done | bytes 2818080 | tf_op jit(solution)/shard_map/all_to_all | solution.py:364
  251.5 4.5 %shard_map.100 = (bf16[2,137,80,128]{3,2,1,0:T(8,128)(2,1)}, bf16[8,11008]{1,0:T(8,128)(2,1)}, bf16[8,11008]{1,0:T(8,128)(2,1)}, bf16[8,11008]{1,0:T(8,128)(2,1)...) custom-call(bf16[16,8,11008]{2,1,0:T(8,128)(2,1)} %all-to-all-done.1, ...), custom_call_target="tpu_custom_call", output_to_operand_aliasing={{1}: (1, {}), {2}: (2, {}), {3}: (3, {}), {4}: (4, {}), {5}... | custom-call | flops 1402880 | bytes 5611520 | tf_op jit(solution)/shard_map/pallas_call | solution.py:132
  256.0 0.0 collective-permute-done.20.refs_6_
  256.0 0.0 collective-permute-start.15
  256.0 0.0 collective-permute-done.21.refs_7_
  256.1 2.7 collective-permute-start.16
  258.8 2.3 collective-permute-start.17
  261.1 0.0 collective-permute-done.23.refs_9_
  261.1 1.2 collective-permute-start.18
  262.3 8.7 %collective-permute-done.24.refs_10_ = bf16[8,11008]{1,0:T(8,128)(2,1)} collective-permute-done((bf16[8,11008]{1,0:T(8,128)(2,1)}, bf16[8,11008]{1,0:T(8,128)(2,1)}, u32[]{:S(2)}, u32[]{:S(2)}) %collective-permute-start.24) | collective-permute-done | bytes 176160 | tf_op jit(solution)/shard_map/ppermute | solution.py:368
  270.9 7.2 %collective-permute-start.25 = (bf16[8,11008]{1,0:T(8,128)(2,1)}, bf16[8,11008]{1,0:T(8,128)(2,1)}, u32[]{:S(2)}, u32[]{:S(2)}) collective-permute-start(bf16[8,11008]{1,0:T(8,128)(2,1)} %get-tuple-element.108), channel_id=1, source_target_pairs={{0,11},{1,12},{2,13},{3,14},{4,15},{5,0},{6,1},{7,2},{8,3},{9,4},{... | collective-permute-start | bytes 528392 | tf_op jit(solution)/shard_map/ppermute | solution.py:368
  278.1 1.0 collective-permute-start.26
  279.1 3.8 %collective-permute-start.28 = (bf16[8,11008]{1,0:T(8,128)(2,1)}, bf16[8,11008]{1,0:T(8,128)(2,1)}, u32[]{:S(2)}, u32[]{:S(2)}) collective-permute-start(bf16[8,11008]{1,0:T(8,128)(2,1)} %get-tuple-element.111), channel_id=1, source_target_pairs={{0,14},{1,15},{2,0},{3,1},{4,2},{5,3},{6,4},{7,5},{8,6},{9,7},{10,... | collective-permute-start | bytes 528392 | tf_op jit(solution)/shard_map/ppermute | solution.py:368
  283.0 16.4 %collective-permute-done.19.refs_5_ = bf16[8,11008]{1,0:T(8,128)(2,1)} collective-permute-done((bf16[8,11008]{1,0:T(8,128)(2,1)}, bf16[8,11008]{1,0:T(8,128)(2,1)}, u32[]{:S(2)}, u32[]{:S(2)}) %collective-permute-start.19) | collective-permute-done | bytes 176160 | tf_op jit(solution)/shard_map/ppermute | solution.py:368
  299.3 0.0 collective-permute-done.27.refs_13_
  299.4 5.4 %collective-permute-done.29.refs_15_ = bf16[8,11008]{1,0:T(8,128)(2,1)} collective-permute-done((bf16[8,11008]{1,0:T(8,128)(2,1)}, bf16[8,11008]{1,0:T(8,128)(2,1)}, u32[]{:S(2)}, u32[]{:S(2)}) %collective-permute-start.29) | collective-permute-done | bytes 176160 | tf_op jit(solution)/shard_map/ppermute | solution.py:368
  304.7 4.8 %shard_map.101 = bf16[2,137,80,128]{3,2,1,0:T(8,128)(2,1)} custom-call(bf16[8,11008]{1,0:T(8,128)(2,1)} %get-tuple-element.86.refs_0_, bf16[8,11008]{1,0:T(8,128)(2,1)} %collective-permute-done.15.refs_1_, bf16[8,11008]{1,0:T(8,128)(2,1)} %collective-permute-done.16.refs_2_, ...), custom_call_target="tpu_custom_call", output_to_operand_aliasing={{}: (16, {})} | custom-call | flops 1402880 | bytes 5611520 | tf_op jit(solution)/shard_map/pallas_call | solution.py:132
  (22 shorter events, 0.0 us)
Async XLA Ops:
  5.9 88.1 %all-to-all-start = ((bf16[16,8,11008]{2,1,0:T(8,128)(2,1)}), bf16[16,8,11008]{2,1,0:T(8,128)(2,1)}, u32[]{:S(2)}, u32[]{:S(2)}) async-start(bf16[16,8,11008]{2,1,0:T(8,128)(2,1)} %shard_map.96), calls=%async_computation | async-start | bytes 5636096 | tf_op jit(solution)/shard_map/all_to_all | solution.py:364
  12.4 13.2 %copy-start.2 = (s32[1280]{0:T(1024)S(1)}, s32[1280]{0:T(1024)}, u32[]{:S(2)}) copy-start(s32[1280]{0:T(1024)} %param.10) | copy-start | bytes 15364
  12.4 13.8 %copy-start.3 = (f32[137]{0:T(256)S(1)}, f32[137]{0:T(256)}, u32[]{:S(2)}) copy-start(f32[137]{0:T(256)} %param.13) | copy-start | bytes 1648
  12.4 17.7 %copy-start.4 = (s32[128]{0:T(128)S(1)}, s32[128]{0:T(128)}, u32[]{:S(2)}) copy-start(s32[128]{0:T(128)} %param.11) | copy-start | bytes 1540
  17.8 108.9 %collective-permute-start.5 = (bf16[8,11008]{1,0:T(8,128)(2,1)}, bf16[8,11008]{1,0:T(8,128)(2,1)S(1)}, u32[]{:S(2)}, u32[]{:S(2)}) collective-permute-start(bf16[8,11008]{1,0:T(8,128)(2,1)} %get-tuple-element.74), channel_id=1, source_target_pairs={{0,6},{1,7},{2,8},{3,9},{4,10},{5,11},{6,12},{7,13},{8,14},{9,15},... | collective-permute-start | bytes 528392 | tf_op jit(solution)/shard_map/ppermute | solution.py:368
  19.9 106.8 %collective-permute-start.6 = (bf16[8,11008]{1,0:T(8,128)(2,1)}, bf16[8,11008]{1,0:T(8,128)(2,1)}, u32[]{:S(2)}, u32[]{:S(2)}) collective-permute-start(bf16[8,11008]{1,0:T(8,128)(2,1)} %get-tuple-element.75), channel_id=1, source_target_pairs={{0,7},{1,8},{2,9},{3,10},{4,11},{5,12},{6,13},{7,14},{8,15},{9,0},... | collective-permute-start | bytes 528392 | tf_op jit(solution)/shard_map/ppermute | solution.py:368
  20.7 106.1 %collective-permute-start.7 = (bf16[8,11008]{1,0:T(8,128)(2,1)}, bf16[8,11008]{1,0:T(8,128)(2,1)}, u32[]{:S(2)}, u32[]{:S(2)}) collective-permute-start(bf16[8,11008]{1,0:T(8,128)(2,1)} %get-tuple-element.76), channel_id=1, source_target_pairs={{0,8},{1,9},{2,10},{3,11},{4,12},{5,13},{6,14},{7,15},{8,0},{9,1},... | collective-permute-start | bytes 528392 | tf_op jit(solution)/shard_map/ppermute | solution.py:368
  22.8 104.1 %collective-permute-start.8 = (bf16[8,11008]{1,0:T(8,128)(2,1)}, bf16[8,11008]{1,0:T(8,128)(2,1)}, u32[]{:S(2)}, u32[]{:S(2)}) collective-permute-start(bf16[8,11008]{1,0:T(8,128)(2,1)} %get-tuple-element.77), channel_id=1, source_target_pairs={{0,9},{1,10},{2,11},{3,12},{4,13},{5,14},{6,15},{7,0},{8,1},{9,2},... | collective-permute-start | bytes 528392 | tf_op jit(solution)/shard_map/ppermute | solution.py:368
  24.0 102.9 %collective-permute-start.9 = (bf16[8,11008]{1,0:T(8,128)(2,1)}, bf16[8,11008]{1,0:T(8,128)(2,1)}, u32[]{:S(2)}, u32[]{:S(2)}) collective-permute-start(bf16[8,11008]{1,0:T(8,128)(2,1)} %get-tuple-element.78), channel_id=1, source_target_pairs={{0,10},{1,11},{2,12},{3,13},{4,14},{5,15},{6,0},{7,1},{8,2},{9,3},... | collective-permute-start | bytes 528392 | tf_op jit(solution)/shard_map/ppermute | solution.py:368
  126.6 38.6 %copy-start = (bf16[8,11008]{1,0:T(8,128)(2,1)}, bf16[8,11008]{1,0:T(8,128)(2,1)S(1)}, u32[]{:S(2)}) copy-start(bf16[8,11008]{1,0:T(8,128)(2,1)S(1)} %collective-permute-done.5.refs_6_.refs_7_) | copy-start | bytes 528388
  126.6 7.8 %collective-permute-start = (bf16[8,11008]{1,0:T(8,128)(2,1)}, bf16[8,11008]{1,0:T(8,128)(2,1)}, u32[]{:S(2)}, u32[]{:S(2)}) collective-permute-start(bf16[8,11008]{1,0:T(8,128)(2,1)} %get-tuple-element.69), channel_id=1, source_target_pairs={{0,1},{1,2},{2,3},{3,4},{4,5},{5,6},{6,7},{7,8},{8,9},{9,10},{10,1... | collective-permute-start | bytes 528392 | tf_op jit(solution)/shard_map/ppermute | solution.py:368
  126.7 11.8 %collective-permute-start.1 = (bf16[8,11008]{1,0:T(8,128)(2,1)}, bf16[8,11008]{1,0:T(8,128)(2,1)}, u32[]{:S(2)}, u32[]{:S(2)}) collective-permute-start(bf16[8,11008]{1,0:T(8,128)(2,1)} %get-tuple-element.70), channel_id=1, source_target_pairs={{0,2},{1,3},{2,4},{3,5},{4,6},{5,7},{6,8},{7,9},{8,10},{9,11},{10,... | collective-permute-start | bytes 528392 | tf_op jit(solution)/shard_map/ppermute | solution.py:368
  126.8 12.9 %collective-permute-start.2 = (bf16[8,11008]{1,0:T(8,128)(2,1)}, bf16[8,11008]{1,0:T(8,128)(2,1)}, u32[]{:S(2)}, u32[]{:S(2)}) collective-permute-start(bf16[8,11008]{1,0:T(8,128)(2,1)} %get-tuple-element.71), channel_id=1, source_target_pairs={{0,3},{1,4},{2,5},{3,6},{4,7},{5,8},{6,9},{7,10},{8,11},{9,12},{10... | collective-permute-start | bytes 528392 | tf_op jit(solution)/shard_map/ppermute | solution.py:368
  126.9 12.8 %collective-permute-start.3 = (bf16[8,11008]{1,0:T(8,128)(2,1)}, bf16[8,11008]{1,0:T(8,128)(2,1)}, u32[]{:S(2)}, u32[]{:S(2)}) collective-permute-start(bf16[8,11008]{1,0:T(8,128)(2,1)} %get-tuple-element.72), channel_id=1, source_target_pairs={{0,4},{1,5},{2,6},{3,7},{4,8},{5,9},{6,10},{7,11},{8,12},{9,13},{1... | collective-permute-start | bytes 528392 | tf_op jit(solution)/shard_map/ppermute | solution.py:368
  126.9 30.0 %collective-permute-start.4 = (bf16[8,11008]{1,0:T(8,128)(2,1)}, bf16[8,11008]{1,0:T(8,128)(2,1)}, u32[]{:S(2)}, u32[]{:S(2)}) collective-permute-start(bf16[8,11008]{1,0:T(8,128)(2,1)} %get-tuple-element.73), channel_id=1, source_target_pairs={{0,5},{1,6},{2,7},{3,8},{4,9},{5,10},{6,11},{7,12},{8,13},{9,14},{... | collective-permute-start | bytes 528392 | tf_op jit(solution)/shard_map/ppermute | solution.py:368
  134.4 22.5 %collective-permute-start.10 = (bf16[8,11008]{1,0:T(8,128)(2,1)}, bf16[8,11008]{1,0:T(8,128)(2,1)}, u32[]{:S(2)}, u32[]{:S(2)}) collective-permute-start(bf16[8,11008]{1,0:T(8,128)(2,1)} %get-tuple-element.79), channel_id=1, source_target_pairs={{0,11},{1,12},{2,13},{3,14},{4,15},{5,0},{6,1},{7,2},{8,3},{9,4},{... | collective-permute-start | bytes 528392 | tf_op jit(solution)/shard_map/ppermute | solution.py:368
  138.5 18.4 %collective-permute-start.11 = (bf16[8,11008]{1,0:T(8,128)(2,1)}, bf16[8,11008]{1,0:T(8,128)(2,1)}, u32[]{:S(2)}, u32[]{:S(2)}) collective-permute-start(bf16[8,11008]{1,0:T(8,128)(2,1)} %get-tuple-element.80), channel_id=1, source_target_pairs={{0,12},{1,13},{2,14},{3,15},{4,0},{5,1},{6,2},{7,3},{8,4},{9,5},{1... | collective-permute-start | bytes 528392 | tf_op jit(solution)/shard_map/ppermute | solution.py:368
  139.7 17.3 %collective-permute-start.12 = (bf16[8,11008]{1,0:T(8,128)(2,1)}, bf16[8,11008]{1,0:T(8,128)(2,1)}, u32[]{:S(2)}, u32[]{:S(2)}) collective-permute-start(bf16[8,11008]{1,0:T(8,128)(2,1)} %get-tuple-element.81), channel_id=1, source_target_pairs={{0,13},{1,14},{2,15},{3,0},{4,1},{5,2},{6,3},{7,4},{8,5},{9,6},{10... | collective-permute-start | bytes 528392 | tf_op jit(solution)/shard_map/ppermute | solution.py:368
  139.7 21.4 %collective-permute-start.13 = (bf16[8,11008]{1,0:T(8,128)(2,1)}, bf16[8,11008]{1,0:T(8,128)(2,1)}, u32[]{:S(2)}, u32[]{:S(2)}) collective-permute-start(bf16[8,11008]{1,0:T(8,128)(2,1)} %get-tuple-element.82), channel_id=1, source_target_pairs={{0,14},{1,15},{2,0},{3,1},{4,2},{5,3},{6,4},{7,5},{8,6},{9,7},{10,... | collective-permute-start | bytes 528392 | tf_op jit(solution)/shard_map/ppermute | solution.py:368
  156.9 8.3 %collective-permute-start.14 = (bf16[8,11008]{1,0:T(8,128)(2,1)}, bf16[8,11008]{1,0:T(8,128)(2,1)}, u32[]{:S(2)}, u32[]{:S(2)}) collective-permute-start(bf16[8,11008]{1,0:T(8,128)(2,1)} %get-tuple-element.83), channel_id=1, source_target_pairs={{0,15},{1,0},{2,1},{3,2},{4,3},{5,4},{6,5},{7,6},{8,7},{9,8},{10,9... | collective-permute-start | bytes 528392 | tf_op jit(solution)/shard_map/ppermute | solution.py:368
  165.2 86.3 %all-to-all-start.1 = ((bf16[16,8,11008]{2,1,0:T(8,128)(2,1)}), bf16[16,8,11008]{2,1,0:T(8,128)(2,1)}, u32[]{:S(2)}, u32[]{:S(2)}) async-start(bf16[16,8,11008]{2,1,0:T(8,128)(2,1)} %shard_map.99), calls=%async_computation.1 | async-start | bytes 5636096 | tf_op jit(solution)/shard_map/all_to_all | solution.py:364
  203.5 52.6 %collective-permute-start.20 = (bf16[8,11008]{1,0:T(8,128)(2,1)}, bf16[8,11008]{1,0:T(8,128)(2,1)S(1)}, u32[]{:S(2)}, u32[]{:S(2)}) collective-permute-start(bf16[8,11008]{1,0:T(8,128)(2,1)} %get-tuple-element.103), channel_id=1, source_target_pairs={{0,6},{1,7},{2,8},{3,9},{4,10},{5,11},{6,12},{7,13},{8,14},{9,15},... | collective-permute-start | bytes 528392 | tf_op jit(solution)/shard_map/ppermute | solution.py:368
  205.6 50.5 %collective-permute-start.21 = (bf16[8,11008]{1,0:T(8,128)(2,1)}, bf16[8,11008]{1,0:T(8,128)(2,1)}, u32[]{:S(2)}, u32[]{:S(2)}) collective-permute-start(bf16[8,11008]{1,0:T(8,128)(2,1)} %get-tuple-element.104), channel_id=1, source_target_pairs={{0,7},{1,8},{2,9},{3,10},{4,11},{5,12},{6,13},{7,14},{8,15},{9,0},... | collective-permute-start | bytes 528392 | tf_op jit(solution)/shard_map/ppermute | solution.py:368
  206.4 52.4 %collective-permute-start.22 = (bf16[8,11008]{1,0:T(8,128)(2,1)}, bf16[8,11008]{1,0:T(8,128)(2,1)}, u32[]{:S(2)}, u32[]{:S(2)}) collective-permute-start(bf16[8,11008]{1,0:T(8,128)(2,1)} %get-tuple-element.105), channel_id=1, source_target_pairs={{0,8},{1,9},{2,10},{3,11},{4,12},{5,13},{6,14},{7,15},{8,0},{9,1},... | collective-permute-start | bytes 528392 | tf_op jit(solution)/shard_map/ppermute | solution.py:368
  208.5 52.6 %collective-permute-start.23 = (bf16[8,11008]{1,0:T(8,128)(2,1)}, bf16[8,11008]{1,0:T(8,128)(2,1)}, u32[]{:S(2)}, u32[]{:S(2)}) collective-permute-start(bf16[8,11008]{1,0:T(8,128)(2,1)} %get-tuple-element.106), channel_id=1, source_target_pairs={{0,9},{1,10},{2,11},{3,12},{4,13},{5,14},{6,15},{7,0},{8,1},{9,2},... | collective-permute-start | bytes 528392 | tf_op jit(solution)/shard_map/ppermute | solution.py:368
  209.7 61.2 %collective-permute-start.24 = (bf16[8,11008]{1,0:T(8,128)(2,1)}, bf16[8,11008]{1,0:T(8,128)(2,1)}, u32[]{:S(2)}, u32[]{:S(2)}) collective-permute-start(bf16[8,11008]{1,0:T(8,128)(2,1)} %get-tuple-element.107), channel_id=1, source_target_pairs={{0,10},{1,11},{2,12},{3,13},{4,14},{5,15},{6,0},{7,1},{8,2},{9,3},... | collective-permute-start | bytes 528392 | tf_op jit(solution)/shard_map/ppermute | solution.py:368
  256.0 48.7 %copy-start.1 = (bf16[8,11008]{1,0:T(8,128)(2,1)}, bf16[8,11008]{1,0:T(8,128)(2,1)S(1)}, u32[]{:S(2)}) copy-start(bf16[8,11008]{1,0:T(8,128)(2,1)S(1)} %collective-permute-done.20.refs_6_) | copy-start | bytes 528388
  256.0 14.9 %collective-permute-start.15 = (bf16[8,11008]{1,0:T(8,128)(2,1)}, bf16[8,11008]{1,0:T(8,128)(2,1)}, u32[]{:S(2)}, u32[]{:S(2)}) collective-permute-start(bf16[8,11008]{1,0:T(8,128)(2,1)} %get-tuple-element.98), channel_id=1, source_target_pairs={{0,1},{1,2},{2,3},{3,4},{4,5},{5,6},{6,7},{7,8},{8,9},{9,10},{10,1... | collective-permute-start | bytes 528392 | tf_op jit(solution)/shard_map/ppermute | solution.py:368
  256.1 22.1 %collective-permute-start.16 = (bf16[8,11008]{1,0:T(8,128)(2,1)}, bf16[8,11008]{1,0:T(8,128)(2,1)}, u32[]{:S(2)}, u32[]{:S(2)}) collective-permute-start(bf16[8,11008]{1,0:T(8,128)(2,1)} %get-tuple-element.99), channel_id=1, source_target_pairs={{0,2},{1,3},{2,4},{3,5},{4,6},{5,7},{6,8},{7,9},{8,10},{9,11},{10,... | collective-permute-start | bytes 528392 | tf_op jit(solution)/shard_map/ppermute | solution.py:368
  258.8 20.3 %collective-permute-start.17 = (bf16[8,11008]{1,0:T(8,128)(2,1)}, bf16[8,11008]{1,0:T(8,128)(2,1)}, u32[]{:S(2)}, u32[]{:S(2)}) collective-permute-start(bf16[8,11008]{1,0:T(8,128)(2,1)} %get-tuple-element.100), channel_id=1, source_target_pairs={{0,3},{1,4},{2,5},{3,6},{4,7},{5,8},{6,9},{7,10},{8,11},{9,12},{10... | collective-permute-start | bytes 528392 | tf_op jit(solution)/shard_map/ppermute | solution.py:368
  261.1 18.0 %collective-permute-start.18 = (bf16[8,11008]{1,0:T(8,128)(2,1)}, bf16[8,11008]{1,0:T(8,128)(2,1)}, u32[]{:S(2)}, u32[]{:S(2)}) collective-permute-start(bf16[8,11008]{1,0:T(8,128)(2,1)} %get-tuple-element.101), channel_id=1, source_target_pairs={{0,4},{1,5},{2,6},{3,7},{4,8},{5,9},{6,10},{7,11},{8,12},{9,13},{1... | collective-permute-start | bytes 528392 | tf_op jit(solution)/shard_map/ppermute | solution.py:368
  270.9 28.4 %collective-permute-start.19 = (bf16[8,11008]{1,0:T(8,128)(2,1)}, bf16[8,11008]{1,0:T(8,128)(2,1)}, u32[]{:S(2)}, u32[]{:S(2)}) collective-permute-start(bf16[8,11008]{1,0:T(8,128)(2,1)} %get-tuple-element.102), channel_id=1, source_target_pairs={{0,5},{1,6},{2,7},{3,8},{4,9},{5,10},{6,11},{7,12},{8,13},{9,14},{... | collective-permute-start | bytes 528392 | tf_op jit(solution)/shard_map/ppermute | solution.py:368
  270.9 28.4 %collective-permute-start.25 = (bf16[8,11008]{1,0:T(8,128)(2,1)}, bf16[8,11008]{1,0:T(8,128)(2,1)}, u32[]{:S(2)}, u32[]{:S(2)}) collective-permute-start(bf16[8,11008]{1,0:T(8,128)(2,1)} %get-tuple-element.108), channel_id=1, source_target_pairs={{0,11},{1,12},{2,13},{3,14},{4,15},{5,0},{6,1},{7,2},{8,3},{9,4},{... | collective-permute-start | bytes 528392 | tf_op jit(solution)/shard_map/ppermute | solution.py:368
  278.1 21.2 %collective-permute-start.26 = (bf16[8,11008]{1,0:T(8,128)(2,1)}, bf16[8,11008]{1,0:T(8,128)(2,1)}, u32[]{:S(2)}, u32[]{:S(2)}) collective-permute-start(bf16[8,11008]{1,0:T(8,128)(2,1)} %get-tuple-element.109), channel_id=1, source_target_pairs={{0,12},{1,13},{2,14},{3,15},{4,0},{5,1},{6,2},{7,3},{8,4},{9,5},{1... | collective-permute-start | bytes 528392 | tf_op jit(solution)/shard_map/ppermute | solution.py:368
  279.1 20.2 %collective-permute-start.27 = (bf16[8,11008]{1,0:T(8,128)(2,1)}, bf16[8,11008]{1,0:T(8,128)(2,1)}, u32[]{:S(2)}, u32[]{:S(2)}) collective-permute-start(bf16[8,11008]{1,0:T(8,128)(2,1)} %get-tuple-element.110), channel_id=1, source_target_pairs={{0,13},{1,14},{2,15},{3,0},{4,1},{5,2},{6,3},{7,4},{8,5},{9,6},{10... | collective-permute-start | bytes 528392 | tf_op jit(solution)/shard_map/ppermute | solution.py:368
  279.1 20.2 %collective-permute-start.28 = (bf16[8,11008]{1,0:T(8,128)(2,1)}, bf16[8,11008]{1,0:T(8,128)(2,1)}, u32[]{:S(2)}, u32[]{:S(2)}) collective-permute-start(bf16[8,11008]{1,0:T(8,128)(2,1)} %get-tuple-element.111), channel_id=1, source_target_pairs={{0,14},{1,15},{2,0},{3,1},{4,2},{5,3},{6,4},{7,5},{8,6},{9,7},{10,... | collective-permute-start | bytes 528392 | tf_op jit(solution)/shard_map/ppermute | solution.py:368
  299.3 5.4 %collective-permute-start.29 = (bf16[8,11008]{1,0:T(8,128)(2,1)}, bf16[8,11008]{1,0:T(8,128)(2,1)}, u32[]{:S(2)}, u32[]{:S(2)}) collective-permute-start(bf16[8,11008]{1,0:T(8,128)(2,1)} %get-tuple-element.112), channel_id=1, source_target_pairs={{0,15},{1,0},{2,1},{3,2},{4,3},{5,4},{6,5},{7,6},{8,7},{9,8},{10,9... | collective-permute-start | bytes 528392 | tf_op jit(solution)/shard_map/ppermute | solution.py:368

commit v7 on v3

--- a/solution.py
+++ b/solution.py
@@ -10,7 +10,7 @@
 
 NMAX = 2559
 VMEM_BYTES = 62 * 1024 * 1024
-GROUP = 48
+GROUPS = 3
 LANES = 128
 
 
@@ -22,18 +22,18 @@
 
 
 def pack_body(north_ref, south_ref, out_ref):
-    summed = north_ref[0].astype(jnp.float32) + south_ref[0].astype(jnp.float32)
-    out_ref[...] = flat_rows(summed.astype(jnp.bfloat16)).T
+    out_ref[...] = flat_rows(north_ref[0] + south_ref[0]).T
 
 
 def pack(part, north, south):
     _, levels, lat_dev, slots = north.shape
-    rows = pl.BlockSpec((1, GROUP, lat_dev, slots), lambda i: (part, i, 0, 0))
+    group = GROUPS * group_size(lat_dev)
+    rows = pl.BlockSpec((1, group, lat_dev, slots), lambda i: (part, i, 0, 0))
     return pl.pallas_call(
         pack_body,
-        grid=(pl.cdiv(levels, GROUP),),
+        grid=(pl.cdiv(levels, group),),
         in_specs=[rows, rows],
-        out_specs=pl.BlockSpec((slots, GROUP * lat_dev), lambda i: (0, i)),
+        out_specs=pl.BlockSpec((slots, group * lat_dev), lambda i: (0, i)),
         out_shape=jax.ShapeDtypeStruct((slots, pl.cdiv(levels * lat_dev, LANES) * LANES), jnp.bfloat16),
         compiler_params=pltpu.CompilerParams(vmem_limit_bytes=VMEM_BYTES),
         cost_estimate=pl.CostEstimate(
@@ -55,7 +55,8 @@
 
 def unpack(part, parts, levels, lat_dev, received, earlier):
     slots = received.shape[0]
-    in_specs = [pl.BlockSpec((slots, GROUP * lat_dev), lambda i: (0, i))]
+    group = GROUPS * group_size(lat_dev)
+    in_specs = [pl.BlockSpec((slots, group * lat_dev), lambda i: (0, i))]
     operands = [received]
     aliases = {}
     if earlier is not None:
@@ -64,9 +65,9 @@
         aliases = {1: 0}
     return pl.pallas_call(
         unpack_body,
-        grid=(pl.cdiv(levels, GROUP),),
+        grid=(pl.cdiv(levels, group),),
         in_specs=in_specs,
-        out_specs=pl.BlockSpec((1, GROUP, lat_dev, slots), lambda i: (part, i, 0, 0)),
+        out_specs=pl.BlockSpec((1, group, lat_dev, slots), lambda i: (part, i, 0, 0)),
         out_shape=jax.ShapeDtypeStruct((parts, levels, lat_dev, slots), jnp.bfloat16),
         input_output_aliases=aliases,
         compiler_params=pltpu.CompilerParams(vmem_limit_bytes=VMEM_BYTES),

time: 284 us -> 286 us (level)
  Pallas kernels: 84.8 us -> 88.4 us
    pallas_call x4, Pallas kernels: 19.5 us -> 23.1 us  [the longest x2 12 us: pack(): pl.pallas_call(pack_body, grid=(pl.cdiv(levels, group),), in_specs=[rows,...]
  transfers between devices with their start and end apart: 4 -> 4, of which waited for: 4 -> 4; matrix products, arithmetic and copies ran while one was open for 1% -> 1% of each run, Pallas kernels for 26% -> 27%
where the time goes in v7:
time: 286 us
  waiting for transfers between devices  172 us (60%)
  Pallas kernels  88.4 us (31%)
  starting transfers between devices  21.4 us (7%)
  local copies, waits for them, and re-layouts  3.48 us (1%)
    all_to_all x2, waiting for transfers between devices, per_device(): returned.append(exchange(rows))  87.7 us
    all_to_all x2, waiting for transfers between devices, per_device(): columns = [exchange(pack(part, north, south)) for part in range(parts)]  83.8 us
    pallas_call x2, Pallas kernels, spectral_step(): pl.pallas_call(step_body, grid_spec=pltpu.PrefetchScalarGridSpec(num_scal...  65.3 us
    pallas_call x2, Pallas kernels, pack(): pl.pallas_call(pack_body, grid=(pl.cdiv(levels, group),), in_specs=[rows,...  12 us
    all_to_all x2, starting transfers between devices, per_device(): columns = [exchange(pack(part, north, south)) for part in range(parts)]  11.6 us
    pallas_call x2, Pallas kernels, unpack(): pl.pallas_call(unpack_body, grid=(pl.cdiv(levels, group),), in_specs=in_s...  11.1 us
    all_to_all x2, starting transfers between devices, per_device(): returned.append(exchange(rows))  9.82 us
  transfers between devices with their start and end apart: 4, of which 4 were waited for; matrix products, arithmetic and copies ran while one was open for 1% of the time, Pallas kernels for 27%

profile of v7, /device:TPU:13, one launch (start us, length us, event | category | flops | bytes accessed | tf_op | source)
XLA Modules:
  0.0 285.5 jit_solution(9625252395782743801)
XLA Ops:
  0.6 6.0 %shard_map.96 = bf16[128,11008]{1,0:T(8,128)(2,1)} custom-call(bf16[2,137,80,128]{3,2,1,0:T(8,128)(2,1)} %bitcast.24, bf16[2,137,80,128]{3,2,1,0:T(8,128)(2,1)} %bitcast.26), custom_call_target="tpu_custom_call" | custom-call | flops 2805760 | bytes 8417280 | tf_op jit(solution)/shard_map/pallas_call | solution.py:32
  6.6 6.6 %all-to-all-start.1 = ((bf16[16,8,11008]{2,1,0:T(8,128)(2,1)}), bf16[16,8,11008]{2,1,0:T(8,128)(2,1)}, u32[]{:S(2)}, u32[]{:S(2)}) async-start(bf16[16,8,11008]{2,1,0:T(8,128)(2,1)} %bitcast.29), calls=%async_computation.1 | async-start | bytes 5636096 | tf_op jit(solution)/shard_map/all_to_all | solution.py:292
  13.2 6.0 %shard_map.95 = bf16[128,11008]{1,0:T(8,128)(2,1)} custom-call(bf16[2,137,80,128]{3,2,1,0:T(8,128)(2,1)} %bitcast.25, bf16[2,137,80,128]{3,2,1,0:T(8,128)(2,1)} %bitcast.27), custom_call_target="tpu_custom_call" | custom-call | flops 2805760 | bytes 8417280 | tf_op jit(solution)/shard_map/pallas_call | solution.py:32
  19.2 57.0 %all-to-all-done.1 = bf16[16,8,11008]{2,1,0:T(8,128)(2,1)} async-done(((bf16[16,8,11008]{2,1,0:T(8,128)(2,1)}), bf16[16,8,11008]{2,1,0:T(8,128)(2,1)}, u32[]{:S(2)}, u32[]{:S(2)}) %all-to-all-start.1) | async-done | bytes 2818080 | tf_op jit(solution)/shard_map/all_to_all | solution.py:292
  76.2 0.0 copy-start.2
  76.2 0.0 copy-start.3
  76.2 0.0 copy-start
  76.2 0.0 copy-start.1
  76.2 0.0 copy-start.4
  76.2 5.1 %all-to-all-start = ((bf16[16,8,11008]{2,1,0:T(8,128)(2,1)}), bf16[16,8,11008]{2,1,0:T(8,128)(2,1)}, u32[]{:S(2)}, u32[]{:S(2)}) async-start(bf16[16,8,11008]{2,1,0:T(8,128)(2,1)} %bitcast.28), calls=%async_computation | async-start | bytes 5636096 | tf_op jit(solution)/shard_map/all_to_all | solution.py:292
  81.2 0.0 copy-done.2
  81.3 0.6 broadcast_in_dim.8.counts_ref
  81.9 0.0 copy-done.3
  81.9 0.7 copy.17.rates_ref
  82.6 0.0 copy-done
  82.6 0.7 copy.14
  83.3 0.0 copy-done.1
  83.3 0.7 copy.15
  84.1 0.0 copy-done.4
  84.1 0.7 dynamic_slice.3.waves_ref
  84.7 32.6 %shard_map.97 = (bf16[2,137,8,1280]{3,2,1,0:T(8,128)(2,1)}, bf16[128,11008]{1,0:T(8,128)(2,1)}) custom-call(s32[8]{0:T(128)} %dynamic_slice.3.waves_ref, bf16[128,11008]{1,0:T(8,128)(2,1)} %bitcast.12.recv_ref, bf16[8,1280,1280]{2,1,0:T(8,128)(2,1)} %legendre_ref.3, s32[1,1280]{1,0:T(1,128)} %broadcast_in_dim.8.counts_ref, f32[137,1]{1,0:T(8,128)} %copy.17.rates_ref, ...), custom_call_target="tpu_custom_call" | custom-call | flops 7182745600 | bytes 34631680 | tf_op jit(solution)/shard_map/pallas_call | solution.py:249
  117.4 26.9 %all-to-all-done = bf16[16,8,11008]{2,1,0:T(8,128)(2,1)} async-done(((bf16[16,8,11008]{2,1,0:T(8,128)(2,1)}), bf16[16,8,11008]{2,1,0:T(8,128)(2,1)}, u32[]{:S(2)}, u32[]{:S(2)}) %all-to-all-start) | async-done | bytes 2818080 | tf_op jit(solution)/shard_map/all_to_all | solution.py:292
  144.2 4.9 %all-to-all-start.3 = ((bf16[16,8,11008]{2,1,0:T(8,128)(2,1)}), bf16[16,8,11008]{2,1,0:T(8,128)(2,1)}, u32[]{:S(2)}, u32[]{:S(2)}) async-start(bf16[16,8,11008]{2,1,0:T(8,128)(2,1)} %bitcast.31), calls=%async_computation.3 | async-start | bytes 5636096 | tf_op jit(solution)/shard_map/all_to_all | solution.py:300
  149.1 32.7 %shard_map.98 = (bf16[2,137,8,1280]{3,2,1,0:T(8,128)(2,1)}, bf16[128,11008]{1,0:T(8,128)(2,1)}) custom-call(s32[8]{0:T(128)} %dynamic_slice.3.waves_ref, bf16[128,11008]{1,0:T(8,128)(2,1)} %bitcast.5.recv_ref, bf16[8,1280,1280]{2,1,0:T(8,128)(2,1)} %legendre_ref.3, s32[1,1280]{1,0:T(1,128)} %broadcast_in_dim.8.counts_ref, ...), custom_call_target="tpu_custom_call", output_to_operand_aliasing={{0}: (7, {})} | custom-call | flops 7182745600 | bytes 34631680 | tf_op jit(solution)/shard_map/pallas_call | solution.py:249
  181.8 30.3 %all-to-all-done.3 = bf16[16,8,11008]{2,1,0:T(8,128)(2,1)} async-done(((bf16[16,8,11008]{2,1,0:T(8,128)(2,1)}), bf16[16,8,11008]{2,1,0:T(8,128)(2,1)}, u32[]{:S(2)}, u32[]{:S(2)}) %all-to-all-start.3) | async-done | bytes 2818080 | tf_op jit(solution)/shard_map/all_to_all | solution.py:300
  212.1 4.9 %all-to-all-start.2 = ((bf16[16,8,11008]{2,1,0:T(8,128)(2,1)}), bf16[16,8,11008]{2,1,0:T(8,128)(2,1)}, u32[]{:S(2)}, u32[]{:S(2)}) async-start(bf16[16,8,11008]{2,1,0:T(8,128)(2,1)} %bitcast.32), calls=%async_computation.2 | async-start | bytes 5636096 | tf_op jit(solution)/shard_map/all_to_all | solution.py:300
  217.0 5.5 %shard_map.99.refs_0_ = bf16[2,137,80,128]{3,2,1,0:T(8,128)(2,1)} custom-call(bf16[128,11008]{1,0:T(8,128)(2,1)} %bitcast.18.in_ref), custom_call_target="tpu_custom_call" | custom-call | flops 1402880 | bytes 5611520 | tf_op jit(solution)/shard_map/pallas_call | solution.py:66
  222.5 57.4 %all-to-all-done.2 = bf16[16,8,11008]{2,1,0:T(8,128)(2,1)} async-done(((bf16[16,8,11008]{2,1,0:T(8,128)(2,1)}), bf16[16,8,11008]{2,1,0:T(8,128)(2,1)}, u32[]{:S(2)}, u32[]{:S(2)}) %all-to-all-start.2) | async-done | bytes 2818080 | tf_op jit(solution)/shard_map/all_to_all | solution.py:300
  280.0 5.5 %shard_map.100 = bf16[2,137,80,128]{3,2,1,0:T(8,128)(2,1)} custom-call(bf16[128,11008]{1,0:T(8,128)(2,1)} %bitcast.16.in_ref, bf16[2,137,80,128]{3,2,1,0:T(8,128)(2,1)} %shard_map.99.refs_0_), custom_call_target="tpu_custom_call", output_to_operand_aliasing={{}: (1, {})} | custom-call | flops 1402880 | bytes 5611520 | tf_op jit(solution)/shard_map/pallas_call | solution.py:66
Async XLA Ops:
  6.6 69.5 %all-to-all-start.1 = ((bf16[16,8,11008]{2,1,0:T(8,128)(2,1)}), bf16[16,8,11008]{2,1,0:T(8,128)(2,1)}, u32[]{:S(2)}, u32[]{:S(2)}) async-start(bf16[16,8,11008]{2,1,0:T(8,128)(2,1)} %bitcast.29), calls=%async_computation.1 | async-start | bytes 5636096 | tf_op jit(solution)/shard_map/all_to_all | solution.py:292
  76.2 5.1 %copy-start.2 = (s32[1280]{0:T(1024)S(1)}, s32[1280]{0:T(1024)}, u32[]{:S(2)}) copy-start(s32[1280]{0:T(1024)} %param.10) | copy-start | bytes 15364
  76.2 5.7 %copy-start.3 = (f32[137]{0:T(256)S(1)}, f32[137]{0:T(256)}, u32[]{:S(2)}) copy-start(f32[137]{0:T(256)} %param.13) | copy-start | bytes 1648
  76.2 6.4 %copy-start = (bf16[137,137]{1,0:T(8,128)(2,1)S(1)}, bf16[137,137]{1,0:T(8,128)(2,1)}, u32[]{:S(2)}) copy-start(bf16[137,137]{1,0:T(8,128)(2,1)} %param.14) | copy-start | bytes 112618
  76.2 7.2 %copy-start.1 = (bf16[137,137]{1,0:T(8,128)(2,1)S(1)}, bf16[137,137]{1,0:T(8,128)(2,1)}, u32[]{:S(2)}) copy-start(bf16[137,137]{1,0:T(8,128)(2,1)} %param.15) | copy-start | bytes 112618
  76.2 7.9 %copy-start.4 = (s32[128]{0:T(128)S(1)}, s32[128]{0:T(128)}, u32[]{:S(2)}) copy-start(s32[128]{0:T(128)} %param.11) | copy-start | bytes 1540
  76.2 68.0 %all-to-all-start = ((bf16[16,8,11008]{2,1,0:T(8,128)(2,1)}), bf16[16,8,11008]{2,1,0:T(8,128)(2,1)}, u32[]{:S(2)}, u32[]{:S(2)}) async-start(bf16[16,8,11008]{2,1,0:T(8,128)(2,1)} %bitcast.28), calls=%async_computation | async-start | bytes 5636096 | tf_op jit(solution)/shard_map/all_to_all | solution.py:292
  144.2 67.9 %all-to-all-start.3 = ((bf16[16,8,11008]{2,1,0:T(8,128)(2,1)}), bf16[16,8,11008]{2,1,0:T(8,128)(2,1)}, u32[]{:S(2)}, u32[]{:S(2)}) async-start(bf16[16,8,11008]{2,1,0:T(8,128)(2,1)} %bitcast.31), calls=%async_computation.3 | async-start | bytes 5636096 | tf_op jit(solution)/shard_map/all_to_all | solution.py:300
  212.1 67.9 %all-to-all-start.2 = ((bf16[16,8,11008]{2,1,0:T(8,128)(2,1)}), bf16[16,8,11008]{2,1,0:T(8,128)(2,1)}, u32[]{:S(2)}, u32[]{:S(2)}) async-start(bf16[16,8,11008]{2,1,0:T(8,128)(2,1)} %bitcast.32), calls=%async_computation.2 | async-start | bytes 5636096 | tf_op jit(solution)/shard_map/all_to_all | solution.py:300

commit v8 on v3

--- a/solution.py
+++ b/solution.py
@@ -10,7 +10,7 @@
 
 NMAX = 2559
 VMEM_BYTES = 62 * 1024 * 1024
-GROUP = 48
+GROUPS = 2
 LANES = 128
 
 
@@ -21,20 +21,64 @@
     return value.reshape(group * lat_dev, slots).astype(jnp.bfloat16)
 
 
-def pack_body(north_ref, south_ref, out_ref):
-    summed = north_ref[0].astype(jnp.float32) + south_ref[0].astype(jnp.float32)
-    out_ref[...] = flat_rows(summed.astype(jnp.bfloat16)).T
+def pieces(levels, lat_dev, width):
+    group = GROUPS * group_size(lat_dev)
+    out = []
+    for first in range(0, levels, group):
+        lane = first * lat_dev
+        count = min(group, levels - first)
+        out.append((first, count, lane, min(group * lat_dev, width - lane)))
+    return out
+
+
+def pack_body(north_ref, south_ref, out_ref, north_buf, south_buf, out_buf, in_sems, out_sems, *, part):
+    _, levels, lat_dev, slots = north_ref.shape
+    cut = pieces(levels, lat_dev, out_ref.shape[1])
+    group = cut[0][1]
+    loads, stores = [], []
+    for i, (first, count, _, _) in enumerate(cut):
+        some = pl.ds(first, count)
+        loads.append(
+            [
+                pltpu.make_async_copy(ref.at[part, some], buf.at[some], in_sems.at[j, i])
+                for j, (ref, buf) in enumerate([(north_ref, north_buf), (south_ref, south_buf)])
+            ]
+        )
+        for load in loads[-1]:
+            load.start()
+    for buf in (north_buf, south_buf):
+        if buf.shape[0] > levels:
+            buf[levels:] = jnp.zeros((buf.shape[0] - levels, lat_dev, slots), buf.dtype)
+    for i, (first, _, lane, lanes) in enumerate(cut):
+        for load in loads[i]:
+            load.wait()
+        summed = north_buf[first : first + group] + south_buf[first : first + group]
+        out_buf[:, lane : lane + lanes] = flat_rows(summed).T[:, :lanes]
+        some = pl.ds(lane, lanes)
+        stores.append(pltpu.make_async_copy(out_buf.at[:, some], out_ref.at[:, some], out_sems.at[i]))
+        stores[-1].start()
+    for store in stores:
+        store.wait()
 
 
 def pack(part, north, south):
     _, levels, lat_dev, slots = north.shape
-    rows = pl.BlockSpec((1, GROUP, lat_dev, slots), lambda i: (part, i, 0, 0))
+    width = pl.cdiv(levels * lat_dev, LANES) * LANES
+    cut = pieces(levels, lat_dev, width)
+    anywhere = pl.BlockSpec(memory_space=pl.ANY)
+    rows = pltpu.VMEM((len(cut) * cut[0][1], lat_dev, slots), jnp.bfloat16)
     return pl.pallas_call(
-        pack_body,
-        grid=(pl.cdiv(levels, GROUP),),
-        in_specs=[rows, rows],
-        out_specs=pl.BlockSpec((slots, GROUP * lat_dev), lambda i: (0, i)),
-        out_shape=jax.ShapeDtypeStruct((slots, pl.cdiv(levels * lat_dev, LANES) * LANES), jnp.bfloat16),
+        functools.partial(pack_body, part=part),
+        in_specs=[anywhere, anywhere],
+        out_specs=anywhere,
+        out_shape=jax.ShapeDtypeStruct((slots, width), jnp.bfloat16),
+        scratch_shapes=[
+            rows,
+            rows,
+            pltpu.VMEM((slots, width), jnp.bfloat16),
+            pltpu.SemaphoreType.DMA((2, len(cut))),
+            pltpu.SemaphoreType.DMA((len(cut),)),
+        ],
         compiler_params=pltpu.CompilerParams(vmem_limit_bytes=VMEM_BYTES),
         cost_estimate=pl.CostEstimate(
             flops=2 * levels * lat_dev * slots,
@@ -44,31 +88,46 @@
     )(north, south)
 
 
-def unpack_body(in_ref, *refs):
-    out_ref = refs[-1]
-    _, group, lat_dev, slots = out_ref.shape
-    rows = in_ref[...].T
-    if lat_dev % 16:
-        rows = rows.astype(jnp.float32)
-    out_ref[0] = rows.reshape(group, lat_dev, slots).astype(jnp.bfloat16)
+def unpack_body(in_ref, *refs, part):
+    out_ref, in_buf, out_buf, in_sems, out_sems = refs[-5:]
+    levels, lat_dev, slots = out_buf.shape
+    cut = pieces(levels, lat_dev, in_ref.shape[1])
+    loads, stores = [], []
+    for i, (_, _, lane, lanes) in enumerate(cut):
+        some = pl.ds(lane, lanes)
+        loads.append(pltpu.make_async_copy(in_ref.at[:, some], in_buf.at[:, some], in_sems.at[i]))
+        loads[-1].start()
+    for i, (first, count, lane, lanes) in enumerate(cut):
+        loads[i].wait()
+        rows = in_buf[:, lane : lane + lanes].T
+        if lat_dev % 16:
+            rows = rows.astype(jnp.float32)
+        rows = rows[: count * lat_dev].reshape(count, lat_dev, slots)
+        out_buf[first : first + count] = rows.astype(jnp.bfloat16)
+        some = pl.ds(first, count)
+        stores.append(pltpu.make_async_copy(out_buf.at[some], out_ref.at[part, some], out_sems.at[i]))
+        stores[-1].start()
+    for store in stores:
+        store.wait()
 
 
 def unpack(part, parts, levels, lat_dev, received, earlier):
-    slots = received.shape[0]
-    in_specs = [pl.BlockSpec((slots, GROUP * lat_dev), lambda i: (0, i))]
-    operands = [received]
-    aliases = {}
-    if earlier is not None:
-        in_specs.append(pl.BlockSpec(memory_space=pl.ANY))
-        operands.append(earlier)
-        aliases = {1: 0}
+    slots, width = received.shape
+    cut = pieces(levels, lat_dev, width)
+    anywhere = pl.BlockSpec(memory_space=pl.ANY)
+    operands = [received] if earlier is None else [received, earlier]
     return pl.pallas_call(
-        unpack_body,
-        grid=(pl.cdiv(levels, GROUP),),
-        in_specs=in_specs,
-        out_specs=pl.BlockSpec((1, GROUP, lat_dev, slots), lambda i: (part, i, 0, 0)),
+        functools.partial(unpack_body, part=part),
+        in_specs=[anywhere] * len(operands),
+        out_specs=anywhere,
         out_shape=jax.ShapeDtypeStruct((parts, levels, lat_dev, slots), jnp.bfloat16),
-        input_output_aliases=aliases,
+        input_output_aliases={} if earlier is None else {1: 0},
+        scratch_shapes=[
+            pltpu.VMEM((slots, width), jnp.bfloat16),
+            pltpu.VMEM((levels, lat_dev, slots), jnp.bfloat16),
+            pltpu.SemaphoreType.DMA((len(cut),)),
+            pltpu.SemaphoreType.DMA((len(cut),)),
+        ],
         compiler_params=pltpu.CompilerParams(vmem_limit_bytes=VMEM_BYTES),
         cost_estimate=pl.CostEstimate(
             flops=levels * lat_dev * slots,

time: 284 us -> 282 us (level)
  Pallas kernels: 84.8 us -> 79.9 us
  waiting for transfers between devices: 173 us -> 176 us
    pallas_call x4, Pallas kernels: 19.5 us -> 14.6 us  [the longest x2 8.57 us: pack(): pl.pallas_call(functools.partial(pack_body, part=part), in_specs=[anywher...]
where the time goes in v8:
time: 282 us; the launch traced here: 281 us
  waiting for transfers between devices  176 us (62%)
  Pallas kernels  79.9 us (28%)
  starting transfers between devices  21.4 us (8%)
  local copies, waits for them, and re-layouts  3.48 us (1%)
    all_to_all x2, waiting for transfers between devices, per_device(): returned.append(exchange(rows))  90.2 us
    all_to_all x2, waiting for transfers between devices, per_device(): columns = [exchange(pack(part, north, south)) for part in range(parts)]  85.6 us
    pallas_call x2, Pallas kernels, spectral_step(): pl.pallas_call(step_body, grid_spec=pltpu.PrefetchScalarGridSpec(num_scal...  65.3 us
    all_to_all x2, starting transfers between devices, per_device(): columns = [exchange(pack(part, north, south)) for part in range(parts)]  11.6 us
    all_to_all x2, starting transfers between devices, per_device(): returned.append(exchange(rows))  9.82 us
    pallas_call x2, Pallas kernels, pack(): pl.pallas_call(functools.partial(pack_body, part=part), in_specs=[anywher...  8.57 us
    pallas_call x2, Pallas kernels, unpack(): pl.pallas_call(functools.partial(unpack_body, part=part), in_specs=[anywh...  6.07 us
  transfers between devices with their start and end apart: 4, of which 4 were waited for; matrix products, arithmetic and copies ran while one was open for 1% of the time, Pallas kernels for 26%

profile of v8, /device:TPU:13, one launch (start us, length us, event | category | flops | bytes accessed | tf_op | source)
XLA Modules:
  0.0 281.3 jit_solution(16624829731162601209)
XLA Ops:
  0.6 4.3 %shard_map.96 = bf16[128,11008]{1,0:T(8,128)(2,1)} custom-call(bf16[2,137,80,128]{3,2,1,0:T(8,128)(2,1)} %bitcast.24, bf16[2,137,80,128]{3,2,1,0:T(8,128)(2,1)} %bitcast.26), custom_call_target="tpu_custom_call" | custom-call | flops 2805760 | bytes 8417280 | tf_op jit(solution)/shard_map/pallas_call | solution.py:70
  4.9 6.6 %all-to-all-start.1 = ((bf16[16,8,11008]{2,1,0:T(8,128)(2,1)}), bf16[16,8,11008]{2,1,0:T(8,128)(2,1)}, u32[]{:S(2)}, u32[]{:S(2)}) async-start(bf16[16,8,11008]{2,1,0:T(8,128)(2,1)} %bitcast.29), calls=%async_computation.1 | async-start | bytes 5636096 | tf_op jit(solution)/shard_map/all_to_all | solution.py:350
  11.5 4.3 %shard_map.95 = bf16[128,11008]{1,0:T(8,128)(2,1)} custom-call(bf16[2,137,80,128]{3,2,1,0:T(8,128)(2,1)} %bitcast.25, bf16[2,137,80,128]{3,2,1,0:T(8,128)(2,1)} %bitcast.27), custom_call_target="tpu_custom_call" | custom-call | flops 2805760 | bytes 8417280 | tf_op jit(solution)/shard_map/pallas_call | solution.py:70
  15.8 58.7 %all-to-all-done.1 = bf16[16,8,11008]{2,1,0:T(8,128)(2,1)} async-done(((bf16[16,8,11008]{2,1,0:T(8,128)(2,1)}), bf16[16,8,11008]{2,1,0:T(8,128)(2,1)}, u32[]{:S(2)}, u32[]{:S(2)}) %all-to-all-start.1) | async-done | bytes 2818080 | tf_op jit(solution)/shard_map/all_to_all | solution.py:350
  74.5 0.0 copy-start.2
  74.5 0.0 copy-start.3
  74.5 0.0 copy-start
  74.5 0.0 copy-start.1
  74.5 0.0 copy-start.4
  74.5 5.1 %all-to-all-start = ((bf16[16,8,11008]{2,1,0:T(8,128)(2,1)}), bf16[16,8,11008]{2,1,0:T(8,128)(2,1)}, u32[]{:S(2)}, u32[]{:S(2)}) async-start(bf16[16,8,11008]{2,1,0:T(8,128)(2,1)} %bitcast.28), calls=%async_computation | async-start | bytes 5636096 | tf_op jit(solution)/shard_map/all_to_all | solution.py:350
  79.5 0.0 copy-done.2
  79.5 0.6 broadcast_in_dim.8.counts_ref
  80.1 0.0 copy-done.3
  80.1 0.7 copy.17.rates_ref
  80.9 0.0 copy-done
  80.9 0.7 copy.14
  81.6 0.0 copy-done.1
  81.6 0.7 copy.15
  82.4 0.0 copy-done.4
  82.4 0.7 dynamic_slice.3.waves_ref
  83.0 32.6 %shard_map.97 = (bf16[2,137,8,1280]{3,2,1,0:T(8,128)(2,1)}, bf16[128,11008]{1,0:T(8,128)(2,1)}) custom-call(s32[8]{0:T(128)} %dynamic_slice.3.waves_ref, bf16[128,11008]{1,0:T(8,128)(2,1)} %bitcast.12.recv_ref, bf16[8,1280,1280]{2,1,0:T(8,128)(2,1)} %legendre_ref.3, s32[1,1280]{1,0:T(1,128)} %broadcast_in_dim.8.counts_ref, f32[137,1]{1,0:T(8,128)} %copy.17.rates_ref, ...), custom_call_target="tpu_custom_call" | custom-call | flops 7182745600 | bytes 34631680 | tf_op jit(solution)/shard_map/pallas_call | solution.py:307
  115.6 26.9 %all-to-all-done = bf16[16,8,11008]{2,1,0:T(8,128)(2,1)} async-done(((bf16[16,8,11008]{2,1,0:T(8,128)(2,1)}), bf16[16,8,11008]{2,1,0:T(8,128)(2,1)}, u32[]{:S(2)}, u32[]{:S(2)}) %all-to-all-start) | async-done | bytes 2818080 | tf_op jit(solution)/shard_map/all_to_all | solution.py:350
  142.5 4.9 %all-to-all-start.3 = ((bf16[16,8,11008]{2,1,0:T(8,128)(2,1)}), bf16[16,8,11008]{2,1,0:T(8,128)(2,1)}, u32[]{:S(2)}, u32[]{:S(2)}) async-start(bf16[16,8,11008]{2,1,0:T(8,128)(2,1)} %bitcast.31), calls=%async_computation.3 | async-start | bytes 5636096 | tf_op jit(solution)/shard_map/all_to_all | solution.py:358
  147.4 32.7 %shard_map.98 = (bf16[2,137,8,1280]{3,2,1,0:T(8,128)(2,1)}, bf16[128,11008]{1,0:T(8,128)(2,1)}) custom-call(s32[8]{0:T(128)} %dynamic_slice.3.waves_ref, bf16[128,11008]{1,0:T(8,128)(2,1)} %bitcast.5.recv_ref, bf16[8,1280,1280]{2,1,0:T(8,128)(2,1)} %legendre_ref.3, s32[1,1280]{1,0:T(1,128)} %broadcast_in_dim.8.counts_ref, ...), custom_call_target="tpu_custom_call", output_to_operand_aliasing={{0}: (7, {})} | custom-call | flops 7182745600 | bytes 34631680 | tf_op jit(solution)/shard_map/pallas_call | solution.py:307
  180.1 30.3 %all-to-all-done.3 = bf16[16,8,11008]{2,1,0:T(8,128)(2,1)} async-done(((bf16[16,8,11008]{2,1,0:T(8,128)(2,1)}), bf16[16,8,11008]{2,1,0:T(8,128)(2,1)}, u32[]{:S(2)}, u32[]{:S(2)}) %all-to-all-start.3) | async-done | bytes 2818080 | tf_op jit(solution)/shard_map/all_to_all | solution.py:358
  210.4 4.9 %all-to-all-start.2 = ((bf16[16,8,11008]{2,1,0:T(8,128)(2,1)}), bf16[16,8,11008]{2,1,0:T(8,128)(2,1)}, u32[]{:S(2)}, u32[]{:S(2)}) async-start(bf16[16,8,11008]{2,1,0:T(8,128)(2,1)} %bitcast.32), calls=%async_computation.2 | async-start | bytes 5636096 | tf_op jit(solution)/shard_map/all_to_all | solution.py:358
  215.3 3.0 %shard_map.99.refs_0_ = bf16[2,137,80,128]{3,2,1,0:T(8,128)(2,1)} custom-call(bf16[128,11008]{1,0:T(8,128)(2,1)} %bitcast.18.in_ref), custom_call_target="tpu_custom_call" | custom-call | flops 1402880 | bytes 5611520 | tf_op jit(solution)/shard_map/pallas_call | solution.py:119
  218.3 59.9 %all-to-all-done.2 = bf16[16,8,11008]{2,1,0:T(8,128)(2,1)} async-done(((bf16[16,8,11008]{2,1,0:T(8,128)(2,1)}), bf16[16,8,11008]{2,1,0:T(8,128)(2,1)}, u32[]{:S(2)}, u32[]{:S(2)}) %all-to-all-start.2) | async-done | bytes 2818080 | tf_op jit(solution)/shard_map/all_to_all | solution.py:358
  278.3 3.0 %shard_map.100 = bf16[2,137,80,128]{3,2,1,0:T(8,128)(2,1)} custom-call(bf16[128,11008]{1,0:T(8,128)(2,1)} %bitcast.16.in_ref, bf16[2,137,80,128]{3,2,1,0:T(8,128)(2,1)} %shard_map.99.refs_0_), custom_call_target="tpu_custom_call", output_to_operand_aliasing={{}: (1, {})} | custom-call | flops 1402880 | bytes 5611520 | tf_op jit(solution)/shard_map/pallas_call | solution.py:119
Async XLA Ops:
  4.9 69.5 %all-to-all-start.1 = ((bf16[16,8,11008]{2,1,0:T(8,128)(2,1)}), bf16[16,8,11008]{2,1,0:T(8,128)(2,1)}, u32[]{:S(2)}, u32[]{:S(2)}) async-start(bf16[16,8,11008]{2,1,0:T(8,128)(2,1)} %bitcast.29), calls=%async_computation.1 | async-start | bytes 5636096 | tf_op jit(solution)/shard_map/all_to_all | solution.py:350
  74.5 5.1 %copy-start.2 = (s32[1280]{0:T(1024)S(1)}, s32[1280]{0:T(1024)}, u32[]{:S(2)}) copy-start(s32[1280]{0:T(1024)} %param.10) | copy-start | bytes 15364
  74.5 5.7 %copy-start.3 = (f32[137]{0:T(256)S(1)}, f32[137]{0:T(256)}, u32[]{:S(2)}) copy-start(f32[137]{0:T(256)} %param.13) | copy-start | bytes 1648
  74.5 6.4 %copy-start = (bf16[137,137]{1,0:T(8,128)(2,1)S(1)}, bf16[137,137]{1,0:T(8,128)(2,1)}, u32[]{:S(2)}) copy-start(bf16[137,137]{1,0:T(8,128)(2,1)} %param.14) | copy-start | bytes 112618
  74.5 7.2 %copy-start.1 = (bf16[137,137]{1,0:T(8,128)(2,1)S(1)}, bf16[137,137]{1,0:T(8,128)(2,1)}, u32[]{:S(2)}) copy-start(bf16[137,137]{1,0:T(8,128)(2,1)} %param.15) | copy-start | bytes 112618
  74.5 7.9 %copy-start.4 = (s32[128]{0:T(128)S(1)}, s32[128]{0:T(128)}, u32[]{:S(2)}) copy-start(s32[128]{0:T(128)} %param.11) | copy-start | bytes 1540
  74.5 68.0 %all-to-all-start = ((bf16[16,8,11008]{2,1,0:T(8,128)(2,1)}), bf16[16,8,11008]{2,1,0:T(8,128)(2,1)}, u32[]{:S(2)}, u32[]{:S(2)}) async-start(bf16[16,8,11008]{2,1,0:T(8,128)(2,1)} %bitcast.28), calls=%async_computation | async-start | bytes 5636096 | tf_op jit(solution)/shard_map/all_to_all | solution.py:350
  142.5 67.9 %all-to-all-start.3 = ((bf16[16,8,11008]{2,1,0:T(8,128)(2,1)}), bf16[16,8,11008]{2,1,0:T(8,128)(2,1)}, u32[]{:S(2)}, u32[]{:S(2)}) async-start(bf16[16,8,11008]{2,1,0:T(8,128)(2,1)} %bitcast.31), calls=%async_computation.3 | async-start | bytes 5636096 | tf_op jit(solution)/shard_map/all_to_all | solution.py:358
  210.4 67.9 %all-to-all-start.2 = ((bf16[16,8,11008]{2,1,0:T(8,128)(2,1)}), bf16[16,8,11008]{2,1,0:T(8,128)(2,1)}, u32[]{:S(2)}, u32[]{:S(2)}) async-start(bf16[16,8,11008]{2,1,0:T(8,128)(2,1)} %bitcast.32), calls=%async_computation.2 | async-start | bytes 5636096 | tf_op jit(solution)/shard_map/all_to_all | solution.py:358

commit v9 on v8

--- a/solution.py
+++ b/solution.py
@@ -11,6 +11,7 @@
 NMAX = 2559
 VMEM_BYTES = 62 * 1024 * 1024
 GROUPS = 2
+AHEAD = 3
 LANES = 128
 
 
@@ -44,14 +45,16 @@
                 for j, (ref, buf) in enumerate([(north_ref, north_buf), (south_ref, south_buf)])
             ]
         )
-        for load in loads[-1]:
-            load.start()
+    for load in sum(loads[:AHEAD], []):
+        load.start()
     for buf in (north_buf, south_buf):
         if buf.shape[0] > levels:
             buf[levels:] = jnp.zeros((buf.shape[0] - levels, lat_dev, slots), buf.dtype)
     for i, (first, _, lane, lanes) in enumerate(cut):
         for load in loads[i]:
             load.wait()
+        for load in sum(loads[i + AHEAD : i + AHEAD + 1], []):
+            load.start()
         summed = north_buf[first : first + group] + south_buf[first : first + group]
         out_buf[:, lane : lane + lanes] = flat_rows(summed).T[:, :lanes]
         some = pl.ds(lane, lanes)
@@ -96,9 +99,12 @@
     for i, (_, _, lane, lanes) in enumerate(cut):
         some = pl.ds(lane, lanes)
         loads.append(pltpu.make_async_copy(in_ref.at[:, some], in_buf.at[:, some], in_sems.at[i]))
-        loads[-1].start()
+    for load in loads[:AHEAD]:
+        load.start()
     for i, (first, count, lane, lanes) in enumerate(cut):
         loads[i].wait()
+        for load in loads[i + AHEAD : i + AHEAD + 1]:
+            load.start()
         rows = in_buf[:, lane : lane + lanes].T
         if lat_dev % 16:
             rows = rows.astype(jnp.float32)

time: 282 us -> 285 us (1.011)
  Pallas kernels: 79.9 us -> 84.9 us
  waiting for transfers between devices: 176 us -> 173 us
    pallas_call x2, Pallas kernels: 6.07 us -> 9.03 us  [unpack(): pl.pallas_call(functools.partial(unpack_body, part=part), in_specs=[anywh...]
where the time goes in v9:
time: 285 us; the launch traced here: 284 us
  waiting for transfers between devices  173 us (61%)
  Pallas kernels  84.9 us (30%)
  starting transfers between devices  21.4 us (8%)
  local copies, waits for them, and re-layouts  3.48 us (1%)
    all_to_all x2, waiting for transfers between devices, per_device(): returned.append(exchange(rows))  88.7 us
    all_to_all x2, waiting for transfers between devices, per_device(): columns = [exchange(pack(part, north, south)) for part in range(parts)]  84.6 us
    pallas_call x2, Pallas kernels, spectral_step(): pl.pallas_call(step_body, grid_spec=pltpu.PrefetchScalarGridSpec(num_scal...  65.3 us
    all_to_all x2, starting transfers between devices, per_device(): columns = [exchange(pack(part, north, south)) for part in range(parts)]  11.6 us
    pallas_call x2, Pallas kernels, pack(): pl.pallas_call(functools.partial(pack_body, part=part), in_specs=[anywher...  10.5 us
    all_to_all x2, starting transfers between devices, per_device(): returned.append(exchange(rows))  9.82 us
    pallas_call x2, Pallas kernels, unpack(): pl.pallas_call(functools.partial(unpack_body, part=part), in_specs=[anywh...  9.03 us
  transfers between devices with their start and end apart: 4, of which 4 were waited for; matrix products, arithmetic and copies ran while one was open for 1% of the time, Pallas kernels for 26%

profile of v9, /device:TPU:13, one launch (start us, length us, event | category | flops | bytes accessed | tf_op | source)
XLA Modules:
  0.0 283.8 jit_solution(537120502950195529)
XLA Ops:
  0.6 5.3 %shard_map.96 = bf16[128,11008]{1,0:T(8,128)(2,1)} custom-call(bf16[2,137,80,128]{3,2,1,0:T(8,128)(2,1)} %bitcast.24, bf16[2,137,80,128]{3,2,1,0:T(8,128)(2,1)} %bitcast.26), custom_call_target="tpu_custom_call" | custom-call | flops 2805760 | bytes 8417280 | tf_op jit(solution)/shard_map/pallas_call | solution.py:73
  5.9 6.6 %all-to-all-start.1 = ((bf16[16,8,11008]{2,1,0:T(8,128)(2,1)}), bf16[16,8,11008]{2,1,0:T(8,128)(2,1)}, u32[]{:S(2)}, u32[]{:S(2)}) async-start(bf16[16,8,11008]{2,1,0:T(8,128)(2,1)} %bitcast.29), calls=%async_computation.1 | async-start | bytes 5636096 | tf_op jit(solution)/shard_map/all_to_all | solution.py:356
  12.5 5.3 %shard_map.95 = bf16[128,11008]{1,0:T(8,128)(2,1)} custom-call(bf16[2,137,80,128]{3,2,1,0:T(8,128)(2,1)} %bitcast.25, bf16[2,137,80,128]{3,2,1,0:T(8,128)(2,1)} %bitcast.27), custom_call_target="tpu_custom_call" | custom-call | flops 2805760 | bytes 8417280 | tf_op jit(solution)/shard_map/pallas_call | solution.py:73
  17.7 57.7 %all-to-all-done.1 = bf16[16,8,11008]{2,1,0:T(8,128)(2,1)} async-done(((bf16[16,8,11008]{2,1,0:T(8,128)(2,1)}), bf16[16,8,11008]{2,1,0:T(8,128)(2,1)}, u32[]{:S(2)}, u32[]{:S(2)}) %all-to-all-start.1) | async-done | bytes 2818080 | tf_op jit(solution)/shard_map/all_to_all | solution.py:356
  75.4 0.0 copy-start.2
  75.4 0.0 copy-start.3
  75.4 0.0 copy-start
  75.5 0.0 copy-start.1
  75.5 0.0 copy-start.4
  75.5 5.1 %all-to-all-start = ((bf16[16,8,11008]{2,1,0:T(8,128)(2,1)}), bf16[16,8,11008]{2,1,0:T(8,128)(2,1)}, u32[]{:S(2)}, u32[]{:S(2)}) async-start(bf16[16,8,11008]{2,1,0:T(8,128)(2,1)} %bitcast.28), calls=%async_computation | async-start | bytes 5636096 | tf_op jit(solution)/shard_map/all_to_all | solution.py:356
  80.5 0.0 copy-done.2
  80.5 0.6 broadcast_in_dim.8.counts_ref
  81.1 0.0 copy-done.3
  81.1 0.7 copy.17.rates_ref
  81.9 0.0 copy-done
  81.9 0.7 copy.14
  82.6 0.0 copy-done.1
  82.6 0.7 copy.15
  83.3 0.0 copy-done.4
  83.3 0.7 dynamic_slice.3.waves_ref
  84.0 32.6 %shard_map.97 = (bf16[2,137,8,1280]{3,2,1,0:T(8,128)(2,1)}, bf16[128,11008]{1,0:T(8,128)(2,1)}) custom-call(s32[8]{0:T(128)} %dynamic_slice.3.waves_ref, bf16[128,11008]{1,0:T(8,128)(2,1)} %bitcast.12.recv_ref, bf16[8,1280,1280]{2,1,0:T(8,128)(2,1)} %legendre_ref.3, s32[1,1280]{1,0:T(1,128)} %broadcast_in_dim.8.counts_ref, f32[137,1]{1,0:T(8,128)} %copy.17.rates_ref, ...), custom_call_target="tpu_custom_call" | custom-call | flops 7182745600 | bytes 34631680 | tf_op jit(solution)/shard_map/pallas_call | solution.py:313
  116.6 26.9 %all-to-all-done = bf16[16,8,11008]{2,1,0:T(8,128)(2,1)} async-done(((bf16[16,8,11008]{2,1,0:T(8,128)(2,1)}), bf16[16,8,11008]{2,1,0:T(8,128)(2,1)}, u32[]{:S(2)}, u32[]{:S(2)}) %all-to-all-start) | async-done | bytes 2818080 | tf_op jit(solution)/shard_map/all_to_all | solution.py:356
  143.5 4.9 %all-to-all-start.3 = ((bf16[16,8,11008]{2,1,0:T(8,128)(2,1)}), bf16[16,8,11008]{2,1,0:T(8,128)(2,1)}, u32[]{:S(2)}, u32[]{:S(2)}) async-start(bf16[16,8,11008]{2,1,0:T(8,128)(2,1)} %bitcast.31), calls=%async_computation.3 | async-start | bytes 5636096 | tf_op jit(solution)/shard_map/all_to_all | solution.py:364
  148.4 32.7 %shard_map.98 = (bf16[2,137,8,1280]{3,2,1,0:T(8,128)(2,1)}, bf16[128,11008]{1,0:T(8,128)(2,1)}) custom-call(s32[8]{0:T(128)} %dynamic_slice.3.waves_ref, bf16[128,11008]{1,0:T(8,128)(2,1)} %bitcast.5.recv_ref, bf16[8,1280,1280]{2,1,0:T(8,128)(2,1)} %legendre_ref.3, s32[1,1280]{1,0:T(1,128)} %broadcast_in_dim.8.counts_ref, ...), custom_call_target="tpu_custom_call", output_to_operand_aliasing={{0}: (7, {})} | custom-call | flops 7182745600 | bytes 34631680 | tf_op jit(solution)/shard_map/pallas_call | solution.py:313
  181.1 30.3 %all-to-all-done.3 = bf16[16,8,11008]{2,1,0:T(8,128)(2,1)} async-done(((bf16[16,8,11008]{2,1,0:T(8,128)(2,1)}), bf16[16,8,11008]{2,1,0:T(8,128)(2,1)}, u32[]{:S(2)}, u32[]{:S(2)}) %all-to-all-start.3) | async-done | bytes 2818080 | tf_op jit(solution)/shard_map/all_to_all | solution.py:364
  211.4 4.9 %all-to-all-start.2 = ((bf16[16,8,11008]{2,1,0:T(8,128)(2,1)}), bf16[16,8,11008]{2,1,0:T(8,128)(2,1)}, u32[]{:S(2)}, u32[]{:S(2)}) async-start(bf16[16,8,11008]{2,1,0:T(8,128)(2,1)} %bitcast.32), calls=%async_computation.2 | async-start | bytes 5636096 | tf_op jit(solution)/shard_map/all_to_all | solution.py:364
  216.3 4.5 %shard_map.99.refs_0_ = bf16[2,137,80,128]{3,2,1,0:T(8,128)(2,1)} custom-call(bf16[128,11008]{1,0:T(8,128)(2,1)} %bitcast.18.in_ref), custom_call_target="tpu_custom_call" | custom-call | flops 1402880 | bytes 5611520 | tf_op jit(solution)/shard_map/pallas_call | solution.py:125
  220.8 58.4 %all-to-all-done.2 = bf16[16,8,11008]{2,1,0:T(8,128)(2,1)} async-done(((bf16[16,8,11008]{2,1,0:T(8,128)(2,1)}), bf16[16,8,11008]{2,1,0:T(8,128)(2,1)}, u32[]{:S(2)}, u32[]{:S(2)}) %all-to-all-start.2) | async-done | bytes 2818080 | tf_op jit(solution)/shard_map/all_to_all | solution.py:364
  279.3 4.5 %shard_map.100 = bf16[2,137,80,128]{3,2,1,0:T(8,128)(2,1)} custom-call(bf16[128,11008]{1,0:T(8,128)(2,1)} %bitcast.16.in_ref, bf16[2,137,80,128]{3,2,1,0:T(8,128)(2,1)} %shard_map.99.refs_0_), custom_call_target="tpu_custom_call", output_to_operand_aliasing={{}: (1, {})} | custom-call | flops 1402880 | bytes 5611520 | tf_op jit(solution)/shard_map/pallas_call | solution.py:125
Async XLA Ops:
  5.9 69.5 %all-to-all-start.1 = ((bf16[16,8,11008]{2,1,0:T(8,128)(2,1)}), bf16[16,8,11008]{2,1,0:T(8,128)(2,1)}, u32[]{:S(2)}, u32[]{:S(2)}) async-start(bf16[16,8,11008]{2,1,0:T(8,128)(2,1)} %bitcast.29), calls=%async_computation.1 | async-start | bytes 5636096 | tf_op jit(solution)/shard_map/all_to_all | solution.py:356
  75.4 5.1 %copy-start.2 = (s32[1280]{0:T(1024)S(1)}, s32[1280]{0:T(1024)}, u32[]{:S(2)}) copy-start(s32[1280]{0:T(1024)} %param.10) | copy-start | bytes 15364
  75.4 5.7 %copy-start.3 = (f32[137]{0:T(256)S(1)}, f32[137]{0:T(256)}, u32[]{:S(2)}) copy-start(f32[137]{0:T(256)} %param.13) | copy-start | bytes 1648
  75.4 6.4 %copy-start = (bf16[137,137]{1,0:T(8,128)(2,1)S(1)}, bf16[137,137]{1,0:T(8,128)(2,1)}, u32[]{:S(2)}) copy-start(bf16[137,137]{1,0:T(8,128)(2,1)} %param.14) | copy-start | bytes 112618
  75.5 7.2 %copy-start.1 = (bf16[137,137]{1,0:T(8,128)(2,1)S(1)}, bf16[137,137]{1,0:T(8,128)(2,1)}, u32[]{:S(2)}) copy-start(bf16[137,137]{1,0:T(8,128)(2,1)} %param.15) | copy-start | bytes 112618
  75.5 7.9 %copy-start.4 = (s32[128]{0:T(128)S(1)}, s32[128]{0:T(128)}, u32[]{:S(2)}) copy-start(s32[128]{0:T(128)} %param.11) | copy-start | bytes 1540
  75.5 68.0 %all-to-all-start = ((bf16[16,8,11008]{2,1,0:T(8,128)(2,1)}), bf16[16,8,11008]{2,1,0:T(8,128)(2,1)}, u32[]{:S(2)}, u32[]{:S(2)}) async-start(bf16[16,8,11008]{2,1,0:T(8,128)(2,1)} %bitcast.28), calls=%async_computation | async-start | bytes 5636096 | tf_op jit(solution)/shard_map/all_to_all | solution.py:356
  143.5 67.9 %all-to-all-start.3 = ((bf16[16,8,11008]{2,1,0:T(8,128)(2,1)}), bf16[16,8,11008]{2,1,0:T(8,128)(2,1)}, u32[]{:S(2)}, u32[]{:S(2)}) async-start(bf16[16,8,11008]{2,1,0:T(8,128)(2,1)} %bitcast.31), calls=%async_computation.3 | async-start | bytes 5636096 | tf_op jit(solution)/shard_map/all_to_all | solution.py:364
  211.4 67.9 %all-to-all-start.2 = ((bf16[16,8,11008]{2,1,0:T(8,128)(2,1)}), bf16[16,8,11008]{2,1,0:T(8,128)(2,1)}, u32[]{:S(2)}, u32[]{:S(2)}) async-start(bf16[16,8,11008]{2,1,0:T(8,128)(2,1)} %bitcast.32), calls=%async_computation.2 | async-start | bytes 5636096 | tf_op jit(solution)/shard_map/all_to_all | solution.py:364

commit v10 on v8

--- a/solution.py
+++ b/solution.py
@@ -10,7 +10,7 @@
 
 NMAX = 2559
 VMEM_BYTES = 62 * 1024 * 1024
-GROUPS = 2
+GROUPS = 1
 LANES = 128
 
 

time: 282 us -> 283 us (level)
  no operation moved by 1% of the time
where the time goes in v10:
time: 283 us; the launch traced here: 282 us
  waiting for transfers between devices  175 us (62%)
  Pallas kernels  82 us (29%)
  starting transfers between devices  21.4 us (8%)
  local copies, waits for them, and re-layouts  3.48 us (1%)
    all_to_all x2, waiting for transfers between devices, per_device(): returned.append(exchange(rows))  89.6 us
    all_to_all x2, waiting for transfers between devices, per_device(): columns = [exchange(pack(part, north, south)) for part in range(parts)]  85.2 us
    pallas_call x2, Pallas kernels, spectral_step(): pl.pallas_call(step_body, grid_spec=pltpu.PrefetchScalarGridSpec(num_scal...  65.3 us
    all_to_all x2, starting transfers between devices, per_device(): columns = [exchange(pack(part, north, south)) for part in range(parts)]  11.6 us
    all_to_all x2, starting transfers between devices, per_device(): returned.append(exchange(rows))  9.82 us
    pallas_call x2, Pallas kernels, pack(): pl.pallas_call(functools.partial(pack_body, part=part), in_specs=[anywher...  9.3 us
    pallas_call x2, Pallas kernels, unpack(): pl.pallas_call(functools.partial(unpack_body, part=part), in_specs=[anywh...  7.41 us
  transfers between devices with their start and end apart: 4, of which 4 were waited for; matrix products, arithmetic and copies ran while one was open for 1% of the time, Pallas kernels for 26%

profile of v10, /device:TPU:13, one launch (start us, length us, event | category | flops | bytes accessed | tf_op | source)
XLA Modules:
  0.0 282.3 jit_solution(12442281370220591127)
XLA Ops:
  0.6 4.7 %shard_map.96 = bf16[128,11008]{1,0:T(8,128)(2,1)} custom-call(bf16[2,137,80,128]{3,2,1,0:T(8,128)(2,1)} %bitcast.24, bf16[2,137,80,128]{3,2,1,0:T(8,128)(2,1)} %bitcast.26), custom_call_target="tpu_custom_call" | custom-call | flops 2805760 | bytes 8417280 | tf_op jit(solution)/shard_map/pallas_call | solution.py:70
  5.3 6.6 %all-to-all-start.1 = ((bf16[16,8,11008]{2,1,0:T(8,128)(2,1)}), bf16[16,8,11008]{2,1,0:T(8,128)(2,1)}, u32[]{:S(2)}, u32[]{:S(2)}) async-start(bf16[16,8,11008]{2,1,0:T(8,128)(2,1)} %bitcast.29), calls=%async_computation.1 | async-start | bytes 5636096 | tf_op jit(solution)/shard_map/all_to_all | solution.py:350
  11.9 4.6 %shard_map.95 = bf16[128,11008]{1,0:T(8,128)(2,1)} custom-call(bf16[2,137,80,128]{3,2,1,0:T(8,128)(2,1)} %bitcast.25, bf16[2,137,80,128]{3,2,1,0:T(8,128)(2,1)} %bitcast.27), custom_call_target="tpu_custom_call" | custom-call | flops 2805760 | bytes 8417280 | tf_op jit(solution)/shard_map/pallas_call | solution.py:70
  16.5 58.3 %all-to-all-done.1 = bf16[16,8,11008]{2,1,0:T(8,128)(2,1)} async-done(((bf16[16,8,11008]{2,1,0:T(8,128)(2,1)}), bf16[16,8,11008]{2,1,0:T(8,128)(2,1)}, u32[]{:S(2)}, u32[]{:S(2)}) %all-to-all-start.1) | async-done | bytes 2818080 | tf_op jit(solution)/shard_map/all_to_all | solution.py:350
  74.8 0.0 copy-start.2
  74.8 0.0 copy-start.3
  74.8 0.0 copy-start
  74.8 0.0 copy-start.1
  74.8 0.0 copy-start.4
  74.9 5.1 %all-to-all-start = ((bf16[16,8,11008]{2,1,0:T(8,128)(2,1)}), bf16[16,8,11008]{2,1,0:T(8,128)(2,1)}, u32[]{:S(2)}, u32[]{:S(2)}) async-start(bf16[16,8,11008]{2,1,0:T(8,128)(2,1)} %bitcast.28), calls=%async_computation | async-start | bytes 5636096 | tf_op jit(solution)/shard_map/all_to_all | solution.py:350
  79.9 0.0 copy-done.2
  79.9 0.6 broadcast_in_dim.8.counts_ref
  80.5 0.0 copy-done.3
  80.5 0.7 copy.17.rates_ref
  81.3 0.0 copy-done
  81.3 0.7 copy.14
  82.0 0.0 copy-done.1
  82.0 0.7 copy.15
  82.7 0.0 copy-done.4
  82.7 0.7 dynamic_slice.3.waves_ref
  83.4 32.6 %shard_map.97 = (bf16[2,137,8,1280]{3,2,1,0:T(8,128)(2,1)}, bf16[128,11008]{1,0:T(8,128)(2,1)}) custom-call(s32[8]{0:T(128)} %dynamic_slice.3.waves_ref, bf16[128,11008]{1,0:T(8,128)(2,1)} %bitcast.12.recv_ref, bf16[8,1280,1280]{2,1,0:T(8,128)(2,1)} %legendre_ref.3, s32[1,1280]{1,0:T(1,128)} %broadcast_in_dim.8.counts_ref, f32[137,1]{1,0:T(8,128)} %copy.17.rates_ref, ...), custom_call_target="tpu_custom_call" | custom-call | flops 7182745600 | bytes 34631680 | tf_op jit(solution)/shard_map/pallas_call | solution.py:307
  116.0 26.9 %all-to-all-done = bf16[16,8,11008]{2,1,0:T(8,128)(2,1)} async-done(((bf16[16,8,11008]{2,1,0:T(8,128)(2,1)}), bf16[16,8,11008]{2,1,0:T(8,128)(2,1)}, u32[]{:S(2)}, u32[]{:S(2)}) %all-to-all-start) | async-done | bytes 2818080 | tf_op jit(solution)/shard_map/all_to_all | solution.py:350
  142.9 4.9 %all-to-all-start.3 = ((bf16[16,8,11008]{2,1,0:T(8,128)(2,1)}), bf16[16,8,11008]{2,1,0:T(8,128)(2,1)}, u32[]{:S(2)}, u32[]{:S(2)}) async-start(bf16[16,8,11008]{2,1,0:T(8,128)(2,1)} %bitcast.31), calls=%async_computation.3 | async-start | bytes 5636096 | tf_op jit(solution)/shard_map/all_to_all | solution.py:358
  147.8 32.7 %shard_map.98 = (bf16[2,137,8,1280]{3,2,1,0:T(8,128)(2,1)}, bf16[128,11008]{1,0:T(8,128)(2,1)}) custom-call(s32[8]{0:T(128)} %dynamic_slice.3.waves_ref, bf16[128,11008]{1,0:T(8,128)(2,1)} %bitcast.5.recv_ref, bf16[8,1280,1280]{2,1,0:T(8,128)(2,1)} %legendre_ref.3, s32[1,1280]{1,0:T(1,128)} %broadcast_in_dim.8.counts_ref, ...), custom_call_target="tpu_custom_call", output_to_operand_aliasing={{0}: (7, {})} | custom-call | flops 7182745600 | bytes 34631680 | tf_op jit(solution)/shard_map/pallas_call | solution.py:307
  180.5 30.3 %all-to-all-done.3 = bf16[16,8,11008]{2,1,0:T(8,128)(2,1)} async-done(((bf16[16,8,11008]{2,1,0:T(8,128)(2,1)}), bf16[16,8,11008]{2,1,0:T(8,128)(2,1)}, u32[]{:S(2)}, u32[]{:S(2)}) %all-to-all-start.3) | async-done | bytes 2818080 | tf_op jit(solution)/shard_map/all_to_all | solution.py:358
  210.8 4.9 %all-to-all-start.2 = ((bf16[16,8,11008]{2,1,0:T(8,128)(2,1)}), bf16[16,8,11008]{2,1,0:T(8,128)(2,1)}, u32[]{:S(2)}, u32[]{:S(2)}) async-start(bf16[16,8,11008]{2,1,0:T(8,128)(2,1)} %bitcast.32), calls=%async_computation.2 | async-start | bytes 5636096 | tf_op jit(solution)/shard_map/all_to_all | solution.py:358
  215.7 3.7 %shard_map.99.refs_0_ = bf16[2,137,80,128]{3,2,1,0:T(8,128)(2,1)} custom-call(bf16[128,11008]{1,0:T(8,128)(2,1)} %bitcast.18.in_ref), custom_call_target="tpu_custom_call" | custom-call | flops 1402880 | bytes 5611520 | tf_op jit(solution)/shard_map/pallas_call | solution.py:119
  219.4 59.3 %all-to-all-done.2 = bf16[16,8,11008]{2,1,0:T(8,128)(2,1)} async-done(((bf16[16,8,11008]{2,1,0:T(8,128)(2,1)}), bf16[16,8,11008]{2,1,0:T(8,128)(2,1)}, u32[]{:S(2)}, u32[]{:S(2)}) %all-to-all-start.2) | async-done | bytes 2818080 | tf_op jit(solution)/shard_map/all_to_all | solution.py:358
  278.6 3.7 %shard_map.100 = bf16[2,137,80,128]{3,2,1,0:T(8,128)(2,1)} custom-call(bf16[128,11008]{1,0:T(8,128)(2,1)} %bitcast.16.in_ref, bf16[2,137,80,128]{3,2,1,0:T(8,128)(2,1)} %shard_map.99.refs_0_), custom_call_target="tpu_custom_call", output_to_operand_aliasing={{}: (1, {})} | custom-call | flops 1402880 | bytes 5611520 | tf_op jit(solution)/shard_map/pallas_call | solution.py:119
Async XLA Ops:
  5.3 69.5 %all-to-all-start.1 = ((bf16[16,8,11008]{2,1,0:T(8,128)(2,1)}), bf16[16,8,11008]{2,1,0:T(8,128)(2,1)}, u32[]{:S(2)}, u32[]{:S(2)}) async-start(bf16[16,8,11008]{2,1,0:T(8,128)(2,1)} %bitcast.29), calls=%async_computation.1 | async-start | bytes 5636096 | tf_op jit(solution)/shard_map/all_to_all | solution.py:350
  74.8 5.1 %copy-start.2 = (s32[1280]{0:T(1024)S(1)}, s32[1280]{0:T(1024)}, u32[]{:S(2)}) copy-start(s32[1280]{0:T(1024)} %param.10) | copy-start | bytes 15364
  74.8 5.7 %copy-start.3 = (f32[137]{0:T(256)S(1)}, f32[137]{0:T(256)}, u32[]{:S(2)}) copy-start(f32[137]{0:T(256)} %param.13) | copy-start | bytes 1648
  74.8 6.4 %copy-start = (bf16[137,137]{1,0:T(8,128)(2,1)S(1)}, bf16[137,137]{1,0:T(8,128)(2,1)}, u32[]{:S(2)}) copy-start(bf16[137,137]{1,0:T(8,128)(2,1)} %param.14) | copy-start | bytes 112618
  74.8 7.2 %copy-start.1 = (bf16[137,137]{1,0:T(8,128)(2,1)S(1)}, bf16[137,137]{1,0:T(8,128)(2,1)}, u32[]{:S(2)}) copy-start(bf16[137,137]{1,0:T(8,128)(2,1)} %param.15) | copy-start | bytes 112618
  74.8 7.9 %copy-start.4 = (s32[128]{0:T(128)S(1)}, s32[128]{0:T(128)}, u32[]{:S(2)}) copy-start(s32[128]{0:T(128)} %param.11) | copy-start | bytes 1540
  74.9 68.0 %all-to-all-start = ((bf16[16,8,11008]{2,1,0:T(8,128)(2,1)}), bf16[16,8,11008]{2,1,0:T(8,128)(2,1)}, u32[]{:S(2)}, u32[]{:S(2)}) async-start(bf16[16,8,11008]{2,1,0:T(8,128)(2,1)} %bitcast.28), calls=%async_computation | async-start | bytes 5636096 | tf_op jit(solution)/shard_map/all_to_all | solution.py:350
  142.9 67.9 %all-to-all-start.3 = ((bf16[16,8,11008]{2,1,0:T(8,128)(2,1)}), bf16[16,8,11008]{2,1,0:T(8,128)(2,1)}, u32[]{:S(2)}, u32[]{:S(2)}) async-start(bf16[16,8,11008]{2,1,0:T(8,128)(2,1)} %bitcast.31), calls=%async_computation.3 | async-start | bytes 5636096 | tf_op jit(solution)/shard_map/all_to_all | solution.py:358
  210.8 67.9 %all-to-all-start.2 = ((bf16[16,8,11008]{2,1,0:T(8,128)(2,1)}), bf16[16,8,11008]{2,1,0:T(8,128)(2,1)}, u32[]{:S(2)}, u32[]{:S(2)}) async-start(bf16[16,8,11008]{2,1,0:T(8,128)(2,1)} %bitcast.32), calls=%async_computation.2 | async-start | bytes 5636096 | tf_op jit(solution)/shard_map/all_to_all | solution.py:358

commit v11 on v10

--- a/solution.py
+++ b/solution.py
@@ -10,7 +10,7 @@
 
 NMAX = 2559
 VMEM_BYTES = 62 * 1024 * 1024
-GROUPS = 1
+GROUPS = 3
 LANES = 128
 
 

time: 283 us -> 282 us (level)
  no operation moved by 1% of the time
where the time goes in v11:
time: 282 us; the launch traced here: 281 us
  waiting for transfers between devices  176 us (62%)
  Pallas kernels  79.5 us (28%)
  starting transfers between devices  21.4 us (8%)
  local copies, waits for them, and re-layouts  3.48 us (1%)
    all_to_all x2, waiting for transfers between devices, per_device(): returned.append(exchange(rows))  90.3 us
    all_to_all x2, waiting for transfers between devices, per_device(): columns = [exchange(pack(part, north, south)) for part in range(parts)]  85.7 us
    pallas_call x2, Pallas kernels, spectral_step(): pl.pallas_call(step_body, grid_spec=pltpu.PrefetchScalarGridSpec(num_scal...  65.3 us
    all_to_all x2, starting transfers between devices, per_device(): columns = [exchange(pack(part, north, south)) for part in range(parts)]  11.6 us
    all_to_all x2, starting transfers between devices, per_device(): returned.append(exchange(rows))  9.82 us
    pallas_call x2, Pallas kernels, pack(): pl.pallas_call(functools.partial(pack_body, part=part), in_specs=[anywher...  8.22 us
    pallas_call x2, Pallas kernels, unpack(): pl.pallas_call(functools.partial(unpack_body, part=part), in_specs=[anywh...  5.95 us
  transfers between devices with their start and end apart: 4, of which 4 were waited for; matrix products, arithmetic and copies ran while one was open for 1% of the time, Pallas kernels for 26%

profile of v11, /device:TPU:13, one launch (start us, length us, event | category | flops | bytes accessed | tf_op | source)
XLA Modules:
  0.0 281.1 jit_solution(15574406026392618024)
XLA Ops:
  0.6 4.1 %shard_map.96 = bf16[128,11008]{1,0:T(8,128)(2,1)} custom-call(bf16[2,137,80,128]{3,2,1,0:T(8,128)(2,1)} %bitcast.24, bf16[2,137,80,128]{3,2,1,0:T(8,128)(2,1)} %bitcast.26), custom_call_target="tpu_custom_call" | custom-call | flops 2805760 | bytes 8417280 | tf_op jit(solution)/shard_map/pallas_call | solution.py:70
  4.7 6.6 %all-to-all-start.1 = ((bf16[16,8,11008]{2,1,0:T(8,128)(2,1)}), bf16[16,8,11008]{2,1,0:T(8,128)(2,1)}, u32[]{:S(2)}, u32[]{:S(2)}) async-start(bf16[16,8,11008]{2,1,0:T(8,128)(2,1)} %bitcast.29), calls=%async_computation.1 | async-start | bytes 5636096 | tf_op jit(solution)/shard_map/all_to_all | solution.py:350
  11.3 4.1 %shard_map.95 = bf16[128,11008]{1,0:T(8,128)(2,1)} custom-call(bf16[2,137,80,128]{3,2,1,0:T(8,128)(2,1)} %bitcast.25, bf16[2,137,80,128]{3,2,1,0:T(8,128)(2,1)} %bitcast.27), custom_call_target="tpu_custom_call" | custom-call | flops 2805760 | bytes 8417280 | tf_op jit(solution)/shard_map/pallas_call | solution.py:70
  15.4 58.9 %all-to-all-done.1 = bf16[16,8,11008]{2,1,0:T(8,128)(2,1)} async-done(((bf16[16,8,11008]{2,1,0:T(8,128)(2,1)}), bf16[16,8,11008]{2,1,0:T(8,128)(2,1)}, u32[]{:S(2)}, u32[]{:S(2)}) %all-to-all-start.1) | async-done | bytes 2818080 | tf_op jit(solution)/shard_map/all_to_all | solution.py:350
  74.3 0.0 copy-start.2
  74.3 0.0 copy-start.3
  74.3 0.0 copy-start
  74.3 0.0 copy-start.1
  74.3 0.0 copy-start.4
  74.3 5.1 %all-to-all-start = ((bf16[16,8,11008]{2,1,0:T(8,128)(2,1)}), bf16[16,8,11008]{2,1,0:T(8,128)(2,1)}, u32[]{:S(2)}, u32[]{:S(2)}) async-start(bf16[16,8,11008]{2,1,0:T(8,128)(2,1)} %bitcast.28), calls=%async_computation | async-start | bytes 5636096 | tf_op jit(solution)/shard_map/all_to_all | solution.py:350
  79.4 0.0 copy-done.2
  79.4 0.6 broadcast_in_dim.8.counts_ref
  80.0 0.0 copy-done.3
  80.0 0.7 copy.17.rates_ref
  80.7 0.0 copy-done
  80.7 0.7 copy.14
  81.5 0.0 copy-done.1
  81.5 0.7 copy.15
  82.2 0.0 copy-done.4
  82.2 0.7 dynamic_slice.3.waves_ref
  82.8 32.6 %shard_map.97 = (bf16[2,137,8,1280]{3,2,1,0:T(8,128)(2,1)}, bf16[128,11008]{1,0:T(8,128)(2,1)}) custom-call(s32[8]{0:T(128)} %dynamic_slice.3.waves_ref, bf16[128,11008]{1,0:T(8,128)(2,1)} %bitcast.12.recv_ref, bf16[8,1280,1280]{2,1,0:T(8,128)(2,1)} %legendre_ref.3, s32[1,1280]{1,0:T(1,128)} %broadcast_in_dim.8.counts_ref, f32[137,1]{1,0:T(8,128)} %copy.17.rates_ref, ...), custom_call_target="tpu_custom_call" | custom-call | flops 7182745600 | bytes 34631680 | tf_op jit(solution)/shard_map/pallas_call | solution.py:307
  115.5 26.9 %all-to-all-done = bf16[16,8,11008]{2,1,0:T(8,128)(2,1)} async-done(((bf16[16,8,11008]{2,1,0:T(8,128)(2,1)}), bf16[16,8,11008]{2,1,0:T(8,128)(2,1)}, u32[]{:S(2)}, u32[]{:S(2)}) %all-to-all-start) | async-done | bytes 2818080 | tf_op jit(solution)/shard_map/all_to_all | solution.py:350
  142.3 4.9 %all-to-all-start.3 = ((bf16[16,8,11008]{2,1,0:T(8,128)(2,1)}), bf16[16,8,11008]{2,1,0:T(8,128)(2,1)}, u32[]{:S(2)}, u32[]{:S(2)}) async-start(bf16[16,8,11008]{2,1,0:T(8,128)(2,1)} %bitcast.31), calls=%async_computation.3 | async-start | bytes 5636096 | tf_op jit(solution)/shard_map/all_to_all | solution.py:358
  147.2 32.7 %shard_map.98 = (bf16[2,137,8,1280]{3,2,1,0:T(8,128)(2,1)}, bf16[128,11008]{1,0:T(8,128)(2,1)}) custom-call(s32[8]{0:T(128)} %dynamic_slice.3.waves_ref, bf16[128,11008]{1,0:T(8,128)(2,1)} %bitcast.5.recv_ref, bf16[8,1280,1280]{2,1,0:T(8,128)(2,1)} %legendre_ref.3, s32[1,1280]{1,0:T(1,128)} %broadcast_in_dim.8.counts_ref, ...), custom_call_target="tpu_custom_call", output_to_operand_aliasing={{0}: (7, {})} | custom-call | flops 7182745600 | bytes 34631680 | tf_op jit(solution)/shard_map/pallas_call | solution.py:307
  180.0 30.3 %all-to-all-done.3 = bf16[16,8,11008]{2,1,0:T(8,128)(2,1)} async-done(((bf16[16,8,11008]{2,1,0:T(8,128)(2,1)}), bf16[16,8,11008]{2,1,0:T(8,128)(2,1)}, u32[]{:S(2)}, u32[]{:S(2)}) %all-to-all-start.3) | async-done | bytes 2818080 | tf_op jit(solution)/shard_map/all_to_all | solution.py:358
  210.2 4.9 %all-to-all-start.2 = ((bf16[16,8,11008]{2,1,0:T(8,128)(2,1)}), bf16[16,8,11008]{2,1,0:T(8,128)(2,1)}, u32[]{:S(2)}, u32[]{:S(2)}) async-start(bf16[16,8,11008]{2,1,0:T(8,128)(2,1)} %bitcast.32), calls=%async_computation.2 | async-start | bytes 5636096 | tf_op jit(solution)/shard_map/all_to_all | solution.py:358
  215.1 3.0 %shard_map.99.refs_0_ = bf16[2,137,80,128]{3,2,1,0:T(8,128)(2,1)} custom-call(bf16[128,11008]{1,0:T(8,128)(2,1)} %bitcast.18.in_ref), custom_call_target="tpu_custom_call" | custom-call | flops 1402880 | bytes 5611520 | tf_op jit(solution)/shard_map/pallas_call | solution.py:119
  218.1 60.0 %all-to-all-done.2 = bf16[16,8,11008]{2,1,0:T(8,128)(2,1)} async-done(((bf16[16,8,11008]{2,1,0:T(8,128)(2,1)}), bf16[16,8,11008]{2,1,0:T(8,128)(2,1)}, u32[]{:S(2)}, u32[]{:S(2)}) %all-to-all-start.2) | async-done | bytes 2818080 | tf_op jit(solution)/shard_map/all_to_all | solution.py:358
  278.1 3.0 %shard_map.100 = bf16[2,137,80,128]{3,2,1,0:T(8,128)(2,1)} custom-call(bf16[128,11008]{1,0:T(8,128)(2,1)} %bitcast.16.in_ref, bf16[2,137,80,128]{3,2,1,0:T(8,128)(2,1)} %shard_map.99.refs_0_), custom_call_target="tpu_custom_call", output_to_operand_aliasing={{}: (1, {})} | custom-call | flops 1402880 | bytes 5611520 | tf_op jit(solution)/shard_map/pallas_call | solution.py:119
Async XLA Ops:
  4.7 69.5 %all-to-all-start.1 = ((bf16[16,8,11008]{2,1,0:T(8,128)(2,1)}), bf16[16,8,11008]{2,1,0:T(8,128)(2,1)}, u32[]{:S(2)}, u32[]{:S(2)}) async-start(bf16[16,8,11008]{2,1,0:T(8,128)(2,1)} %bitcast.29), calls=%async_computation.1 | async-start | bytes 5636096 | tf_op jit(solution)/shard_map/all_to_all | solution.py:350
  74.3 5.1 %copy-start.2 = (s32[1280]{0:T(1024)S(1)}, s32[1280]{0:T(1024)}, u32[]{:S(2)}) copy-start(s32[1280]{0:T(1024)} %param.10) | copy-start | bytes 15364
  74.3 5.7 %copy-start.3 = (f32[137]{0:T(256)S(1)}, f32[137]{0:T(256)}, u32[]{:S(2)}) copy-start(f32[137]{0:T(256)} %param.13) | copy-start | bytes 1648
  74.3 6.4 %copy-start = (bf16[137,137]{1,0:T(8,128)(2,1)S(1)}, bf16[137,137]{1,0:T(8,128)(2,1)}, u32[]{:S(2)}) copy-start(bf16[137,137]{1,0:T(8,128)(2,1)} %param.14) | copy-start | bytes 112618
  74.3 7.2 %copy-start.1 = (bf16[137,137]{1,0:T(8,128)(2,1)S(1)}, bf16[137,137]{1,0:T(8,128)(2,1)}, u32[]{:S(2)}) copy-start(bf16[137,137]{1,0:T(8,128)(2,1)} %param.15) | copy-start | bytes 112618
  74.3 7.9 %copy-start.4 = (s32[128]{0:T(128)S(1)}, s32[128]{0:T(128)}, u32[]{:S(2)}) copy-start(s32[128]{0:T(128)} %param.11) | copy-start | bytes 1540
  74.3 68.0 %all-to-all-start = ((bf16[16,8,11008]{2,1,0:T(8,128)(2,1)}), bf16[16,8,11008]{2,1,0:T(8,128)(2,1)}, u32[]{:S(2)}, u32[]{:S(2)}) async-start(bf16[16,8,11008]{2,1,0:T(8,128)(2,1)} %bitcast.28), calls=%async_computation | async-start | bytes 5636096 | tf_op jit(solution)/shard_map/all_to_all | solution.py:350
  142.3 67.9 %all-to-all-start.3 = ((bf16[16,8,11008]{2,1,0:T(8,128)(2,1)}), bf16[16,8,11008]{2,1,0:T(8,128)(2,1)}, u32[]{:S(2)}, u32[]{:S(2)}) async-start(bf16[16,8,11008]{2,1,0:T(8,128)(2,1)} %bitcast.31), calls=%async_computation.3 | async-start | bytes 5636096 | tf_op jit(solution)/shard_map/all_to_all | solution.py:358
  210.2 67.9 %all-to-all-start.2 = ((bf16[16,8,11008]{2,1,0:T(8,128)(2,1)}), bf16[16,8,11008]{2,1,0:T(8,128)(2,1)}, u32[]{:S(2)}, u32[]{:S(2)}) async-start(bf16[16,8,11008]{2,1,0:T(8,128)(2,1)} %bitcast.32), calls=%async_computation.2 | async-start | bytes 5636096 | tf_op jit(solution)/shard_map/all_to_all | solution.py:358

commit v12 on v11

--- a/solution.py
+++ b/solution.py
@@ -10,7 +10,7 @@
 
 NMAX = 2559
 VMEM_BYTES = 62 * 1024 * 1024
-GROUPS = 3
+GROUPS = 6
 LANES = 128
 
 

time: 282 us -> 281 us (level)
  no operation moved by 1% of the time
where the time goes in v12:
time: 281 us
  waiting for transfers between devices  176 us (63%)
  Pallas kernels  79.2 us (28%)
  starting transfers between devices  21.4 us (8%)
  local copies, waits for them, and re-layouts  3.48 us (1%)
    all_to_all x2, waiting for transfers between devices, per_device(): returned.append(exchange(rows))  90.2 us
    all_to_all x2, waiting for transfers between devices, per_device(): columns = [exchange(pack(part, north, south)) for part in range(parts)]  86 us
    pallas_call x2, Pallas kernels, spectral_step(): pl.pallas_call(step_body, grid_spec=pltpu.PrefetchScalarGridSpec(num_scal...  65.3 us
    all_to_all x2, starting transfers between devices, per_device(): columns = [exchange(pack(part, north, south)) for part in range(parts)]  11.6 us
    all_to_all x2, starting transfers between devices, per_device(): returned.append(exchange(rows))  9.82 us
    pallas_call x2, Pallas kernels, pack(): pl.pallas_call(functools.partial(pack_body, part=part), in_specs=[anywher...  7.68 us
    pallas_call x2, Pallas kernels, unpack(): pl.pallas_call(functools.partial(unpack_body, part=part), in_specs=[anywh...  6.2 us
  transfers between devices with their start and end apart: 4, of which 4 were waited for; matrix products, arithmetic and copies ran while one was open for 1% of the time, Pallas kernels for 26%

profile of v12, /device:TPU:13, one launch (start us, length us, event | category | flops | bytes accessed | tf_op | source)
XLA Modules:
  0.0 280.9 jit_solution(14364194306438663873)
XLA Ops:
  0.6 3.8 %shard_map.96 = bf16[128,11008]{1,0:T(8,128)(2,1)} custom-call(bf16[2,137,80,128]{3,2,1,0:T(8,128)(2,1)} %bitcast.24, bf16[2,137,80,128]{3,2,1,0:T(8,128)(2,1)} %bitcast.26), custom_call_target="tpu_custom_call" | custom-call | flops 2805760 | bytes 8417280 | tf_op jit(solution)/shard_map/pallas_call | solution.py:70
  4.5 6.6 %all-to-all-start.1 = ((bf16[16,8,11008]{2,1,0:T(8,128)(2,1)}), bf16[16,8,11008]{2,1,0:T(8,128)(2,1)}, u32[]{:S(2)}, u32[]{:S(2)}) async-start(bf16[16,8,11008]{2,1,0:T(8,128)(2,1)} %bitcast.29), calls=%async_computation.1 | async-start | bytes 5636096 | tf_op jit(solution)/shard_map/all_to_all | solution.py:350
  11.0 3.8 %shard_map.95 = bf16[128,11008]{1,0:T(8,128)(2,1)} custom-call(bf16[2,137,80,128]{3,2,1,0:T(8,128)(2,1)} %bitcast.25, bf16[2,137,80,128]{3,2,1,0:T(8,128)(2,1)} %bitcast.27), custom_call_target="tpu_custom_call" | custom-call | flops 2805760 | bytes 8417280 | tf_op jit(solution)/shard_map/pallas_call | solution.py:70
  14.9 59.1 %all-to-all-done.1 = bf16[16,8,11008]{2,1,0:T(8,128)(2,1)} async-done(((bf16[16,8,11008]{2,1,0:T(8,128)(2,1)}), bf16[16,8,11008]{2,1,0:T(8,128)(2,1)}, u32[]{:S(2)}, u32[]{:S(2)}) %all-to-all-start.1) | async-done | bytes 2818080 | tf_op jit(solution)/shard_map/all_to_all | solution.py:350
  74.0 0.0 copy-start.2
  74.0 0.0 copy-start.3
  74.0 0.0 copy-start
  74.0 0.0 copy-start.1
  74.0 0.0 copy-start.4
  74.0 5.1 %all-to-all-start = ((bf16[16,8,11008]{2,1,0:T(8,128)(2,1)}), bf16[16,8,11008]{2,1,0:T(8,128)(2,1)}, u32[]{:S(2)}, u32[]{:S(2)}) async-start(bf16[16,8,11008]{2,1,0:T(8,128)(2,1)} %bitcast.28), calls=%async_computation | async-start | bytes 5636096 | tf_op jit(solution)/shard_map/all_to_all | solution.py:350
  79.1 0.0 copy-done.2
  79.1 0.6 broadcast_in_dim.8.counts_ref
  79.7 0.0 copy-done.3
  79.7 0.7 copy.17.rates_ref
  80.4 0.0 copy-done
  80.4 0.7 copy.14
  81.2 0.0 copy-done.1
  81.2 0.7 copy.15
  81.9 0.0 copy-done.4
  81.9 0.7 dynamic_slice.3.waves_ref
  82.6 32.6 %shard_map.97 = (bf16[2,137,8,1280]{3,2,1,0:T(8,128)(2,1)}, bf16[128,11008]{1,0:T(8,128)(2,1)}) custom-call(s32[8]{0:T(128)} %dynamic_slice.3.waves_ref, bf16[128,11008]{1,0:T(8,128)(2,1)} %bitcast.12.recv_ref, bf16[8,1280,1280]{2,1,0:T(8,128)(2,1)} %legendre_ref.3, s32[1,1280]{1,0:T(1,128)} %broadcast_in_dim.8.counts_ref, f32[137,1]{1,0:T(8,128)} %copy.17.rates_ref, ...), custom_call_target="tpu_custom_call" | custom-call | flops 7182745600 | bytes 34631680 | tf_op jit(solution)/shard_map/pallas_call | solution.py:307
  115.2 26.9 %all-to-all-done = bf16[16,8,11008]{2,1,0:T(8,128)(2,1)} async-done(((bf16[16,8,11008]{2,1,0:T(8,128)(2,1)}), bf16[16,8,11008]{2,1,0:T(8,128)(2,1)}, u32[]{:S(2)}, u32[]{:S(2)}) %all-to-all-start) | async-done | bytes 2818080 | tf_op jit(solution)/shard_map/all_to_all | solution.py:350
  142.1 4.9 %all-to-all-start.3 = ((bf16[16,8,11008]{2,1,0:T(8,128)(2,1)}), bf16[16,8,11008]{2,1,0:T(8,128)(2,1)}, u32[]{:S(2)}, u32[]{:S(2)}) async-start(bf16[16,8,11008]{2,1,0:T(8,128)(2,1)} %bitcast.31), calls=%async_computation.3 | async-start | bytes 5636096 | tf_op jit(solution)/shard_map/all_to_all | solution.py:358
  147.0 32.7 %shard_map.98 = (bf16[2,137,8,1280]{3,2,1,0:T(8,128)(2,1)}, bf16[128,11008]{1,0:T(8,128)(2,1)}) custom-call(s32[8]{0:T(128)} %dynamic_slice.3.waves_ref, bf16[128,11008]{1,0:T(8,128)(2,1)} %bitcast.5.recv_ref, bf16[8,1280,1280]{2,1,0:T(8,128)(2,1)} %legendre_ref.3, s32[1,1280]{1,0:T(1,128)} %broadcast_in_dim.8.counts_ref, ...), custom_call_target="tpu_custom_call", output_to_operand_aliasing={{0}: (7, {})} | custom-call | flops 7182745600 | bytes 34631680 | tf_op jit(solution)/shard_map/pallas_call | solution.py:307
  179.7 30.3 %all-to-all-done.3 = bf16[16,8,11008]{2,1,0:T(8,128)(2,1)} async-done(((bf16[16,8,11008]{2,1,0:T(8,128)(2,1)}), bf16[16,8,11008]{2,1,0:T(8,128)(2,1)}, u32[]{:S(2)}, u32[]{:S(2)}) %all-to-all-start.3) | async-done | bytes 2818080 | tf_op jit(solution)/shard_map/all_to_all | solution.py:358
  210.0 4.9 %all-to-all-start.2 = ((bf16[16,8,11008]{2,1,0:T(8,128)(2,1)}), bf16[16,8,11008]{2,1,0:T(8,128)(2,1)}, u32[]{:S(2)}, u32[]{:S(2)}) async-start(bf16[16,8,11008]{2,1,0:T(8,128)(2,1)} %bitcast.32), calls=%async_computation.2 | async-start | bytes 5636096 | tf_op jit(solution)/shard_map/all_to_all | solution.py:358
  214.9 3.1 %shard_map.99.refs_0_ = bf16[2,137,80,128]{3,2,1,0:T(8,128)(2,1)} custom-call(bf16[128,11008]{1,0:T(8,128)(2,1)} %bitcast.18.in_ref), custom_call_target="tpu_custom_call" | custom-call | flops 1402880 | bytes 5611520 | tf_op jit(solution)/shard_map/pallas_call | solution.py:119
  218.0 59.9 %all-to-all-done.2 = bf16[16,8,11008]{2,1,0:T(8,128)(2,1)} async-done(((bf16[16,8,11008]{2,1,0:T(8,128)(2,1)}), bf16[16,8,11008]{2,1,0:T(8,128)(2,1)}, u32[]{:S(2)}, u32[]{:S(2)}) %all-to-all-start.2) | async-done | bytes 2818080 | tf_op jit(solution)/shard_map/all_to_all | solution.py:358
  277.8 3.1 %shard_map.100 = bf16[2,137,80,128]{3,2,1,0:T(8,128)(2,1)} custom-call(bf16[128,11008]{1,0:T(8,128)(2,1)} %bitcast.16.in_ref, bf16[2,137,80,128]{3,2,1,0:T(8,128)(2,1)} %shard_map.99.refs_0_), custom_call_target="tpu_custom_call", output_to_operand_aliasing={{}: (1, {})} | custom-call | flops 1402880 | bytes 5611520 | tf_op jit(solution)/shard_map/pallas_call | solution.py:119
Async XLA Ops:
  4.5 69.5 %all-to-all-start.1 = ((bf16[16,8,11008]{2,1,0:T(8,128)(2,1)}), bf16[16,8,11008]{2,1,0:T(8,128)(2,1)}, u32[]{:S(2)}, u32[]{:S(2)}) async-start(bf16[16,8,11008]{2,1,0:T(8,128)(2,1)} %bitcast.29), calls=%async_computation.1 | async-start | bytes 5636096 | tf_op jit(solution)/shard_map/all_to_all | solution.py:350
  74.0 5.1 %copy-start.2 = (s32[1280]{0:T(1024)S(1)}, s32[1280]{0:T(1024)}, u32[]{:S(2)}) copy-start(s32[1280]{0:T(1024)} %param.10) | copy-start | bytes 15364
  74.0 5.7 %copy-start.3 = (f32[137]{0:T(256)S(1)}, f32[137]{0:T(256)}, u32[]{:S(2)}) copy-start(f32[137]{0:T(256)} %param.13) | copy-start | bytes 1648
  74.0 6.4 %copy-start = (bf16[137,137]{1,0:T(8,128)(2,1)S(1)}, bf16[137,137]{1,0:T(8,128)(2,1)}, u32[]{:S(2)}) copy-start(bf16[137,137]{1,0:T(8,128)(2,1)} %param.14) | copy-start | bytes 112618
  74.0 7.2 %copy-start.1 = (bf16[137,137]{1,0:T(8,128)(2,1)S(1)}, bf16[137,137]{1,0:T(8,128)(2,1)}, u32[]{:S(2)}) copy-start(bf16[137,137]{1,0:T(8,128)(2,1)} %param.15) | copy-start | bytes 112618
  74.0 7.9 %copy-start.4 = (s32[128]{0:T(128)S(1)}, s32[128]{0:T(128)}, u32[]{:S(2)}) copy-start(s32[128]{0:T(128)} %param.11) | copy-start | bytes 1540
  74.0 68.0 %all-to-all-start = ((bf16[16,8,11008]{2,1,0:T(8,128)(2,1)}), bf16[16,8,11008]{2,1,0:T(8,128)(2,1)}, u32[]{:S(2)}, u32[]{:S(2)}) async-start(bf16[16,8,11008]{2,1,0:T(8,128)(2,1)} %bitcast.28), calls=%async_computation | async-start | bytes 5636096 | tf_op jit(solution)/shard_map/all_to_all | solution.py:350
  142.1 67.9 %all-to-all-start.3 = ((bf16[16,8,11008]{2,1,0:T(8,128)(2,1)}), bf16[16,8,11008]{2,1,0:T(8,128)(2,1)}, u32[]{:S(2)}, u32[]{:S(2)}) async-start(bf16[16,8,11008]{2,1,0:T(8,128)(2,1)} %bitcast.31), calls=%async_computation.3 | async-start | bytes 5636096 | tf_op jit(solution)/shard_map/all_to_all | solution.py:358
  210.0 67.9 %all-to-all-start.2 = ((bf16[16,8,11008]{2,1,0:T(8,128)(2,1)}), bf16[16,8,11008]{2,1,0:T(8,128)(2,1)}, u32[]{:S(2)}, u32[]{:S(2)}) async-start(bf16[16,8,11008]{2,1,0:T(8,128)(2,1)} %bitcast.32), calls=%async_computation.2 | async-start | bytes 5636096 | tf_op jit(solution)/shard_map/all_to_all | solution.py:358
